TPU v7x, 32 devices: a whole 2x2x4 slice. The times are simulated.
32 devices in a mesh: dp: 8 (over y, x, core), tensor: 4 (over z).
Axes of the slice: x: 2, y: 2, z: 4, core: 2. Of those that a mesh axis runs over, the one named last changes fastest.
Arguments:
- tokens: bfloat16 [8192, 2048], P('dp'), may hold values from -6 to 6
- cotangent: bfloat16 [8192, 2048], P('dp'), may hold values from -6 to 6
- segments: int32 [8, 1024], P('dp'), may hold values from 0 to 5, never falling along the last dimension, each value on 1 to 512 neighbouring positions
- norm_gains: bfloat16 [2, 2048], replicated, may hold values from 0.5 to 1.5
- w_qkv: bfloat16 [2048, 8, 384], P(None, 'tensor'), may hold values from -0.125 to 0.125
- qkv_down: bfloat16 [3, 8, 2048], replicated, may hold values from -0.125 to 0.125
- query_key_value_up: bfloat16 [8, 8, 384], P(None, 'tensor'), may hold values from -1 to 1
- feature_maps: bfloat16 [8, 64, 320], P('tensor'), may hold values from -0.75 to 0.75
- w_out: bfloat16 [2048, 2048], P('tensor'), may hold values from -1 to 1
- o_down: bfloat16 [8, 8, 256], P(None, 'tensor'), may hold values from -0.125 to 0.125
- o_up: bfloat16 [8, 2048], replicated, may hold values from -6 to 6
- w_gate_up: bfloat16 [2048, 2, 8192], P(None, None, 'tensor'), may hold values from -0.125 to 0.125
- w_down: bfloat16 [8192, 2048], P('tensor'), may hold values from -0.0625 to 0.0625
Outputs:
- output: bfloat16 [8192, 2048], P(('dp', 'tensor'))
- grad_input: bfloat16 [8192, 2048], P(('dp', 'tensor'))
- grad_norm_gains: float32 [2, 2048], P(None, ('dp', 'tensor'))
- grad_w_qkv: float32 [2048, 8, 384], P('dp', 'tensor')
- grad_qkv_down: float32 [3, 8, 2048], P(None, None, ('dp', 'tensor'))
- grad_qkv_up: float32 [8, 8, 384], P(None, 'tensor', 'dp')
- grad_feature_maps: float32 [8, 64, 320], P('tensor', None, 'dp')
- grad_w_out: float32 [2048, 2048], P('tensor', 'dp')
- grad_o_down: float32 [8, 8, 256], P(None, 'tensor', 'dp')
- grad_o_up: float32 [8, 2048], P(None, ('dp', 'tensor'))
- grad_w_gate_up: float32 [2048, 2, 8192], P('dp', None, 'tensor')
- grad_w_down: float32 [8192, 2048], P('tensor', 'dp')
Inputs may be any that keep to these rules, and one draw needn't show every extreme that they name: `segments`: within each packed sequence the numbers never fall, so that each document is one run of positions; no document is longer than 512 positions, and some document reaches that length.
All inputs are finite; a program needn't handle non-finite values.
Results may differ from a plain program's by a relative error of at most 0.024.
Values may be sent and summed in bfloat16 or wider, within the bound.
A program may use at most 320 MiB of HBM per device.

v0:
```python
from functools import partial

import jax
import jax.numpy as jnp
from jax import lax
from jax.sharding import PartitionSpec as P

HEADS = 32
KVH = 8
HEAD_SIZE = 64
WINDOW = 64


highest = lax.Precision.HIGHEST
epsilon = 1e-05
rope_base = 500000.0


def rotary_tables(length, head_span_width):
    half_width = head_span_width // 2
    frequency = rope_base ** (-(jnp.arange(half_width, dtype=jnp.float32) * 2.0) / head_span_width)
    angles = jnp.arange(length, dtype=jnp.float32)[:, None] * frequency[None, :]
    return (jnp.cos(angles), jnp.sin(angles))


def rotate(values, cosines, sine_values):
    half_width = values.shape[-1] // 2
    leading = values[..., :half_width]
    trailing = values[..., half_width:]
    return jnp.concatenate(
        [leading * cosines - trailing * sine_values, trailing * cosines + leading * sine_values],
        axis=-1,
    )


def rotate_back(gradients, cosines, sine_values):
    half_width = gradients.shape[-1] // 2
    leading = gradients[..., :half_width]
    trailing = gradients[..., half_width:]
    return jnp.concatenate(
        [leading * cosines + trailing * sine_values, trailing * cosines - leading * sine_values],
        axis=-1,
    )


def hedgehog(logits):
    return jnp.concatenate(
        [jax.nn.softmax(logits, axis=-1), jax.nn.softmax(-logits, axis=-1)], axis=-1
    )


def hedgehog_back(logits, gradients):
    half_width = gradients.shape[-1] // 2
    upper_half = jax.nn.softmax(logits, axis=-1)
    lower_half = jax.nn.softmax(-logits, axis=-1)
    grad_upper = gradients[..., :half_width]
    grad_lower = gradients[..., half_width:]
    return upper_half * (
        grad_upper - jnp.sum(grad_upper * upper_half, axis=-1, keepdims=True)
    ) - lower_half * (grad_lower - jnp.sum(grad_lower * lower_half, axis=-1, keepdims=True))


def normalize(values, gain_row):
    inverse = lax.rsqrt(jnp.mean(values * values, axis=-1, keepdims=True) + epsilon)
    scaled = values * inverse
    return (scaled, inverse, (scaled * gain_row).astype(jnp.bfloat16))


def norm_back(scaled, inverse, gain_row, gradients):
    weighted = gradients * gain_row
    return inverse * (weighted - scaled * jnp.mean(weighted * scaled, axis=-1, keepdims=True))


def adapter_columns(lowrank_update, up_maps_float, query_span_width, head_span_width):
    upper_key = query_span_width + head_span_width
    return jnp.concatenate(
        [
            jnp.einsum(
                "tr,rkc->tkc",
                lowrank_update[:, 0],
                up_maps_float[:, :, :query_span_width],
                precision=highest,
            ),
            jnp.einsum(
                "tr,rkc->tkc",
                lowrank_update[:, 1],
                up_maps_float[:, :, query_span_width:upper_key],
                precision=highest,
            ),
            jnp.einsum(
                "tr,rkc->tkc",
                lowrank_update[:, 2],
                up_maps_float[:, :, upper_key:],
                precision=highest,
            ),
        ],
        axis=2,
    )


def block_weights(
    query_block, qfeat_block, key_rows, kfeat_rows, query_segs, key_segs, query_pos, score_scale
):
    scores = (
        jnp.einsum("ikgd,jkd->kgij", query_block, key_rows, preferred_element_type=jnp.float32)
        * score_scale
    )
    linear = jnp.einsum(
        "ikge,jke->kgij", qfeat_block, kfeat_rows, preferred_element_type=jnp.float32
    )
    key_pos = jnp.arange(key_rows.shape[0], dtype=jnp.int32)
    distance = query_pos[:, None] - key_pos[None, :]
    same_doc = query_segs[:, None] == key_segs[None, :]
    inside = same_doc & (distance >= 0) & (distance < WINDOW)
    distant = same_doc & (distance >= WINDOW)
    exponent = jnp.exp(scores)
    weights = jnp.where(inside, exponent, jnp.where(distant, linear, 0.0))
    return (exponent, weights, inside, distant)


def attend_sequence(sequence, block_rows, score_scale):
    query_rows, qfeat_rows, key_rows, kfeat_rows, value_rows, segment_row = sequence
    starts = jnp.arange(query_rows.shape[0] // block_rows, dtype=jnp.int32) * block_rows

    def one_block(offset):
        query_block = lax.dynamic_slice_in_dim(query_rows, offset, block_rows, 0)
        qfeat_block = lax.dynamic_slice_in_dim(qfeat_rows, offset, block_rows, 0)
        query_segs = lax.dynamic_slice_in_dim(segment_row, offset, block_rows, 0)
        query_pos = offset + jnp.arange(block_rows, dtype=jnp.int32)
        exponent, weights, inside, distant = block_weights(
            query_block,
            qfeat_block,
            key_rows,
            kfeat_rows,
            query_segs,
            segment_row,
            query_pos,
            score_scale,
        )
        totals = jnp.sum(weights, axis=-1, keepdims=True)
        probabilities = (weights / totals).astype(jnp.bfloat16)
        attended = jnp.einsum(
            "kgij,jkd->ikgd", probabilities, value_rows, preferred_element_type=jnp.float32
        )
        return (attended.astype(jnp.bfloat16), totals)

    attended, totals = lax.map(one_block, starts)
    return (attended.reshape(query_rows.shape), totals)


def attend_back(sequence, block_rows, score_scale):
    query_rows, qfeat_rows, key_rows, kfeat_rows, value_rows, segment_row, totals, grad_rows = (
        sequence
    )
    starts = jnp.arange(query_rows.shape[0] // block_rows, dtype=jnp.int32) * block_rows
    initial = (
        jnp.zeros(key_rows.shape, jnp.float32),
        jnp.zeros(kfeat_rows.shape, jnp.float32),
        jnp.zeros(value_rows.shape, jnp.float32),
    )

    def one_block(running, packed):
        offset, block_totals = packed
        query_block = lax.dynamic_slice_in_dim(query_rows, offset, block_rows, 0)
        qfeat_block = lax.dynamic_slice_in_dim(qfeat_rows, offset, block_rows, 0)
        grad_block = lax.dynamic_slice_in_dim(grad_rows, offset, block_rows, 0)
        query_segs = lax.dynamic_slice_in_dim(segment_row, offset, block_rows, 0)
        query_pos = offset + jnp.arange(block_rows, dtype=jnp.int32)
        exponent, weights, inside, distant = block_weights(
            query_block,
            qfeat_block,
            key_rows,
            kfeat_rows,
            query_segs,
            segment_row,
            query_pos,
            score_scale,
        )
        probabilities = weights / block_totals
        grad_values = running[2] + jnp.einsum(
            "kgij,ikgd->jkd",
            probabilities.astype(jnp.bfloat16),
            grad_block,
            preferred_element_type=jnp.float32,
        )
        grad_probs = jnp.einsum(
            "ikgd,jkd->kgij", grad_block, value_rows, preferred_element_type=jnp.float32
        )
        grad_weights = (
            grad_probs - jnp.sum(grad_probs * probabilities, axis=-1, keepdims=True)
        ) / block_totals
        grad_scores = jnp.where(inside, grad_weights * exponent * score_scale, 0.0).astype(
            jnp.bfloat16
        )
        grad_linear = jnp.where(distant, grad_weights, 0.0).astype(jnp.bfloat16)
        grad_query = jnp.einsum(
            "kgij,jkd->ikgd", grad_scores, key_rows, preferred_element_type=jnp.float32
        )
        grad_qfeat = jnp.einsum(
            "kgij,jke->ikge", grad_linear, kfeat_rows, preferred_element_type=jnp.float32
        )
        grad_keys = running[0] + jnp.einsum(
            "kgij,ikgd->jkd", grad_scores, query_block, preferred_element_type=jnp.float32
        )
        grad_kfeat = running[1] + jnp.einsum(
            "kgij,ikge->jke", grad_linear, qfeat_block, preferred_element_type=jnp.float32
        )
        return ((grad_keys, grad_kfeat, grad_values), (grad_query, grad_qfeat))

    running, stacked = lax.scan(one_block, initial, (starts, totals))
    return (
        stacked[0].reshape(query_rows.shape),
        stacked[1].reshape(qfeat_rows.shape),
        running[0],
        running[1],
        running[2],
    )


def local(
    tokens,
    cotangent,
    segments,
    norm_gains,
    w_qkv,
    qkv_down,
    query_key_value_up,
    feature_maps,
    w_out,
    o_down,
    o_up,
    w_gate_up,
    w_down,
):
    token_rows, model_width = tokens.shape
    seq_count, seq_length = segments.shape
    local_kv = w_qkv.shape[1]
    group_size = HEADS // KVH
    query_span_width = group_size * HEAD_SIZE
    upper_key = query_span_width + HEAD_SIZE
    tensor_size = lax.axis_size("tensor")
    tensor_index = lax.axis_index("tensor")
    share_rows = token_rows // tensor_size
    share_start = tensor_index * share_rows
    score_scale = HEAD_SIZE ** (-0.5)
    block_rows = min(512, seq_length)
    cosines, sine_values = rotary_tables(seq_length, HEAD_SIZE)
    cosines = jnp.tile(cosines, (seq_count, 1))
    sine_values = jnp.tile(sine_values, (seq_count, 1))
    gain_rows = norm_gains.astype(jnp.float32)
    inputs = tokens.astype(jnp.float32)
    scaled_one, inverse_one, normed_one = normalize(inputs, gain_rows[0])
    lowrank_update = jnp.einsum(
        "td,jrd->tjr", normed_one, qkv_down, preferred_element_type=jnp.float32
    )
    up_maps_float = query_key_value_up.astype(jnp.float32)
    joined_adapters = jnp.einsum(
        "td,dkc->tkc", normed_one, w_qkv, preferred_element_type=jnp.float32
    ) + adapter_columns(lowrank_update, up_maps_float, query_span_width, HEAD_SIZE)
    queries = rotate(
        joined_adapters[:, :, :query_span_width].reshape(
            token_rows, local_kv, group_size, HEAD_SIZE
        ),
        cosines[:, None, None, :],
        sine_values[:, None, None, :],
    ).astype(jnp.bfloat16)
    keys_low = rotate(
        joined_adapters[:, :, query_span_width:upper_key],
        cosines[:, None, :],
        sine_values[:, None, :],
    ).astype(jnp.bfloat16)
    values_low = joined_adapters[:, :, upper_key:].astype(jnp.bfloat16)
    query_maps = feature_maps[:, :, :query_span_width].reshape(
        local_kv, HEAD_SIZE, group_size, HEAD_SIZE
    )
    key_maps = feature_maps[:, :, query_span_width:]
    query_logits = jnp.einsum(
        "tkgd,kdge->tkge", queries, query_maps, preferred_element_type=jnp.float32
    )
    key_logits = jnp.einsum("tkd,kde->tke", keys_low, key_maps, preferred_element_type=jnp.float32)
    query_feat = hedgehog(query_logits).astype(jnp.bfloat16)
    key_feat = hedgehog(key_logits).astype(jnp.bfloat16)

    def by_sequence(array):
        return array.reshape((seq_count, seq_length) + array.shape[1:])

    sequences = (
        by_sequence(queries),
        by_sequence(query_feat),
        by_sequence(keys_low),
        by_sequence(key_feat),
        by_sequence(values_low),
        segments,
    )
    attended, totals = lax.map(
        partial(attend_sequence, block_rows=block_rows, score_scale=score_scale), sequences
    )
    attended = attended.reshape(token_rows, local_kv * query_span_width)
    down_flat = o_down.reshape(o_down.shape[0], -1)
    lowrank_out = jnp.einsum("tc,rc->tr", attended, down_flat, preferred_element_type=jnp.float32)
    partial_out = jnp.dot(attended, w_out, preferred_element_type=jnp.float32) + jnp.dot(
        lowrank_out, o_up.astype(jnp.float32), precision=highest
    )
    hidden = inputs + lax.psum(partial_out.astype(jnp.bfloat16), "tensor").astype(jnp.float32)
    scaled_two, inverse_two, normed_input = normalize(hidden, gain_rows[1])
    gate_up = jnp.einsum("td,dsf->tsf", normed_input, w_gate_up, preferred_element_type=jnp.float32)
    gate_part = gate_up[:, 0]
    up_part = gate_up[:, 1]
    gate_sigmoid = jax.nn.sigmoid(gate_part)
    activated = gate_part * gate_sigmoid
    product = (activated * up_part).astype(jnp.bfloat16)
    partial_mlp = jnp.dot(product, w_down, preferred_element_type=jnp.float32)
    mixed = hidden + lax.psum(partial_mlp.astype(jnp.bfloat16), "tensor").astype(jnp.float32)
    output = lax.dynamic_slice_in_dim(mixed, share_start, share_rows, 0).astype(jnp.bfloat16)
    grad_product = jnp.einsum("td,fd->tf", cotangent, w_down, preferred_element_type=jnp.float32)
    grad_w_down = jnp.einsum("tf,td->fd", product, cotangent, preferred_element_type=jnp.float32)
    grad_gate = grad_product * up_part * gate_sigmoid * (1.0 + gate_part * (1.0 - gate_sigmoid))
    grad_up = grad_product * activated
    grad_gate_up = jnp.stack([grad_gate, grad_up], axis=1).astype(jnp.bfloat16)
    grad_w_gate_up = jnp.einsum(
        "td,tsf->dsf", normed_input, grad_gate_up, preferred_element_type=jnp.float32
    )
    grad_normed_two = jnp.einsum(
        "tsf,dsf->td", grad_gate_up, w_gate_up, preferred_element_type=jnp.float32
    )
    grad_normed_two = lax.psum(grad_normed_two.astype(jnp.bfloat16), "tensor").astype(jnp.float32)
    grad_hidden = cotangent.astype(jnp.float32) + norm_back(
        scaled_two, inverse_two, gain_rows[1], grad_normed_two
    )
    gain_two = jnp.sum(
        lax.dynamic_slice_in_dim(grad_normed_two, share_start, share_rows, 0)
        * lax.dynamic_slice_in_dim(scaled_two, share_start, share_rows, 0),
        axis=0,
    )
    grad_branch = grad_hidden.astype(jnp.bfloat16)
    grad_lowrank_out = jnp.einsum(
        "td,rd->tr", grad_branch, o_up, preferred_element_type=jnp.float32
    ).astype(jnp.bfloat16)
    grad_o_up = jnp.einsum(
        "tr,td->rd", lowrank_out, grad_branch, precision=highest, preferred_element_type=jnp.float32
    )
    grad_w_out = jnp.einsum("tc,td->cd", attended, grad_branch, preferred_element_type=jnp.float32)
    grad_o_down = jnp.einsum(
        "tr,tc->rc", grad_lowrank_out, attended, preferred_element_type=jnp.float32
    ).reshape(o_down.shape)
    grad_attended = (
        jnp.einsum("td,cd->tc", grad_branch, w_out, preferred_element_type=jnp.float32)
        + jnp.einsum("tr,rc->tc", grad_lowrank_out, down_flat, preferred_element_type=jnp.float32)
    ).astype(jnp.bfloat16)
    back_sequences = sequences + (
        totals,
        by_sequence(grad_attended.reshape(token_rows, local_kv, group_size, HEAD_SIZE)),
    )
    grad_queries, grad_qfeat, grad_keys, grad_kfeat, grad_values = lax.map(
        partial(attend_back, block_rows=block_rows, score_scale=score_scale), back_sequences
    )
    grad_queries = grad_queries.reshape(queries.shape)
    grad_qfeat = grad_qfeat.reshape(query_feat.shape)
    grad_keys = grad_keys.reshape(keys_low.shape)
    grad_kfeat = grad_kfeat.reshape(key_feat.shape)
    grad_values = grad_values.reshape(values_low.shape)
    grad_qlogits = hedgehog_back(query_logits, grad_qfeat).astype(jnp.bfloat16)
    grad_klogits = hedgehog_back(key_logits, grad_kfeat).astype(jnp.bfloat16)
    grad_queries = grad_queries + jnp.einsum(
        "tkge,kdge->tkgd", grad_qlogits, query_maps, preferred_element_type=jnp.float32
    )
    grad_keys = grad_keys + jnp.einsum(
        "tke,kde->tkd", grad_klogits, key_maps, preferred_element_type=jnp.float32
    )
    grad_query_maps = jnp.einsum(
        "tkgd,tkge->kdge", queries, grad_qlogits, preferred_element_type=jnp.float32
    ).reshape(local_kv, HEAD_SIZE, query_span_width)
    grad_key_maps = jnp.einsum(
        "tkd,tke->kde", keys_low, grad_klogits, preferred_element_type=jnp.float32
    )
    grad_feature_maps = jnp.concatenate([grad_query_maps, grad_key_maps], axis=2)
    grad_joined = jnp.concatenate(
        [
            rotate_back(
                grad_queries, cosines[:, None, None, :], sine_values[:, None, None, :]
            ).reshape(token_rows, local_kv, query_span_width),
            rotate_back(grad_keys, cosines[:, None, :], sine_values[:, None, :]),
            grad_values,
        ],
        axis=2,
    ).astype(jnp.bfloat16)
    grad_w_qkv = jnp.einsum(
        "td,tkc->dkc", normed_one, grad_joined, preferred_element_type=jnp.float32
    )
    grad_float = grad_joined.astype(jnp.float32)
    column_parts = (
        (0, query_span_width),
        (query_span_width, upper_key),
        (upper_key, upper_key + HEAD_SIZE),
    )
    grad_qkv_up = jnp.concatenate(
        [
            jnp.einsum(
                "tr,tkc->rkc",
                lowrank_update[:, index],
                grad_float[:, :, lower:upper],
                precision=highest,
            )
            for index, (lower, upper) in enumerate(column_parts)
        ],
        axis=2,
    )
    grad_lowrank = jnp.stack(
        [
            jnp.einsum(
                "tkc,rkc->tr",
                grad_joined[:, :, lower:upper],
                query_key_value_up[:, :, lower:upper],
                preferred_element_type=jnp.float32,
            )
            for lower, upper in column_parts
        ],
        axis=1,
    ).astype(jnp.bfloat16)
    grad_qkv_down = jnp.einsum(
        "tjr,td->jrd", grad_lowrank, normed_one, preferred_element_type=jnp.float32
    )
    grad_normed_one = jnp.einsum(
        "tkc,dkc->td", grad_joined, w_qkv, preferred_element_type=jnp.float32
    ) + jnp.einsum("tjr,jrd->td", grad_lowrank, qkv_down, preferred_element_type=jnp.float32)
    grad_normed_one = lax.psum(grad_normed_one.astype(jnp.bfloat16), "tensor").astype(jnp.float32)
    grad_first_share = lax.dynamic_slice_in_dim(grad_normed_one, share_start, share_rows, 0)
    scaled_share = lax.dynamic_slice_in_dim(scaled_one, share_start, share_rows, 0)
    inverse_share = lax.dynamic_slice_in_dim(inverse_one, share_start, share_rows, 0)
    grad_input = (
        lax.dynamic_slice_in_dim(grad_hidden, share_start, share_rows, 0)
        + norm_back(scaled_share, inverse_share, gain_rows[0], grad_first_share)
    ).astype(jnp.bfloat16)
    gain_one = jnp.sum(grad_first_share * scaled_share, axis=0)
    gain_grads = jnp.stack([gain_one, gain_two], axis=0)
    rows_qkv, rows_gate_up = (
        lax.psum_scatter(
            grad_w_qkv.astype(jnp.bfloat16), "dp", scatter_dimension=0, tiled=True
        ).astype(jnp.float32),
        lax.psum_scatter(
            grad_w_gate_up.astype(jnp.bfloat16), "dp", scatter_dimension=0, tiled=True
        ).astype(jnp.float32),
    )
    cols_out, cols_down = (
        lax.psum_scatter(
            grad_w_out.astype(jnp.bfloat16), "dp", scatter_dimension=1, tiled=True
        ).astype(jnp.float32),
        lax.psum_scatter(
            grad_w_down.astype(jnp.bfloat16), "dp", scatter_dimension=1, tiled=True
        ).astype(jnp.float32),
    )
    adapter_up, adapter_maps, adapter_down = (
        lax.psum_scatter(
            grad_qkv_up.astype(jnp.bfloat16), "dp", scatter_dimension=2, tiled=True
        ).astype(jnp.float32),
        lax.psum_scatter(
            grad_feature_maps.astype(jnp.bfloat16), "dp", scatter_dimension=2, tiled=True
        ).astype(jnp.float32),
        lax.psum_scatter(
            grad_o_down.astype(jnp.bfloat16), "dp", scatter_dimension=2, tiled=True
        ).astype(jnp.float32),
    )
    shared_gains, shared_down, shared_up = (
        lax.psum_scatter(gain_grads, ("dp", "tensor"), scatter_dimension=1, tiled=True),
        lax.psum_scatter(
            grad_qkv_down.reshape(-1, model_width),
            ("dp", "tensor"),
            scatter_dimension=1,
            tiled=True,
        ),
        lax.psum_scatter(grad_o_up, ("dp", "tensor"), scatter_dimension=1, tiled=True),
    )
    return (
        output,
        grad_input,
        shared_gains,
        rows_qkv,
        shared_down.reshape(3, -1, shared_down.shape[1]),
        adapter_up,
        adapter_maps,
        cols_out,
        adapter_down,
        shared_up,
        rows_gate_up,
        cols_down,
    )


def solution(mesh):
    in_specs = (
        P("dp", None),
        P("dp", None),
        P("dp", None),
        P(),
        P(None, "tensor", None),
        P(),
        P(None, "tensor", None),
        P("tensor", None, None),
        P("tensor", None),
        P(None, "tensor", None),
        P(),
        P(None, None, "tensor"),
        P("tensor", None),
    )
    out_specs = (
        P(("dp", "tensor"), None),
        P(("dp", "tensor"), None),
        P(None, ("dp", "tensor")),
        P("dp", "tensor", None),
        P(None, None, ("dp", "tensor")),
        P(None, "tensor", "dp"),
        P("tensor", None, "dp"),
        P("tensor", "dp"),
        P(None, "tensor", "dp"),
        P(None, ("dp", "tensor")),
        P("dp", None, "tensor"),
        P("tensor", "dp"),
    )
    return jax.shard_map(local, mesh=mesh, in_specs=in_specs, out_specs=out_specs, check_vma=False)
```

profile of v0, /device:TPU:12, one launch (start us, length us, event | category | flops | bytes accessed | tf_op | source)
XLA Modules:
  0.0 2022.4 jit_solution(998034077086791706)
XLA Ops:
  55.4 72.6 %while.55 = (s32[]{:T(128)}, bf16[2,512,2,4,64]{1,4,3,2,0:T(8,128)(2,1)}, f32[2,2,4,512,1]{3,2,1,4,0:T(4,128)S(1)}, s32[2]{0:T(128)S(1)}, s32[1024]{0:T(1024)S(1...) while((s32[]{:T(128)}, ...), condition=%wide.region_11.12_spmd, body=%wide.region_9.11_spmd.sunk | while | flops 2177102336 | bytes 76626144 | solution.py:147
  59.9 9.5 fusion.301
  69.5 12.8 bitcast_reduce_fusion.3
  82.3 9.3 fusion.303
  96.1 9.5 fusion.301
  105.6 12.8 bitcast_reduce_fusion.3
  118.4 9.3 fusion.303
  139.8 154.3 %all-reduce.7.cloned.1.call-done = bf16[1024,2048]{1,0:T(8,128)(2,1)} async-done(((bf16[1024,2048]{1,0:T(8,128)(2,1)}), bf16[1024,2048]{1,0:T(8,128)(2,1)}) %all-reduce.7.cloned.1.call-update) | async-done | bytes 4194320 | tf_op jit(solution)/shard_map/psum | solution.py:304
  294.1 6.9 convert_multiply_fusion
  300.9 11.9 broadcast_multiply_fusion
  312.9 25.2 %fusion.93 = f32[1024,2,2048]{2,0,1:T(8,128)} fusion(bf16[2048,2,2048]{2,1,0:T(2,128)(2,1)} %param.28, f32[1024,2048]{1,0:T(8,128)} %get-tuple-element.485, f32[2048]{0:T(1024)S(1)} %bitcast.408), kind=kOutput, calls=%fused_computation.94 | convolution fusion | flops 17184063488 | bytes 41951232 | tf_op jit(solution)/shard_map/td,dsf->tsf/dot_general | solution.py:306
  338.1 21.9 %fusion.101 = (bf16[1024,1,2048]{2,0,1:T(8,128)(2,1)}, bf16[1024,1,2048]{2,0,1:T(8,128)(2,1)}, bf16[1024,2048]{1,0:T(8,128)(2,1)}) fusion(f32[1024,2,2048]{2,0,1:T(8,128)} %fusion.93, bf16[1024,2048]{1,0:T(8,128)(2,1)} %param.18, bf16[2048,2048]{1,0:T(8,128)(2,1)} %param.29), kind=kOutput, calls=%fused_computation.123 | convolution fusion | flops 8621391872 | bytes 41943040 | tf_op jit(solution)/shard_map/td,fd->tf/dot_general | solution.py:315
  360.0 27.4 %bitcast_convert_fusion = bf16[1024,2048]{1,0:T(8,128)(2,1)} fusion(bf16[2048,2,2048]{2,1,0:T(2,128)(2,1)} %param.28, bf16[1024,1,2048]{2,0,1:T(8,128)(2,1)} %get-tuple-element.483, bf16[1024,1,2048]{2,0,1:T(8,128)(2,1)} %get-tuple-element.482), kind=kOutput, calls=%fused_computation.106 | convolution fusion | flops 17186160640 | bytes 29360128 | tf_op jit(solution)/shard_map/tsf,dsf->td/dot_general | solution.py:323
  387.5 14.3 convolution_convert_fusion.2
  401.8 139.8 %all-reduce.9.cloned.1.call-done = bf16[1024,2048]{1,0:T(8,128)(2,1)} async-done(((bf16[1024,2048]{1,0:T(8,128)(2,1)}), bf16[1024,2048]{1,0:T(8,128)(2,1)}) %all-reduce.9.cloned.1.call-update) | async-done | bytes 4194320 | tf_op jit(solution)/shard_map/psum | solution.py:326
  548.6 7.5 fusion.209
  563.1 279.0 %while.56 = (s32[]{:T(128)}, f32[1024,2,64]{0,2,1:T(8,128)}, f32[1024,2,128]{0,2,1:T(8,128)}, f32[1024,2,64]{0,2,1:T(8,128)}, f32[2,512,2,4,64]{1,0,4,3,2:T(2,12...) while((s32[]{:T(128)}, f32[1024,2,64]{0,2,1:T(8,128)}, ...), condition=%wide.region_19.20_spmd.clone, body=%wide.region_17.19_spmd.clone.sunk | while | flops 6514808320 | bytes 280051328 | solution.py:210
  567.8 9.7 fusion.320
  577.5 12.1 fusion.322
  589.6 22.7 %fusion.323 = (bf16[2,4,512,1024]{3,2,1,0:T(8,128)(2,1)}, bf16[2,4,512,1024]{3,2,1,0:T(8,128)(2,1)}) fusion(f32[2,512,4,1024]{3,1,2,0:T(8,128)} %fusion.320, pred[512,1024]{1,0:T(8,128)(4,1)} %copy-done.14, f32[2,4,512]{2,1,0:T(4,128)S(1)} %dynamic-slice_bitcast_fusion.2, f32[2,4,512,1024]{3,2,1,0:T(8,128)} %fusion.322, ...), kind=kOutput, calls=%fused_computation.31.clone.1 | convolution fusion | flops 1111495680 | bytes 52446208 | tf_op jit(solution)/shard_map/while/body/eval_jaxpr/while/body/eval_jaxpr/sub | solution.py:190
  612.3 8.5 fusion.326
  638.2 6.0 copy.239
  644.2 19.6 dynamic_update_slice.46
  663.8 38.1 %dynamic_update_slice.47 = f32[2,512,2,4,128]{1,0,4,3,2:T(2,128)} dynamic-update-slice(f32[2,512,2,4,128]{1,0,4,3,2:T(2,128)} %get-tuple-element.747, f32[1,512,2,4,128]{1,0,4,3,2:T(1,128)} %copy.239, s32[]{:T(128)S(6)} %copy.261, s32[]{:T(128)} %constant.79.clone.1..sunk.1, s32[]{:T(128)} %constant.79.clone.1..sunk.1, s32[]{:T(128)} %constant.79.clone.1..sunk.1, s32[]{:T(128)} %constant.79.clone.1..sunk.1) | dynamic-update-slice | bytes 4194308 | tf_op jit(solution)/shard_map/while/body/eval_jaxpr/while/body/jit(dynamic_update_index_in_dim)/dynamic_update_slice | solution.py:210
  706.5 9.6 fusion.320
  716.1 12.1 fusion.322
  728.3 22.7 %fusion.323 = (bf16[2,4,512,1024]{3,2,1,0:T(8,128)(2,1)}, bf16[2,4,512,1024]{3,2,1,0:T(8,128)(2,1)}) fusion(f32[2,512,4,1024]{3,1,2,0:T(8,128)} %fusion.320, pred[512,1024]{1,0:T(8,128)(4,1)} %copy-done.14, f32[2,4,512]{2,1,0:T(4,128)S(1)} %dynamic-slice_bitcast_fusion.2, f32[2,4,512,1024]{3,2,1,0:T(8,128)} %fusion.322, ...), kind=kOutput, calls=%fused_computation.31.clone.1 | convolution fusion | flops 1111495680 | bytes 52446208 | tf_op jit(solution)/shard_map/while/body/eval_jaxpr/while/body/eval_jaxpr/sub | solution.py:190
  751.0 8.5 fusion.326
  784.0 19.6 dynamic_update_slice.46
  803.6 38.1 %dynamic_update_slice.47 = f32[2,512,2,4,128]{1,0,4,3,2:T(2,128)} dynamic-update-slice(f32[2,512,2,4,128]{1,0,4,3,2:T(2,128)} %get-tuple-element.747, f32[1,512,2,4,128]{1,0,4,3,2:T(1,128)} %copy.239, s32[]{:T(128)S(6)} %copy.261, s32[]{:T(128)} %constant.79.clone.1..sunk.1, s32[]{:T(128)} %constant.79.clone.1..sunk.1, s32[]{:T(128)} %constant.79.clone.1..sunk.1, s32[]{:T(128)} %constant.79.clone.1..sunk.1) | dynamic-update-slice | bytes 4194308 | tf_op jit(solution)/shard_map/while/body/eval_jaxpr/while/body/jit(dynamic_update_index_in_dim)/dynamic_update_slice | solution.py:210
  858.1 6.6 reshape.241
  872.6 8.6 bitcast_add_fusion.1
  904.9 7.6 fusion.145
  920.2 7.8 convolution_bitcast_fusion.2
  932.8 6.2 convolution_convert_fusion.4
  939.3 8.5 convolution_convert_fusion.3
  947.9 14.1 convolution_convert_fusion.1
  967.3 218.6 %all-reduce.13.cloned.1.call-done = (bf16[1024,2048]{1,0:T(8,128)(2,1)}, bf16[1024,2048]{1,0:T(8,128)(2,1)}) async-done(((bf16[1024,2048]{1,0:T(8,128)(2,1)}, bf16[1024,2048]{1,0:T(8,128)(2,1)}), (bf16[1024,2048]{1,0:T(8,128)(2,1)}, bf16[1024,2048]{1,0:T(8,128)(2,1)})) %all-reduce.13.cloned.1.call-update) | async-done | bytes 8388624 | tf_op jit(solution)/shard_map/psum | solution.py:313
  1190.1 26.2 %convolution_convert_fusion = bf16[2048,2,2048]{2,0,1:T(8,128)(2,1)} fusion(bf16[1024,1,2048]{2,0,1:T(8,128)(2,1)} %get-tuple-element.483, bf16[1024,1,2048]{2,0,1:T(8,128)(2,1)} %get-tuple-element.482, f32[1024,2048]{1,0:T(8,128)} %get-tuple-element.485, f32[2048]{0:T(1024)S(1)} %bitcast.411), kind=kOutput, calls=%fused_computation.99 | convolution fusion | flops 17209229312 | bytes 33562624 | tf_op jit(solution)/shard_map/td,tsf->dsf/dot_general | solution.py:320
  1224.4 34.7 %reduce-scatter.33.cloned.1.call-done = bf16[48,16]{1,0:T(8,128)(2,1)} async-done(((bf16[384,16]{1,0:T(8,128)(2,1)}), bf16[48,16]{1,0:T(8,128)(2,1)}) %reduce-scatter.33.cloned.1.call-update) | async-done | bytes 1552
  1260.7 55.1 %all-reduce.11.cloned.1.call-done = bf16[2,64,320]{1,2,0:T(8,128)(2,1)} async-done(((bf16[2,64,320]{1,2,0:T(8,128)(2,1)}), bf16[2,64,320]{1,2,0:T(8,128)(2,1)}) %all-reduce.11.cloned.1.call-update) | async-done | bytes 81936
  1317.2 133.2 %reduce-scatter.37.cloned.1.call-done = f32[64,8]{1,0:T(8,128)} async-done(((f32[2048,8]{1,0:T(8,128)}), f32[64,8]{1,0:T(8,128)}) %reduce-scatter.37.cloned.1.call-update) | async-done | bytes 2064
  1451.7 133.4 %reduce-scatter.31.cloned.1.call-done = f32[64,24]{1,0:T(8,128)} async-done(((f32[2048,24]{1,0:T(8,128)}), f32[64,24]{1,0:T(8,128)}) %reduce-scatter.31.cloned.1.call-update) | async-done | bytes 6160
  1586.5 44.4 %reduce-scatter.23.cloned.1.call-done = bf16[512,256]{1,0:T(8,128)(2,1)} async-done(((bf16[512,2048]{1,0:T(8,128)(2,1)}), bf16[512,256]{1,0:T(8,128)(2,1)}) %reduce-scatter.23.cloned.1.call-update) | async-done | bytes 262160 | tf_op jit(solution)/shard_map/reduce_scatter | solution.py:445
  1632.7 47.7 %reduce-scatter.21.cloned.1.call-done = bf16[256,2,384]{2,0,1:T(8,128)(2,1)} async-done(((bf16[2048,2,384]{2,0,1:T(8,128)(2,1)}), bf16[256,2,384]{2,0,1:T(8,128)(2,1)}) %reduce-scatter.21.cloned.1.call-update) | async-done | bytes 393232 | tf_op jit(solution)/shard_map/reduce_scatter | solution.py:437
  1682.7 72.8 %reduce-scatter.27.cloned.1.call-done = bf16[2048,256]{1,0:T(8,128)(2,1)} async-done(((bf16[2048,2048]{1,0:T(8,128)(2,1)}), bf16[2048,256]{1,0:T(8,128)(2,1)}) %reduce-scatter.27.cloned.1.call-update) | async-done | bytes 1048592 | tf_op jit(solution)/shard_map/reduce_scatter | solution.py:448
  1765.4 123.9 %reduce-scatter.29.cloned.1.call-done = f32[64,2]{1,0:T(8,128)} async-done(((f32[2048,2]{1,0:T(8,128)}), f32[64,2]{1,0:T(8,128)}) %reduce-scatter.29.cloned.1.call-update) | async-done | bytes 528
  1890.7 118.9 %reduce-scatter.25.cloned.1.call-done = bf16[256,2,2048]{2,0,1:T(8,128)(2,1)} async-done(((bf16[2048,2,2048]{2,0,1:T(8,128)(2,1)}), bf16[256,2,2048]{2,0,1:T(8,128)(2,1)}) %reduce-scatter.25.cloned.1.call-update) | async-done | bytes 2097168 | tf_op jit(solution)/shard_map/reduce_scatter | solution.py:440
  (329 shorter events, 229.2 us)
Async XLA Ops:
  7.2 10.3 copy-start
  7.2 286.9 %all-reduce.7.cloned.1.call-start = ((), (), s32[]{:S(2)}) async-start(), calls=%async_computation.9 | async-start | bytes 8388608 | tf_op jit(solution)/shard_map/psum | solution.py:304
  8.6 7.8 copy-start.34
  24.8 10.4 copy-start.17
  27.8 14.9 copy-start.58
  29.9 12.8 copy-start.56
  38.7 11.0 copy-start.46
  42.0 7.6 copy-start.47
  59.9 9.5 copy-start.2
  96.1 9.5 copy-start.2
  139.7 154.4 %copy-start.50 = (f32[1024]{0:T(1024)S(1)}, f32[1024]{0:T(1024)}, u32[]{:S(2)}) copy-start(f32[1024]{0:T(1024)} %copy-done.49) | copy-start | bytes 12292
  139.7 401.9 %all-reduce.9.cloned.1.call-start = ((), (), s32[]{:S(2)}) async-start(), calls=%async_computation.10 | async-start | bytes 8388608 | tf_op jit(solution)/shard_map/psum | solution.py:326
  300.9 11.9 copy-start.39
  387.4 798.5 %all-reduce.13.cloned.1.call-start = ((), (), s32[]{:S(2)}) async-start(), calls=%async_computation.21 | async-start | bytes 16777216 | tf_op jit(solution)/shard_map/psum | solution.py:313
  563.1 280.1 %copy-start.45 = (bf16[8,2,64]{2,1,0:T(2,128)(2,1)S(1)}, bf16[8,2,64]{2,1,0:T(2,128)(2,1)}, u32[]{:S(2)}) copy-start(bf16[8,2,64]{2,1,0:T(2,128)(2,1)} %copy-done.44) | copy-start | bytes 6148
  567.7 9.7 copy-start.12
  567.8 9.7 copy-start.14
  567.8 9.7 copy-start.7
  567.8 9.7 copy-start.9
  612.3 8.6 copy-start.1
  612.3 8.6 copy-start.3
  626.1 8.4 slice-start
  706.5 9.7 copy-start.12
  706.5 9.7 copy-start.14
  706.5 9.7 copy-start.7
  706.5 9.7 copy-start.9
  751.0 8.6 copy-start.1
  751.0 8.7 copy-start.3
  765.8 8.4 slice-start
  843.2 7.3 copy-start.18
  845.0 9.3 copy-start.55
  895.2 327.7 %reduce-scatter.35.cloned.1.call-start = ((), (), s32[]{:S(2)}) async-start(), calls=%async_computation.18 | async-start | bytes 73728
  904.9 7.6 copy-start.28
  904.9 15.3 copy-start.26
  913.6 14.5 copy-start.38
  913.6 14.5 copy-start.42
  915.8 12.3 copy-start.51
  915.8 12.4 copy-start.53
  915.8 343.4 %reduce-scatter.33.cloned.1.call-start = ((), (), s32[]{:S(2)}) async-start(), calls=%async_computation.17 | async-start | bytes 110592
  918.5 397.3 %all-reduce.11.cloned.1.call-start = ((), (), s32[]{:S(2)}) async-start(), calls=%async_computation.20 | async-start | bytes 327680
  920.2 530.2 %reduce-scatter.37.cloned.1.call-start = ((), (), s32[]{:S(2)}) async-start(), calls=%async_computation.19 | async-start | bytes 1081344
  928.0 657.1 %reduce-scatter.31.cloned.1.call-start = ((), (), s32[]{:S(2)}) async-start(), calls=%async_computation.16 | async-start | bytes 1081344
  932.8 698.1 %reduce-scatter.23.cloned.1.call-start = ((), (), s32[]{:S(2)}) async-start(), calls=%async_computation.12 | async-start | bytes 2359296 | tf_op jit(solution)/shard_map/reduce_scatter | solution.py:445
  939.0 741.4 %reduce-scatter.21.cloned.1.call-start = ((), (), s32[]{:S(2)}) async-start(), calls=%async_computation.11 | async-start | bytes 3538944 | tf_op jit(solution)/shard_map/reduce_scatter | solution.py:437
  947.9 807.7 %reduce-scatter.27.cloned.1.call-start = ((), (), s32[]{:S(2)}) async-start(), calls=%async_computation.14 | async-start | bytes 9437184 | tf_op jit(solution)/shard_map/reduce_scatter | solution.py:448
  962.0 927.2 %reduce-scatter.29.cloned.1.call-start = ((), (), s32[]{:S(2)}) async-start(), calls=%async_computation.15 | async-start | bytes 1081344
  965.4 224.8 %copy-start.40 = (f32[1,2048]{1,0:T(1,128)S(1)}, f32[1,2048]{1,0:T(1,128)}, u32[]{:S(2)}) copy-start(f32[1,2048]{1,0:T(1,128)} %get-tuple-element.499) | copy-start | bytes 24580
  1189.8 819.7 %reduce-scatter.25.cloned.1.call-start = ((), (), s32[]{:S(2)}) async-start(), calls=%async_computation.13 | async-start | bytes 18874368 | tf_op jit(solution)/shard_map/reduce_scatter | solution.py:440
  (47 other events, 181.0 us)
Sparse Core Ops, SparseCore 0:
  139.8 154.1 all-reduce.6
  387.6 153.9 all-reduce.8
  895.3 290.5 all-reduce.12
  1188.8 34.1 reduce-scatter.34
  1226.7 32.4 reduce-scatter.32
  1263.0 52.7 all-reduce.10
  1318.7 131.5 reduce-scatter.36
  1453.1 131.9 reduce-scatter.30
  1589.3 41.5 reduce-scatter.22
  1634.1 46.2 reduce-scatter.20
  1684.3 71.2 reduce-scatter.26
  1757.6 131.5 reduce-scatter.28
  1893.3 116.2 reduce-scatter.24
where the time goes:
time: 2040 us; the launch traced here: 2020 us
  waiting for transfers between devices  1280 us (63%)
  matrix products  427 us (21%)
  local copies, waits for them, and re-layouts  200 us (10%)
  other arithmetic  87.8 us (4%)
    unnamed x19, waiting for transfers between devices  485 us
    psum x1, waiting for transfers between devices, local(): lax.psum(partial_mlp.astype(jnp.bfloat16), 'tensor').astype(jnp.float32)  219 us
    psum x1, waiting for transfers between devices, local(): lax.psum(partial_out.astype(jnp.bfloat16), 'tensor').astype(jnp.float32)  154 us
    psum x1, waiting for transfers between devices, local(): lax.psum(grad_normed_two.astype(jnp.bfloat16), 'tensor').astype(jnp.float32)  140 us
    dynamic_update_slice x8, local copies, waits for them, and re-layouts, attend_back(): running, stacked = lax.scan(one_block, initial, (starts, totals))  132 us
    reduce_scatter x1, waiting for transfers between devices, local(): lax.psum_scatter(grad_w_gate_up.astype(jnp.bfloat16), 'dp', scatter_dimen...  119 us
    reduce_scatter x1, waiting for transfers between devices, local(): lax.psum_scatter(grad_w_down.astype(jnp.bfloat16), 'dp', scatter_dimensio...  72.8 us
    reduce_scatter x1, waiting for transfers between devices, local(): lax.psum_scatter(grad_w_qkv.astype(jnp.bfloat16), 'dp', scatter_dimension...  47.7 us
  transfers between devices with their start and end apart: 13, of which 13 were waited for; matrix products, arithmetic and copies ran while one was open for 7% of the time, Pallas kernels for 0%

commit v1 on v0

v1 whole, which is shorter than its diff:
```python
from functools import partial
import jax, jax.numpy as jnp
from jax import lax
from jax.experimental import pallas as pl
from jax.experimental.pallas import tpu as pltpu
from jax.sharding import PartitionSpec as P

HEADS = 32
KVH = 8
HEAD_SIZE = 64
WINDOW = 64
LONGEST = 512
epsilon = 1e-05
rope_base = 500000.0
F32 = jnp.float32
BF16 = jnp.bfloat16


def nn(a, b):
    return lax.dot_general(a, b, (((1,), (0,)), ((), ())), preferred_element_type=F32)


def nt(a, b):
    return lax.dot_general(a, b, (((1,), (1,)), ((), ())), preferred_element_type=F32)


def rotate_t(part, cosines, sines):
    half = part.shape[0] // 2
    a, b = part[:half], part[half:]
    return jnp.concatenate([a * cosines - b * sines, b * cosines + a * sines], axis=0)


def rotate_back_t(part, cosines, sines):
    half = part.shape[0] // 2
    a, b = part[:half], part[half:]
    return jnp.concatenate([a * cosines + b * sines, b * cosines - a * sines], axis=0)


def softmaxes_t(logits):
    up = jnp.exp(logits - jnp.max(logits, axis=0, keepdims=True))
    down = jnp.exp(jnp.min(logits, axis=0, keepdims=True) - logits)
    up = up * (1.0 / jnp.sum(up, axis=0, keepdims=True))
    down = down * (1.0 / jnp.sum(down, axis=0, keepdims=True))
    return up, down


def tile_plan(length, block):
    back = LONGEST // block
    return [(i, list(range(max(0, i - back), i + 1))) for i in range(length // block)]


def tile_masks(same, query_block, key_block, block):
    lowest = (query_block - key_block) * block - (block - 1)
    if lowest >= WINDOW:
        return None, same
    shape = (block, block)
    distance = (
        lax.broadcasted_iota(jnp.int32, shape, 1)
        - lax.broadcasted_iota(jnp.int32, shape, 0)
        + (query_block - key_block) * block
    )
    inside = same & (distance < WINDOW)
    if lowest < 0:
        inside = inside & (distance >= 0)
    return inside, same & (distance >= WINDOW)


def forward_kernel(heads, block, joined_ref, cos_ref, sin_ref, map_ref, row_ref, col_ref,
                   low_ref, att_ref, root_ref, keys, kfeat):
    length = cos_ref.shape[1]
    width = heads * HEAD_SIZE
    scale = HEAD_SIZE ** -0.5
    key_t = rotate_t(joined_ref[0, width:width + HEAD_SIZE], cos_ref[...], sin_ref[...]).astype(BF16)
    low_ref[0, width:width + HEAD_SIZE] = key_t
    value_t = joined_ref[0, width + HEAD_SIZE:].astype(BF16)
    low_ref[0, width + HEAD_SIZE:] = value_t
    up, down = softmaxes_t(nn(map_ref[0, width:], key_t))
    kfeat[...] = jnp.concatenate([up, down], axis=0).T.astype(BF16)
    keys[...] = key_t.astype(F32).T.astype(BF16)

    for i, tiles in tile_plan(length, block):
        cols = slice(i * block, (i + 1) * block)

        def one_head(h, carry, i=i, tiles=tiles, cols=cols):
            rows = pl.ds(pl.multiple_of(h * HEAD_SIZE, HEAD_SIZE), HEAD_SIZE)
            query = rotate_t(joined_ref[0, rows, cols], cos_ref[:, cols], sin_ref[:, cols]).astype(BF16)
            low_ref[0, rows, cols] = query
            up, down = softmaxes_t(nn(map_ref[0, rows], query))
            feat = jnp.concatenate([up, down], axis=0).astype(BF16)
            weights = []
            total = None
            for j in tiles:
                span = slice(j * block, (j + 1) * block)
                same = col_ref[span, :] == row_ref[:, cols]
                inside, far = tile_masks(same, i, j, block)
                linear = nn(kfeat[span, :], feat)
                w = jnp.where(far, linear, 0.0)
                if inside is not None:
                    w = jnp.where(inside, jnp.exp(nn(keys[span, :], query) * scale), w)
                part = jnp.sum(w, axis=0, keepdims=True)
                total = part if total is None else total + part
                weights.append(w)
            root = lax.rsqrt(total)
            root_ref[0, h, :, cols] = root
            att = None
            for j, w in zip(tiles, weights):
                p = (w * root * root).astype(BF16)
                piece = nn(low_ref[0, width + HEAD_SIZE:, j * block:(j + 1) * block], p)
                att = piece if att is None else att + piece
            att_ref[0, rows, cols] = att.astype(BF16)
            return carry

        lax.fori_loop(0, heads, one_head, 0)


def attention_forward(joined_t, cosines, sines, maps_t, seg_row, seg_col, heads, block=256):
    groups, width, length = joined_t.shape
    qw = heads * HEAD_SIZE
    whole = lambda shape: pl.BlockSpec(shape, lambda g: (0,) * len(shape))
    mine = lambda shape: pl.BlockSpec((1,) + shape, lambda g: (g,) + (0,) * len(shape))
    return pl.pallas_call(
        partial(forward_kernel, heads, block),
        grid=(groups,),
        out_shape=(
            jax.ShapeDtypeStruct((groups, width, length), BF16),
            jax.ShapeDtypeStruct((groups, qw, length), BF16),
            jax.ShapeDtypeStruct((groups, heads, 1, length), F32),
        ),
        in_specs=[mine((width, length)), whole(cosines.shape), whole(sines.shape),
                  mine(maps_t.shape[1:]), whole(seg_row.shape), whole(seg_col.shape)],
        out_specs=(mine((width, length)), mine((qw, length)), mine((heads, 1, length))),
        scratch_shapes=[pltpu.VMEM((length, HEAD_SIZE), BF16), pltpu.VMEM((length, 2 * HEAD_SIZE), BF16)],
        compiler_params=pltpu.CompilerParams(vmem_limit_bytes=48 * 2**20),
        name="attention_forward",
    )(joined_t, cosines, sines, maps_t, seg_row, seg_col)


def backward_kernel(heads, block, low_ref, cos_ref, sin_ref, map_ref, back_ref, row_ref, col_ref,
                    att_ref, root_ref, gatt_ref, grad_ref, gmap_ref,
                    keys, kfeat, kfeat_t, values, gkeys, gkfeat, gvalues):
    length = cos_ref.shape[1]
    width = heads * HEAD_SIZE
    scale = HEAD_SIZE ** -0.5
    key_t = low_ref[0, width:width + HEAD_SIZE]
    key_up, key_down = softmaxes_t(nn(map_ref[0, width:], key_t))
    both = jnp.concatenate([key_up, key_down], axis=0)
    kfeat_t[...] = both.astype(BF16)
    kfeat[...] = both.T.astype(BF16)
    keys[...] = key_t.astype(F32).T.astype(BF16)
    values[...] = low_ref[0, width + HEAD_SIZE:].astype(F32).T.astype(BF16)
    gkeys[...] = jnp.zeros_like(gkeys)
    gkfeat[...] = jnp.zeros_like(gkfeat)
    gvalues[...] = jnp.zeros_like(gvalues)
    gmap_ref[...] = jnp.zeros_like(gmap_ref)

    for i, tiles in tile_plan(length, block):
        cols = slice(i * block, (i + 1) * block)

        def one_head(h, carry, i=i, tiles=tiles, cols=cols):
            rows = pl.ds(pl.multiple_of(h * HEAD_SIZE, HEAD_SIZE), HEAD_SIZE)
            query = low_ref[0, rows, cols]
            gatt = gatt_ref[0, rows, cols]
            up, down = softmaxes_t(nn(map_ref[0, rows], query))
            feat = jnp.concatenate([up, down], axis=0).astype(BF16)
            root = root_ref[0, h, :, cols]
            inverse = root * root
            delta = jnp.sum(gatt.astype(F32) * att_ref[0, rows, cols].astype(F32), axis=0, keepdims=True)
            gquery = jnp.zeros((HEAD_SIZE, block), F32)
            gfeat = jnp.zeros((2 * HEAD_SIZE, block), F32)
            for j in tiles:
                span = slice(j * block, (j + 1) * block)
                same = col_ref[span, :] == row_ref[:, cols]
                inside, far = tile_masks(same, i, j, block)
                gprob = nn(values[span, :], gatt) - delta
                grad_far = jnp.where(far, gprob * root * root, 0.0).astype(BF16)
                p = jnp.where(far, nn(kfeat[span, :], feat) * root * root, 0.0)
                if inside is not None:
                    near = jnp.where(inside, jnp.exp(nn(keys[span, :], query) * scale) * root * root, 0.0)
                    p = jnp.where(inside, near, p)
                    grad_near = (near * gprob * scale).astype(BF16)
                    gquery = gquery + nn(low_ref[0, width:width + HEAD_SIZE, span], grad_near)
                    gkeys[span, :] += nt(grad_near, query)
                gvalues[span, :] += nt(p.astype(BF16), gatt)
                gfeat = gfeat + nn(kfeat_t[:, span], grad_far)
                gkfeat[span, :] += nt(grad_far, feat)
            glogits = softmaxes_back_t(up, down, gfeat)
            gquery = gquery + nn(back_ref[0, h], glogits)
            gmap_ref[0, h] += nt(query, glogits)
            grad_ref[0, rows, cols] = rotate_back_t(gquery, cos_ref[:, cols], sin_ref[:, cols]).astype(BF16)
            return carry

        lax.fori_loop(0, heads, one_head, 0)
    glogits = softmaxes_back_t(key_up, key_down, gkfeat[...].T)
    gkey_t = gkeys[...].T + nn(back_ref[0, heads], glogits)
    gmap_ref[0, heads] = nt(key_t, glogits)
    grad_ref[0, width:width + HEAD_SIZE] = rotate_back_t(gkey_t, cos_ref[...], sin_ref[...]).astype(BF16)
    grad_ref[0, width + HEAD_SIZE:] = gvalues[...].T.astype(BF16)


def softmaxes_back_t(up, down, grads):
    gup, gdown = grads[:HEAD_SIZE], grads[HEAD_SIZE:]
    return (
        up * (gup - jnp.sum(gup * up, axis=0, keepdims=True))
        - down * (gdown - jnp.sum(gdown * down, axis=0, keepdims=True))
    ).astype(BF16)


def attention_backward(low, cosines, sines, maps_t, maps, seg_row, seg_col, att, root, gatt, heads, block=256):
    groups, width, length = low.shape
    qw = heads * HEAD_SIZE
    whole = lambda shape: pl.BlockSpec(shape, lambda g: (0,) * len(shape))
    mine = lambda shape: pl.BlockSpec((1,) + shape, lambda g: (g,) + (0,) * len(shape))
    return pl.pallas_call(
        partial(backward_kernel, heads, block),
        grid=(groups,),
        out_shape=(
            jax.ShapeDtypeStruct((groups, width, length), BF16),
            jax.ShapeDtypeStruct((groups, heads + 1, HEAD_SIZE, HEAD_SIZE), F32),
        ),
        in_specs=[mine((width, length)), whole(cosines.shape), whole(sines.shape),
                  mine(maps_t.shape[1:]), mine(maps.shape[1:]), whole(seg_row.shape), whole(seg_col.shape),
                  mine((qw, length)), mine((heads, 1, length)), mine((qw, length))],
        out_specs=(mine((width, length)), mine((heads + 1, HEAD_SIZE, HEAD_SIZE))),
        scratch_shapes=[
            pltpu.VMEM((length, HEAD_SIZE), BF16), pltpu.VMEM((length, 2 * HEAD_SIZE), BF16),
            pltpu.VMEM((2 * HEAD_SIZE, length), BF16), pltpu.VMEM((length, HEAD_SIZE), BF16),
            pltpu.VMEM((length, HEAD_SIZE), F32), pltpu.VMEM((length, 2 * HEAD_SIZE), F32),
            pltpu.VMEM((length, HEAD_SIZE), F32)],
        compiler_params=pltpu.CompilerParams(vmem_limit_bytes=48 * 2**20),
        name="attention_backward",
    )(low, cosines, sines, maps_t, maps, seg_row, seg_col, att, root, gatt)


def rotary_tables_t(length, width):
    half = width // 2
    frequency = rope_base ** (-(jnp.arange(half, dtype=F32) * 2.0) / width)
    angles = frequency[:, None] * jnp.arange(length, dtype=F32)[None, :]
    return jnp.cos(angles), jnp.sin(angles)


def normalize(values, gain_row):
    inverse = lax.rsqrt(jnp.mean(values * values, axis=-1, keepdims=True) + epsilon)
    scaled = values * inverse
    return scaled, inverse, (scaled * gain_row).astype(BF16)


def ring(size, shift=1):
    return [(i, (i + shift) % size) for i in range(size)]


def flip(size, bit):
    return [(i, i ^ (1 << bit)) for i in range(size)]


def pick(array, index, axis):
    return lax.dynamic_index_in_dim(array, index, axis, keepdims=False)


def chunk_of(array, index, rows, axis):
    return lax.dynamic_slice_in_dim(array, index * rows, rows, axis)


def ring_sum(parts):
    size = len(parts)
    running = parts[1].astype(BF16)
    for step in range(2, size + 1):
        arrived = lax.ppermute(running, "tensor", ring(size)).astype(F32)
        running = arrived + parts[step % size].astype(F32)
        if step < size:
            running = running.astype(BF16)
    return running


def bits_of(size):
    return size.bit_length() - 1


def halve(current, axis, order, left=None):
    size = lax.axis_size("dp")
    mine = lax.axis_index("dp")
    remaining = sorted(order, reverse=True)
    shape = current.shape
    current = current.reshape(shape[:axis] + (2,) * len(remaining) + shape[axis + 1:])
    for place, bit in enumerate(order):
        where = axis + remaining.index(bit)
        own = (mine >> bit) & 1
        arrived = lax.ppermute(pick(current, 1 - own, where), "dp", flip(size, bit))
        current = pick(current, own, where).astype(F32) + arrived.astype(F32)
        remaining.remove(bit)
        if place < len(order) - 1:
            current = current.astype(BF16)
    return current


def scatter_dp(make, axis, stream_axis):
    size = lax.axis_size("dp")
    core = lax.axis_index("dp") & 1
    arrived = lax.ppermute(make(1 - core).astype(BF16), "dp", flip(size, 0))
    current = (make(core) + arrived.astype(F32)).astype(BF16)
    rest = list(range(1, bits_of(size)))
    half = current.shape[stream_axis] // 2
    first = halve(lax.slice_in_dim(current, 0, half, axis=stream_axis), axis, rest)
    second = halve(lax.slice_in_dim(current, half, 2 * half, axis=stream_axis), axis, rest[::-1])
    return jnp.concatenate([first, second], axis=stream_axis - (1 if stream_axis > axis else 0))


def scatter_small(blocks, over_tensor):
    size = lax.axis_size("dp")
    for bit in reversed(range(bits_of(size))):
        own = (lax.axis_index("dp") >> bit) & 1
        blocks = blocks.reshape((2, blocks.shape[0] // 2) + blocks.shape[1:])
        blocks = pick(blocks, own, 0) + lax.ppermute(pick(blocks, 1 - own, 0), "dp", flip(size, bit))
    blocks = blocks[0]
    if over_tensor:
        size = lax.axis_size("tensor")
        for bit in reversed(range(bits_of(size))):
            own = (lax.axis_index("tensor") >> bit) & 1
            blocks = blocks.reshape((2, blocks.shape[0] // 2) + blocks.shape[1:])
            blocks = pick(blocks, own, 0) + lax.ppermute(
                pick(blocks, 1 - own, 0), "tensor", flip(size, bit)
            )
        blocks = blocks[0]
    return blocks


def double(pieces, order):
    size = lax.axis_size("dp")
    mine = lax.axis_index("dp")
    n, rows, cols = pieces.shape
    done = []
    current = pieces.reshape((n, rows, cols))
    for bit in order:
        arrived = lax.ppermute(current, "dp", flip(size, bit))
        own = ((mine >> bit) & 1) == 0
        place = 1 + sum(1 for other in done if other > bit)
        low = jnp.where(own, current, arrived)
        high = jnp.where(own, arrived, current)
        current = jnp.stack([low, high], axis=place)
        done.append(bit)
    return current.reshape(n, size * rows, cols)


def gather_weight(shard):
    size = lax.axis_size("dp")
    n = lax.axis_size("tensor")
    rows = shard.shape[0] // size
    pieces = [chunk_of(shard, lax.axis_index("dp"), rows, 0)]
    for _ in range(n - 1):
        pieces.append(lax.ppermute(pieces[-1], "tensor", ring(n)))
    pieces = jnp.stack(pieces)
    half = shard.shape[1] // 2
    rest = list(range(1, bits_of(size)))
    first = double(pieces[:, :, :half], rest + [0])
    second = double(pieces[:, :, half:], rest[::-1] + [0])
    return jnp.concatenate([first, second], axis=2)


def local(
    tokens,
    cotangent,
    segments,
    norm_gains,
    w_qkv,
    qkv_down,
    query_key_value_up,
    feature_maps,
    w_out,
    o_down,
    o_up,
    w_gate_up,
    w_down,
):
    token_rows, model_width = tokens.shape
    groups = w_qkv.shape[1]
    heads = HEADS // KVH
    query_width = heads * HEAD_SIZE
    joined_width = w_qkv.shape[2]
    rank = o_up.shape[0]
    dp = lax.axis_size("dp")
    n = lax.axis_size("tensor")
    me = lax.axis_index("tensor")
    share = token_rows // n
    gains = norm_gains.astype(F32)
    cosines, sines = rotary_tables_t(token_rows, HEAD_SIZE)
    dot = partial(jnp.einsum, preferred_element_type=F32)

    up = query_key_value_up.astype(BF16)
    edges = ((0, query_width), (query_width, query_width + HEAD_SIZE), (query_width + HEAD_SIZE, joined_width))
    up_wide = jnp.stack(
        [jnp.pad(up[:, :, a:b], ((0, 0), (0, 0), (a, joined_width - b))) for a, b in edges]
    )
    w_joined = (
        jnp.transpose(w_qkv, (1, 2, 0)).astype(F32) + dot("jrkc,jrd->kcd", up_wide, qkv_down)
    ).astype(BF16).reshape(groups * joined_width, model_width)
    down_flat = o_down.reshape(rank, -1)
    w_branch = (w_out.astype(F32) + dot("rc,rd->cd", down_flat, o_up)).astype(BF16)
    down_all = lax.all_gather(down_flat, "tensor")
    all_branch = gather_weight(w_branch)
    all_joined = gather_weight(w_joined)

    _, _, normed_one = normalize(tokens.astype(F32), gains[0])
    lowrank = dot("td,jrd->tjr", normed_one, qkv_down)
    joined = dot("cd,td->ct", w_joined, normed_one).reshape(groups, joined_width, token_rows)
    maps_t = jnp.swapaxes(feature_maps, 1, 2)
    maps = jnp.stack(
        [feature_maps[:, :, i * HEAD_SIZE:(i + 1) * HEAD_SIZE] for i in range(heads + 1)], axis=1
    )
    seg_row = segments.reshape(1, token_rows)
    seg_col = segments.reshape(token_rows, 1)
    low, attended, root = attention_forward(joined, cosines, sines, maps_t, seg_row, seg_col, heads)
    attended_flat = attended.reshape(groups * query_width, token_rows)
    att_parts = [chunk_of(attended_flat, me, share, 1)]
    for s in range(1, n):
        att_parts.append(
            lax.ppermute(chunk_of(attended_flat, (me + s) % n, share, 1), "tensor", ring(n, s))
        )
    att_share = jnp.stack(att_parts)
    down_places = jnp.stack([pick(down_all, (me + n - s) % n, 0) for s in range(n)])
    lowrank_out = dot("nct,nrc->tr", att_share, down_places)
    tokens_share = chunk_of(tokens, me, share, 0).astype(F32)
    hidden = tokens_share + dot("nct,ncd->td", att_share, all_branch)
    scaled_two, inverse_two, normed_two = normalize(hidden, gains[1])

    normed, acts, grads, cots, mixed_parts, grad_parts = [normed_two], [], [], [], [], []
    for k in range(n):
        if k < n - 1:
            normed.append(lax.ppermute(normed[k], "tensor", ring(n)))
        cot = chunk_of(cotangent, (me + n - k) % n, share, 0)
        gate_up = dot("td,dsf->tsf", normed[k], w_gate_up)
        gate, upper = gate_up[:, 0], gate_up[:, 1]
        sigma = jax.nn.sigmoid(gate)
        silu = gate * sigma
        act = (silu * upper).astype(BF16)
        grad_act = dot("td,fd->tf", cot, w_down)
        grad_gate = grad_act * upper * sigma * (1.0 + gate * (1.0 - sigma))
        grad_gate_up = jnp.stack([grad_gate, grad_act * silu], axis=1).astype(BF16)
        grad_parts.append(dot("tsf,dsf->td", grad_gate_up, w_gate_up).astype(BF16))
        mixed_parts.append(dot("tf,fd->td", act, w_down).astype(BF16))
        acts.append(act)
        grads.append(grad_gate_up)
        cots.append(cot)
    grad_normed_two = ring_sum(grad_parts)
    weighted = grad_normed_two * gains[1]
    grad_hidden = chunk_of(cotangent, me, share, 0).astype(F32) + inverse_two * (
        weighted - scaled_two * jnp.mean(weighted * scaled_two, axis=-1, keepdims=True)
    )
    gain_two = jnp.sum(grad_normed_two * scaled_two, axis=0)
    grad_branch = grad_hidden.astype(BF16)

    grad_att_share = dot("ncd,td->nct", all_branch, grad_branch).astype(BF16)
    back = [grad_att_share[0]]
    for s in range(1, n):
        back.append(lax.ppermute(grad_att_share[s], "tensor", ring(n, -s)))
    order = [pick(jnp.stack(back), (j + n - me) % n, 0) for j in range(n)]
    grad_attended = jnp.concatenate(order, axis=1).reshape(groups, query_width, token_rows)
    mixed = ring_sum(mixed_parts)
    output = (hidden + mixed).astype(BF16)

    grad_joined, grad_maps = attention_backward(
        low, cosines, sines, maps_t, maps, seg_row, seg_col, attended, root, grad_attended, heads
    )
    flat_joined = grad_joined.reshape(groups * joined_width, token_rows)
    parts = [chunk_of(flat_joined, me, share, 1)]
    for s in range(1, n):
        parts.append(
            lax.ppermute(chunk_of(flat_joined, (me + s) % n, share, 1), "tensor", ring(n, s))
        )
    grad_normed_one = dot("nct,ncd->td", jnp.stack(parts), all_joined)
    scaled_one, inverse_one, _ = normalize(tokens_share, gains[0])
    weighted = grad_normed_one * gains[0]
    grad_input = (
        grad_hidden
        + inverse_one
        * (weighted - scaled_one * jnp.mean(weighted * scaled_one, axis=-1, keepdims=True))
    ).astype(BF16)
    gain_one = jnp.sum(grad_normed_one * scaled_one, axis=0)

    all_normed = jnp.concatenate(normed, axis=0)
    all_acts = jnp.concatenate(acts, axis=0)
    all_grads = jnp.concatenate(grads, axis=0)
    all_cots = jnp.concatenate(cots, axis=0)
    width = model_width // dp

    def of_core(array, core):
        return pick(array.reshape(array.shape[0], dp // 2, 2, width), core, 2)

    out_gate_up = scatter_dp(
        lambda core: dot("tbe,tsf->besf", of_core(all_normed, core), all_grads), 0, 2
    )
    out_down = scatter_dp(lambda core: dot("tf,tbe->fbe", all_acts, of_core(all_cots, core)), 1, 0)
    flat_att = att_share.reshape(-1, share)
    out_branch = scatter_dp(
        lambda core: dot("ct,tbe->cbe", flat_att, of_core(grad_branch, core)), 1, 0
    )
    branch_rows = out_branch.shape[0] // n
    out_branch = ring_sum([out_branch[s * branch_rows:(s + 1) * branch_rows] for s in range(n)])
    out_qkv = scatter_dp(
        lambda core: dot("tbe,kct->bekc", of_core(normed_one, core), grad_joined), 0, 1
    )

    lowrank_low = lowrank.astype(BF16)
    grad_up = jnp.concatenate(
        [dot("tr,kct->rkc", lowrank_low[:, j], grad_joined[:, a:b]) for j, (a, b) in enumerate(edges)],
        axis=2,
    )
    grad_maps = jnp.transpose(grad_maps, (0, 2, 1, 3)).reshape(groups, HEAD_SIZE, -1)
    small = jnp.concatenate(
        [
            jnp.moveaxis(grad_up.reshape(rank, groups, dp, -1), 2, 0).reshape(dp, -1),
            jnp.moveaxis(grad_maps.reshape(groups, HEAD_SIZE, dp, -1), 2, 0).reshape(dp, -1),
        ],
        axis=1,
    )
    small = scatter_small(small, False)
    cut = rank * groups * (joined_width // dp)
    out_up = small[:cut].reshape(rank, groups, -1)
    out_maps = small[cut:].reshape(groups, HEAD_SIZE, -1)

    grad_lowrank = dot("kct,jrkc->jrt", grad_joined, up_wide).astype(BF16)
    grad_qkv_down = dot("jrt,td->jrd", grad_lowrank, normed_one)
    grad_lowrank_out = dot("td,rd->tr", grad_branch, o_up).astype(BF16)
    grad_o_up = dot("tr,td->rd", lowrank_out.astype(BF16), grad_branch)
    grad_o_down = dot("tr,nct->nrc", grad_lowrank_out, att_share)
    grad_o_down = jnp.stack([pick(grad_o_down, (me + n - j) % n, 0) for j in range(n)])
    shared = jnp.concatenate(
        [gain_one[None], gain_two[None], grad_qkv_down.reshape(-1, model_width), grad_o_up], axis=0
    )
    lines = shared.shape[0]
    shared = jnp.transpose(shared.reshape(lines, dp, n, -1), (1, 2, 0, 3)).reshape(dp, n, -1)
    downs = grad_o_down.reshape(n, rank, groups, dp, -1)
    downs = jnp.transpose(downs, (3, 0, 1, 2, 4)).reshape(dp, n, -1)
    cut = shared.shape[2]
    packed = scatter_small(jnp.concatenate([shared, downs], axis=2), True)
    shared = packed[:cut].reshape(lines, -1)
    out_o_down = packed[cut:].reshape(rank, groups, -1)
    return (
        output,
        grad_input,
        shared[:2],
        out_qkv,
        shared[2:lines - rank].reshape(3, rank, -1),
        out_up,
        out_maps,
        out_branch,
        out_o_down,
        shared[lines - rank:],
        out_gate_up,
        out_down,
    )


def solution(mesh):
    in_specs = (
        P("dp", None),
        P("dp", None),
        P("dp", None),
        P(),
        P(None, "tensor", None),
        P(),
        P(None, "tensor", None),
        P("tensor", None, None),
        P("tensor", None),
        P(None, "tensor", None),
        P(),
        P(None, None, "tensor"),
        P("tensor", None),
    )
    out_specs = (
        P(("dp", "tensor"), None),
        P(("dp", "tensor"), None),
        P(None, ("dp", "tensor")),
        P("dp", "tensor", None),
        P(None, None, ("dp", "tensor")),
        P(None, "tensor", "dp"),
        P("tensor", None, "dp"),
        P("tensor", "dp"),
        P(None, "tensor", "dp"),
        P(None, ("dp", "tensor")),
        P("dp", None, "tensor"),
        P("tensor", "dp"),
    )
    return jax.shard_map(
        local, mesh=mesh, in_specs=in_specs, out_specs=out_specs, check_vma=False
    )
```

time: 2040 us -> 1020 us (0.50)
  waiting for transfers between devices: 1280 us -> 292 us
  matrix products: 427 us -> 298 us
  starting transfers between devices: 1.18 us -> 78.7 us
  Pallas kernels: 0 us -> 67.3 us
  local copies, waits for them, and re-layouts: 200 us -> 179 us
    psum x3 -> x0, waiting for transfers between devices: 513 us -> none  [the longest x1 219 us: local(): lax.psum(partial_mlp.astype(jnp.bfloat16), 'tensor').astype(jnp.float32)]
    unnamed x19 -> x0, waiting for transfers between devices: 485 us -> none
    ppermute x0 -> x67, waiting for transfers between devices: none -> 292 us  [the longest x16 97.9 us: halve(): arrived = lax.ppermute(pick(current, 1 - own, where), 'dp', flip(size, bit))]
    reduce_scatter x4 -> x0, waiting for transfers between devices: 284 us -> none  [the longest x1 119 us: local(): lax.psum_scatter(grad_w_gate_up.astype(jnp.bfloat16), 'dp', scatter_dimen...]
    dynamic_update_slice x10 -> x0, local copies, waits for them, and re-layouts: 132 us -> none  [the longest x8 132 us: attend_back(): running, stacked = lax.scan(one_block, initial, (starts, totals))]
    ppermute x0 -> x67, starting transfers between devices: none -> 78.7 us  [the longest x16 21.4 us: halve(): arrived = lax.ppermute(pick(current, 1 - own, where), 'dp', flip(size, bit))]
    pallas_call x0 -> x2, Pallas kernels: none -> 67.3 us  [the longest x1 41.3 us: attention_backward(): pl.pallas_call(partial(backward_kernel, heads, block), grid=(groups,), ou...]
    dot_general x53 -> x37, matrix products: 363 us -> 298 us  [the longest x4 80.8 us: local(): grad_parts.append(dot('tsf,dsf->td', grad_gate_up, w_gate_up).astype(BF16))]
  transfers between devices with their start and end apart: 13 -> 67, of which waited for: 13 -> 32; matrix products, arithmetic and copies ran while one was open for 7% -> 53% of each run, Pallas kernels for 0% -> 7%
where the time goes in v1:
time: 1020 us; the launch traced here: 1010 us
  matrix products  298 us (29%)
  waiting for transfers between devices  292 us (29%)
  local copies, waits for them, and re-layouts  179 us (18%)
  starting transfers between devices  78.7 us (8%)
  other arithmetic  75.3 us (7%)
  Pallas kernels  67.3 us (7%)
  blocking collectives  13.1 us (1%)
    ppermute x16, waiting for transfers between devices, halve(): arrived = lax.ppermute(pick(current, 1 - own, where), 'dp', flip(size, bit))  97.9 us
    dot_general x4, matrix products, local(): grad_parts.append(dot('tsf,dsf->td', grad_gate_up, w_gate_up).astype(BF16))  80.8 us
    dot_general x4, matrix products, local(): gate_up = dot('td,dsf->tsf', normed[k], w_gate_up)  71.6 us
    ppermute x3, waiting for transfers between devices, local(): normed.append(lax.ppermute(normed[k], 'tensor', ring(n)))  59.5 us
    dynamic_slice x13, local copies, waits for them, and re-layouts, pick(): return lax.dynamic_index_in_dim(array, index, axis, keepdims=False)  57.5 us
    unnamed x249, local copies, waits for them, and re-layouts  55.9 us
    pallas_call x1, Pallas kernels, attention_backward(): pl.pallas_call(partial(backward_kernel, heads, block), grid=(groups,), ou...  41.3 us
    ppermute x12, waiting for transfers between devices, double(): arrived = lax.ppermute(current, 'dp', flip(size, bit))  39.4 us
  transfers between devices with their start and end apart: 67, of which 32 were waited for; matrix products, arithmetic and copies ran while one was open for 53% of the time, Pallas kernels for 7%

profile of v1, /device:TPU:12, one launch (start us, length us, event | category | flops | bytes accessed | tf_op | source)
XLA Modules:
  0.0 1006.6 jit_solution(14407536276143406896)
XLA Ops:
  6.6 6.7 copy.125
  28.1 26.0 %attention_forward.1 = (bf16[2,384,1024]{2,1,0:T(8,128)(2,1)S(1)}, bf16[2,256,1024]{2,1,0:T(8,128)(2,1)S(1)}, f32[2,4,1,1024]{3,2,1,0:T(1,128)S(1)}) custom-call(f32[2,384,1024]{2,1,0:T(8,128)} %fusion.16.joined_ref, f32[32,1024]{1,0:T(8,128)S(1)} %get-tuple-element.152.cos_ref, f32[32,1024]{1,0:T(8,128)S(1)} %get-tuple-element.151.sin_ref, ...), custom_call_target="tpu_custom_call" | custom-call | tf_op jit(solution)/shard_map/attention_forward/pallas_call | solution.py:121
  60.5 7.8 reshape.311
  75.4 7.8 reshape.327
  83.2 11.4 %constant_dynamic-slice_fusion.1 = (bf16[1024,4,1,256]{3,2,1,0:T(2,128)(2,1)}, bf16[1024,4,1,256]{3,2,1,0:T(2,128)(2,1)}) fusion(bf16[1024,4,2,256]{3,2,1,0:T(2,128)(2,1)} %reshape.327, s32[]{:T(128)S(6)} %select_n.418, s32[]{:T(128)S(6)} %select_n.419), kind=kLoop, calls=%fused_computation.317 | loop fusion | bytes 8388616 | tf_op jit(solution)/shard_map/jit(dynamic_index_in_dim)/dynamic_slice | solution.py:256
  94.6 9.9 constant_dynamic-slice_fusion.12
  109.6 6.2 collective-permute-done.4
  138.7 6.1 collective-permute-done.6
  150.2 11.4 %collective-permute-done.30 = bf16[4,96,1024]{2,1,0:T(8,128)(2,1)S(1)} collective-permute-done((bf16[4,96,1024]{2,1,0:T(8,128)(2,1)S(1)}, bf16[4,96,1024]{2,1,0:T(8,128)(2,1)S(1)}, u32[]{:S(2)}, u32[]{:S(2)}) %collective-permute-start.30) | collective-permute-done | bytes 786464 | tf_op jit(solution)/shard_map/ppermute | solution.py:333
  165.9 19.4 %collective-permute-done.7 = bf16[4,2,64,1024]{3,2,0,1:T(8,128)(2,1)S(1)} collective-permute-done((bf16[4,2,64,1024]{3,2,0,1:T(8,128)(2,1)S(1)}, bf16[4,2,64,1024]{3,2,0,1:T(8,128)(2,1)S(1)}, u32[]{:S(2)}, u32[]{:S(2)}) %collective-permute-start.7) | collective-permute-done | bytes 1048608 | tf_op jit(solution)/shard_map/ppermute | solution.py:333
  191.2 13.1 %all_gather.3 = bf16[4,8,512]{2,1,0:T(8,128)(2,1)S(1)} all-gather(bf16[1,8,512]{2,1,0:T(8,128)(2,1)S(1)} %all_gather_reshape.3), channel_id=1, replica_groups=mesh['dp'=8,'tensor'=4] {'tensor'}, dimensions={0}, use_global_device_ids=true | all-gather | bytes 40960 | tf_op jit(solution)/shard_map/all_gather | solution.py:397
  212.2 9.4 collective-permute-done.1
  222.6 10.6 %copy.202 = bf16[1024,4,1,256]{0,3,1,2:T(8,128)(2,1)} copy(bf16[1024,4,1,256]{3,2,1,0:T(2,128)(2,1)} %get-tuple-element.77) | data formatting | bytes 4194304
  233.2 10.6 %copy.201 = bf16[1024,4,1,256]{0,3,1,2:T(8,128)(2,1)} copy(bf16[1024,4,1,256]{3,2,1,0:T(2,128)(2,1)} %get-tuple-element.76) | data formatting | bytes 4194304
  271.1 19.5 %fusion.29 = f32[256,2,2048]{2,0,1:T(8,128)} fusion(bf16[2048,2,2048]{2,1,0:T(2,128)(2,1)} %param.24, bf16[256,2048]{1,0:T(8,128)(2,1)S(1)} %multiply_convert_fusion.12), kind=kOutput, calls=%fused_computation.60 | convolution fusion | flops 4294967296 | bytes 22020096 | tf_op jit(solution)/shard_map/td,dsf->tsf/dot_general | solution.py:429
  290.6 7.1 fusion.159
  301.6 19.3 %fusion.35 = f32[256,2,2048]{2,0,1:T(8,128)} fusion(bf16[2048,2,2048]{2,1,0:T(2,128)(2,1)} %param.24, bf16[256,2048]{1,0:T(8,128)(2,1)} %collective-permute-done.12), kind=kOutput, calls=%fused_computation.66 | convolution fusion | flops 4294967296 | bytes 22020096 | tf_op jit(solution)/shard_map/td,dsf->tsf/dot_general | solution.py:429
  320.9 6.8 fusion.156
  334.9 18.3 %fusion.71 = bf16[256,2048]{1,0:T(8,128)(2,1)} fusion(bf16[2048,2,2048]{2,1,0:T(2,128)(2,1)} %param.24, bf16[256,1,2048]{2,0,1:T(8,128)(2,1)} %get-tuple-element.63, bf16[256,1,2048]{2,0,1:T(8,128)(2,1)} %get-tuple-element.62), kind=kOutput, calls=%fused_computation.80 | convolution fusion | flops 4296540160 | bytes 19922944 | tf_op jit(solution)/shard_map/tsf,dsf->td/dot_general | solution.py:437
  354.0 26.6 %collective-permute-done.14 = bf16[256,2048]{1,0:T(8,128)(2,1)} collective-permute-done((bf16[256,2048]{1,0:T(8,128)(2,1)}, bf16[256,2048]{1,0:T(8,128)(2,1)}, u32[]{:S(2)}, u32[]{:S(2)}) %collective-permute-start.14) | collective-permute-done | bytes 1048608 | tf_op jit(solution)/shard_map/ppermute | solution.py:427
  380.5 16.2 %fusion.33 = f32[256,2,2048]{2,0,1:T(8,128)S(1)} fusion(bf16[2048,2,2048]{2,1,0:T(2,128)(2,1)} %param.24, bf16[256,2048]{1,0:T(8,128)(2,1)} %collective-permute-done.14), kind=kOutput, calls=%fused_computation.64 | convolution fusion | flops 4294967296 | bytes 22020096 | tf_op jit(solution)/shard_map/td,dsf->tsf/dot_general | solution.py:429
  396.7 8.0 fusion.157
  404.7 7.3 add_convert_fusion.8
  414.7 18.5 %add_convert_fusion.5 = bf16[256,2048]{1,0:T(8,128)(2,1)} fusion(bf16[256,2048]{1,0:T(8,128)(2,1)} %collective-permute-done.18, bf16[2048,2,2048]{2,1,0:T(2,128)(2,1)} %param.24, bf16[256,1,2048]{2,0,1:T(8,128)(2,1)} %get-tuple-element.61, bf16[256,1,2048]{2,0,1:T(8,128)(2,1)} %get-tuple-element.60), kind=kOutput, calls=%fused_computation.149 | convolution fusion | flops 4298637312 | bytes 20971520 | tf_op jit(solution)/shard_map/tsf,dsf->td/dot_general | solution.py:437
  448.6 33.0 %collective-permute-done.16 = bf16[256,2048]{1,0:T(8,128)(2,1)} collective-permute-done((bf16[256,2048]{1,0:T(8,128)(2,1)}, bf16[256,2048]{1,0:T(8,128)(2,1)}, u32[]{:S(2)}, u32[]{:S(2)}) %collective-permute-start.16) | collective-permute-done | bytes 1048608 | tf_op jit(solution)/shard_map/ppermute | solution.py:427
  481.6 16.6 %fusion.31 = f32[256,2,2048]{2,0,1:T(8,128)S(1)} fusion(bf16[2048,2,2048]{2,1,0:T(2,128)(2,1)} %param.24, bf16[256,2048]{1,0:T(8,128)(2,1)} %collective-permute-done.16), kind=kOutput, calls=%fused_computation.62 | convolution fusion | flops 4294967296 | bytes 22020096 | tf_op jit(solution)/shard_map/td,dsf->tsf/dot_general | solution.py:429
  502.8 8.6 convolution_convert_fusion.2
  515.0 7.8 reshape.324
  522.8 11.4 %constant_dynamic-slice_fusion.3 = (bf16[1024,4,1,256]{3,2,1,0:T(2,128)(2,1)}, bf16[1024,4,1,256]{3,2,1,0:T(2,128)(2,1)}) fusion(bf16[1024,4,2,256]{3,2,1,0:T(2,128)(2,1)} %reshape.324, s32[]{:T(128)S(6)} %select_n.418, s32[]{:T(128)S(6)} %select_n.419), kind=kLoop, calls=%fused_computation.319 | loop fusion | bytes 8388616 | tf_op jit(solution)/shard_map/jit(dynamic_index_in_dim)/dynamic_slice | solution.py:256
  534.2 9.0 copy.173
  543.2 13.4 %convolution_convert_fusion = bf16[4,256,2,2048]{3,1,2,0:T(8,128)(2,1)} fusion(bf16[1024,4,1,256]{0,3,1,2:T(8,128)(2,1)S(1)} %copy.173, bf16[256,1,2048]{2,0,1:T(8,128)(2,1)} %get-tuple-element.65, bf16[256,1,2048]{2,0,1:T(8,128)(2,1)} %get-tuple-element.64, bf16[256,1,2048]{2,0,1:T(8,128)(2,1)} %get-tuple-element.61, ...), kind=kOutput, calls=%fused_computation.20 | convolution fusion | flops 8661237760 | bytes 18874368 | tf_op jit(solution)/shard_map/tbe,tsf->besf/dot_general | solution.py:488
  557.1 10.6 %copy.172 = bf16[1024,4,1,256]{0,3,1,2:T(8,128)(2,1)} copy(bf16[1024,4,1,256]{3,2,1,0:T(2,128)(2,1)} %get-tuple-element.72) | data formatting | bytes 4194304 | tf_op jit(solution)/shard_map/jit(dynamic_index_in_dim)/dynamic_slice | solution.py:256
  567.7 21.6 %fusion.62 = f32[256,2048]{1,0:T(8,128)S(1)} fusion(bf16[2048,2,2048]{2,1,0:T(2,128)(2,1)} %param.24, bf16[256,1,2048]{2,0,1:T(8,128)(2,1)} %get-tuple-element.65, bf16[256,1,2048]{2,0,1:T(8,128)(2,1)} %get-tuple-element.64), kind=kOutput, calls=%fused_computation.77 | convolution fusion | flops 4297064448 | bytes 20971520 | tf_op jit(solution)/shard_map/tsf,dsf->td/dot_general | solution.py:437
  601.2 17.2 %collective-permute-done.20 = bf16[256,2048]{1,0:T(8,128)(2,1)S(1)} collective-permute-done((bf16[256,2048]{1,0:T(8,128)(2,1)S(1)}, bf16[256,2048]{1,0:T(8,128)(2,1)S(1)}, u32[]{:S(2)}, u32[]{:S(2)}) %collective-permute-start.20) | collective-permute-done | bytes 1048608 | tf_op jit(solution)/shard_map/ppermute | solution.py:267
  618.4 22.4 %multiply_reduce_fusion = (f32[2048]{0:T(1024)}, f32[256]{0:T(256)S(1)}, f32[256,2048]{1,0:T(8,128)S(1)}) fusion(f32[256,2048]{1,0:T(8,128)S(1)} %copy-done.34, f32[256]{0:T(256)S(1)} %copy-done.96, bf16[256,2048]{1,0:T(8,128)(2,1)S(1)} %collective-permute-done.20, f32[2048]{0:T(1024)S(1)} %bitcast.611, bf16[2048,2,2048]{2,1,0:T(2,128)(2,1)} %param.24, ...), kind=kOutput, calls=%fused_computation.140 | convolution fusion | flops 4301256704 | bytes 24135680 | tf_op jit(solution)/shard_map/tsf,dsf->td/dot_general | solution.py:437
  673.1 6.2 collective-permute-done.21
  685.0 41.3 %attention_backward.1 = (bf16[2,384,1024]{2,1,0:T(8,128)(2,1)S(1)}, f32[2,5,64,64]{3,2,1,0:T(8,128)S(1)}) custom-call(bf16[2,384,1024]{2,1,0:T(8,128)(2,1)} %copy-done.6, f32[32,1024]{1,0:T(8,128)S(1)} %copy-done.12, f32[32,1024]{1,0:T(8,128)S(1)} %copy-done.10, bf16[2,320,64]{2,1,0:T(8,128)(2,1)S(1)} %bitcast.551, bf16[2,5,64,64]{3,2,1,0:T(8,128)(2,1)S(1)} %copy-done.14, ...), custom_call_target="tpu_custom_call" | custom-call | tf_op jit(solution)/shard_map/attention_backward/pallas_call | solution.py:213
  755.2 18.4 %collective-permute-done.24 = bf16[768,256]{0,1:T(8,128)(2,1)} collective-permute-done((bf16[768,256]{0,1:T(8,128)(2,1)}, bf16[768,256]{0,1:T(8,128)(2,1)}, u32[]{:S(2)}, u32[]{:S(2)}) %collective-permute-start.24) | collective-permute-done | bytes 393248 | tf_op jit(solution)/shard_map/ppermute | solution.py:466
  773.6 6.9 collective-permute-done.25
  781.0 10.1 %fusion.82 = (f32[2048]{0:T(1024)S(1)}, f32[256]{0:T(256)S(1)}, f32[256,2048]{1,0:T(8,128)}) fusion(f32[256]{0:T(256)S(1)} %copy-done.100, bf16[1024,2048]{1,0:T(8,128)(2,1)} %param.13, s32[]{:T(128)S(6)} %select_n.351, f32[2048]{0:T(1024)S(1)} %bitcast.608, bf16[4,768,1024]{2,1,0:T(8,128)(2,1)} %bitcast.569, bf16[4,768,1024]{2,1,0:T(8,128)(2,1)} %bitcast.568, ...), kind=kOutput, calls=%fused_computation.93 | convolution fusion | flops 3252418304 | bytes 17319940 | tf_op jit(solution)/shard_map/nct,ncd->td/dot_general | solution.py:468
  842.1 7.4 add_convert_fusion.1
  857.4 18.6 %collective-permute-done.63 = bf16[1024,2,256]{2,0,1:T(8,128)(2,1)S(1)} collective-permute-done((bf16[1024,2,256]{2,0,1:T(8,128)(2,1)S(1)}, bf16[1024,2,256]{2,0,1:T(8,128)(2,1)S(1)}, u32[]{:S(2)}, u32[]{:S(2)}) %collective-permute-start.63) | collective-permute-done | bytes 1048608 | tf_op jit(solution)/shard_map/ppermute | solution.py:287
  882.2 9.2 collective-permute-done.64
  892.5 6.0 collective-permute-done.50
  899.8 15.1 %add_convert_fusion = bf16[4,256,2,2048]{3,1,2,0:T(8,128)(2,1)} fusion(bf16[4,256,2,2048]{3,1,2,0:T(8,128)(2,1)} %collective-permute-done.57, bf16[1024,4,1,256]{0,3,1,2:T(8,128)(2,1)} %copy.172, bf16[256,1,2048]{2,0,1:T(8,128)(2,1)} %get-tuple-element.65, bf16[256,1,2048]{2,0,1:T(8,128)(2,1)} %get-tuple-element.64, ...), kind=kOutput, calls=%fused_computation | convolution fusion | flops 8669626368 | bytes 27262976 | tf_op jit(solution)/shard_map/tbe,tsf->besf/dot_general | solution.py:488
  925.7 9.9 collective-permute-done.51
  938.4 33.1 %collective-permute-done.54 = bf16[1024,256]{1,0:T(8,128)(2,1)S(1)} collective-permute-done((bf16[1024,256]{1,0:T(8,128)(2,1)S(1)}, bf16[1024,256]{1,0:T(8,128)(2,1)S(1)}, u32[]{:S(2)}, u32[]{:S(2)}) %collective-permute-start.54) | collective-permute-done | bytes 524320 | tf_op jit(solution)/shard_map/ppermute | solution.py:287
  987.5 10.3 %collective-permute-done.59 = bf16[256,1,2048]{2,0,1:T(8,128)(2,1)S(1)} collective-permute-done((bf16[256,1,2048]{2,0,1:T(8,128)(2,1)S(1)}, bf16[256,1,2048]{2,0,1:T(8,128)(2,1)S(1)}, u32[]{:S(2)}, u32[]{:S(2)}) %collective-permute-start.59) | collective-permute-done | bytes 1048608 | tf_op jit(solution)/shard_map/ppermute | solution.py:287
  (552 shorter events, 335.6 us)
Async XLA Ops:
  4.9 101.4 %collective-permute-start.3 = (bf16[64,2048]{1,0:T(8,128)(2,1)}, bf16[64,2048]{1,0:T(8,128)(2,1)}, u32[]{:S(2)}, u32[]{:S(2)}) collective-permute-start(bf16[64,2048]{1,0:T(8,128)(2,1)} %fusion.167), channel_id=1, source_target_pairs={{0,1},{1,2},{2,3},{3,0},{4,5},{5,6},{6,7},{7,4},{8,9},{9,10},{10,1... | collective-permute-start | bytes 786440 | tf_op jit(solution)/shard_map/ppermute | solution.py:349
  57.2 153.4 %collective-permute-start = (bf16[512,256]{0,1:T(8,128)(2,1)}, bf16[512,256]{0,1:T(8,128)(2,1)}, u32[]{:S(2)}, u32[]{:S(2)}) collective-permute-start(bf16[512,256]{0,1:T(8,128)(2,1)} %copy.195), channel_id=1, source_target_pairs={{0,1},{1,2},{2,3},{3,0},{4,5},{5,6},{6,7},{7,4},{8,9},{9,10},{10,1... | collective-permute-start | bytes 786440 | tf_op jit(solution)/shard_map/ppermute | solution.py:415
  59.8 48.2 %collective-permute-start.27 = (bf16[96,2048]{1,0:T(8,128)(2,1)S(1)}, bf16[96,2048]{1,0:T(8,128)(2,1)S(1)}, u32[]{:S(2)}, u32[]{:S(2)}) collective-permute-start(bf16[96,2048]{1,0:T(8,128)(2,1)S(1)} %constant_dynamic-slice_fusion.26), channel_id=1, source_target_pairs={{0,1},{1,2},{2,3},{3,0},{4,5},{5,6},{6,7},{7,4},{8,9},{9,10},{10,1... | collective-permute-start | bytes 1179656 | tf_op jit(solution)/shard_map/ppermute | solution.py:349
  108.0 16.2 %collective-permute-start.28 = (bf16[96,2048]{1,0:T(8,128)(2,1)S(1)}, bf16[96,2048]{1,0:T(8,128)(2,1)S(1)}, u32[]{:S(2)}, u32[]{:S(2)}) collective-permute-start(bf16[96,2048]{1,0:T(8,128)(2,1)S(1)} %collective-permute-done.27), channel_id=1, source_target_pairs={{0,1},{1,2},{2,3},{3,0},{4,5},{5,6},{6,7},{7,4},{8,9},{9,10},{10,1... | collective-permute-start | bytes 1179656 | tf_op jit(solution)/shard_map/ppermute | solution.py:349
  136.6 25.0 %collective-permute-start.30 = (bf16[4,96,1024]{2,1,0:T(8,128)(2,1)S(1)}, bf16[4,96,1024]{2,1,0:T(8,128)(2,1)S(1)}, u32[]{:S(2)}, u32[]{:S(2)}) collective-permute-start(bf16[4,96,1024]{2,1,0:T(8,128)(2,1)S(1)} %get-tuple-element.111), channel_id=1, source_target_pairs={{0,8},{4,12},{8,0},{12,4},{16,24},{20,28},{24,16},{28,20},{1,9},{5... | collective-permute-start | bytes 2359304 | tf_op jit(solution)/shard_map/ppermute | solution.py:333
  138.2 24.7 %collective-permute-start.33 = (bf16[4,96,1024]{2,1,0:T(8,128)(2,1)S(1)}, bf16[4,96,1024]{2,1,0:T(8,128)(2,1)S(1)}, u32[]{:S(2)}, u32[]{:S(2)}) collective-permute-start(bf16[4,96,1024]{2,1,0:T(8,128)(2,1)S(1)} %get-tuple-element.112), channel_id=1, source_target_pairs={{0,16},{4,20},{8,24},{12,28},{16,0},{20,4},{24,8},{28,12},{1,17},{... | collective-permute-start | bytes 2359304 | tf_op jit(solution)/shard_map/ppermute | solution.py:333
  146.3 39.1 %collective-permute-start.7 = (bf16[4,2,64,1024]{3,2,0,1:T(8,128)(2,1)S(1)}, bf16[4,2,64,1024]{3,2,0,1:T(8,128)(2,1)S(1)}, u32[]{:S(2)}, u32[]{:S(2)}) collective-permute-start(bf16[4,2,64,1024]{3,2,0,1:T(8,128)(2,1)S(1)} %pad_maximum_fusion.26), channel_id=1, source_target_pairs={{0,16},{4,20},{8,24},{12,28},{16,0},{20,4},{24,8},{28,12},{1,17},{... | collective-permute-start | bytes 3145736 | tf_op jit(solution)/shard_map/ppermute | solution.py:333
  149.5 54.9 %collective-permute-start.10 = (bf16[4,2,64,1024]{3,2,0,1:T(8,128)(2,1)}, bf16[4,2,64,1024]{3,2,0,1:T(8,128)(2,1)}, u32[]{:S(2)}, u32[]{:S(2)}) collective-permute-start(bf16[4,2,64,1024]{3,2,0,1:T(8,128)(2,1)} %pad_maximum_fusion.27), channel_id=1, source_target_pairs={{0,8},{4,12},{8,0},{12,4},{16,24},{20,28},{24,16},{28,20},{1,9},{5... | collective-permute-start | bytes 3145736 | tf_op jit(solution)/shard_map/ppermute | solution.py:333
  163.3 83.8 %collective-permute-start.31 = (bf16[4,2,96,1024]{3,2,0,1:T(8,128)(2,1)S(1)}, bf16[4,2,96,1024]{3,2,0,1:T(8,128)(2,1)}, u32[]{:S(2)}, u32[]{:S(2)}) collective-permute-start(bf16[4,2,96,1024]{3,2,0,1:T(8,128)(2,1)S(1)} %pad_maximum_fusion.20), channel_id=1, source_target_pairs={{0,16},{4,20},{8,24},{12,28},{16,0},{20,4},{24,8},{28,12},{1,17},{... | collective-permute-start | bytes 4718600 | tf_op jit(solution)/shard_map/ppermute | solution.py:333
  165.2 86.3 %collective-permute-start.34 = (bf16[4,2,96,1024]{3,2,0,1:T(8,128)(2,1)}, bf16[4,2,96,1024]{3,2,0,1:T(8,128)(2,1)}, u32[]{:S(2)}, u32[]{:S(2)}) collective-permute-start(bf16[4,2,96,1024]{3,2,0,1:T(8,128)(2,1)} %pad_maximum_fusion.21), channel_id=1, source_target_pairs={{0,8},{4,12},{8,0},{12,4},{16,24},{20,28},{24,16},{28,20},{1,9},{5... | collective-permute-start | bytes 4718600 | tf_op jit(solution)/shard_map/ppermute | solution.py:333
  188.0 68.2 %collective-permute-start.8 = (bf16[4,2,2,64,1024]{4,3,0,1,2:T(8,128)(2,1)}, bf16[4,2,2,64,1024]{4,3,0,1,2:T(8,128)(2,1)}, u32[]{:S(2)}, u32[]{:S(2)}) collective-permute-start(bf16[4,2,2,64,1024]{4,3,0,1,2:T(8,128)(2,1)} %pad_maximum_fusion.16), channel_id=1, source_target_pairs={{0,4},{4,0},{8,12},{12,8},{16,20},{20,16},{24,28},{28,24},{1,5},{5... | collective-permute-start | bytes 6291464 | tf_op jit(solution)/shard_map/ppermute | solution.py:333
  204.4 17.3 %collective-permute-start.1 = (bf16[512,256]{0,1:T(8,128)(2,1)}, bf16[512,256]{0,1:T(8,128)(2,1)S(1)}, u32[]{:S(2)}, u32[]{:S(2)}) collective-permute-start(bf16[512,256]{0,1:T(8,128)(2,1)} %copy.196), channel_id=1, source_target_pairs={{0,2},{1,3},{2,0},{3,1},{4,6},{5,7},{6,4},{7,5},{8,10},{9,11},{10,... | collective-permute-start | bytes 786440 | tf_op jit(solution)/shard_map/ppermute | solution.py:415
  210.6 33.2 %collective-permute-start.2 = (bf16[512,256]{0,1:T(8,128)(2,1)S(1)}, bf16[512,256]{0,1:T(8,128)(2,1)S(1)}, u32[]{:S(2)}, u32[]{:S(2)}) collective-permute-start(bf16[512,256]{0,1:T(8,128)(2,1)S(1)} %copy-done.71), channel_id=1, source_target_pairs={{0,3},{1,0},{2,1},{3,2},{4,7},{5,4},{6,5},{7,6},{8,11},{9,8},{10,9... | collective-permute-start | bytes 786440 | tf_op jit(solution)/shard_map/ppermute | solution.py:415
  221.6 37.9 %collective-permute-start.11 = (bf16[4,2,2,64,1024]{4,3,0,1,2:T(8,128)(2,1)}, bf16[4,2,2,64,1024]{4,3,0,1,2:T(8,128)(2,1)}, u32[]{:S(2)}, u32[]{:S(2)}) collective-permute-start(bf16[4,2,2,64,1024]{4,3,0,1,2:T(8,128)(2,1)} %pad_maximum_fusion.17), channel_id=1, source_target_pairs={{0,4},{4,0},{8,12},{12,8},{16,20},{20,16},{24,28},{28,24},{1,5},{5... | collective-permute-start | bytes 6291464 | tf_op jit(solution)/shard_map/ppermute | solution.py:333
  251.2 185.1 %collective-permute-start.32 = (bf16[4,2,2,96,1024]{4,3,0,1,2:T(8,128)(2,1)}, bf16[4,2,2,96,1024]{4,3,0,1,2:T(8,128)(2,1)}, u32[]{:S(2)}, u32[]{:S(2)}) collective-permute-start(bf16[4,2,2,96,1024]{4,3,0,1,2:T(8,128)(2,1)} %pad_maximum_fusion.10), channel_id=1, source_target_pairs={{0,4},{4,0},{8,12},{12,8},{16,20},{20,16},{24,28},{28,24},{1,5},{5... | collective-permute-start | bytes 9437192 | tf_op jit(solution)/shard_map/ppermute | solution.py:333
  256.0 186.4 %collective-permute-start.35 = (bf16[4,2,2,96,1024]{4,3,0,1,2:T(8,128)(2,1)}, bf16[4,2,2,96,1024]{4,3,0,1,2:T(8,128)(2,1)}, u32[]{:S(2)}, u32[]{:S(2)}) collective-permute-start(bf16[4,2,2,96,1024]{4,3,0,1,2:T(8,128)(2,1)} %pad_maximum_fusion.11), channel_id=1, source_target_pairs={{0,4},{4,0},{8,12},{12,8},{16,20},{20,16},{24,28},{28,24},{1,5},{5... | collective-permute-start | bytes 9437192 | tf_op jit(solution)/shard_map/ppermute | solution.py:333
  270.9 30.7 %collective-permute-start.12 = (bf16[256,2048]{1,0:T(8,128)(2,1)S(1)}, bf16[256,2048]{1,0:T(8,128)(2,1)}, u32[]{:S(2)}, u32[]{:S(2)}) collective-permute-start(bf16[256,2048]{1,0:T(8,128)(2,1)S(1)} %multiply_convert_fusion.12), channel_id=1, source_target_pairs={{0,1},{1,2},{2,3},{3,0},{4,5},{5,6},{6,7},{7,4},{8,9},{9,10},{10,1... | collective-permute-start | bytes 3145736 | tf_op jit(solution)/shard_map/ppermute | solution.py:427
  331.0 73.7 %collective-permute-start.13 = (bf16[256,2048]{1,0:T(8,128)(2,1)}, bf16[256,2048]{1,0:T(8,128)(2,1)}, u32[]{:S(2)}, u32[]{:S(2)}) collective-permute-start(bf16[256,2048]{1,0:T(8,128)(2,1)} %convolution_convert_fusion.6), channel_id=1, source_target_pairs={{0,1},{1,2},{2,3},{3,0},{4,5},{5,6},{6,7},{7,4},{8,9},{9,10},{10,1... | collective-permute-start | bytes 3145736 | tf_op jit(solution)/shard_map/ppermute | solution.py:267
  334.2 46.3 %collective-permute-start.14 = (bf16[256,2048]{1,0:T(8,128)(2,1)}, bf16[256,2048]{1,0:T(8,128)(2,1)}, u32[]{:S(2)}, u32[]{:S(2)}) collective-permute-start(bf16[256,2048]{1,0:T(8,128)(2,1)} %collective-permute-done.12), channel_id=1, source_target_pairs={{0,1},{1,2},{2,3},{3,0},{4,5},{5,6},{6,7},{7,4},{8,9},{9,10},{10,1... | collective-permute-start | bytes 3145736 | tf_op jit(solution)/shard_map/ppermute | solution.py:427
  353.1 61.6 %collective-permute-start.18 = (bf16[256,2048]{1,0:T(8,128)(2,1)}, bf16[256,2048]{1,0:T(8,128)(2,1)}, u32[]{:S(2)}, u32[]{:S(2)}) collective-permute-start(bf16[256,2048]{1,0:T(8,128)(2,1)} %fusion.71), channel_id=1, source_target_pairs={{0,1},{1,2},{2,3},{3,0},{4,5},{5,6},{6,7},{7,4},{8,9},{9,10},{10,1... | collective-permute-start | bytes 3145736 | tf_op jit(solution)/shard_map/ppermute | solution.py:267
  412.1 186.1 %collective-permute-start.15 = (bf16[256,2048]{1,0:T(8,128)(2,1)}, bf16[256,2048]{1,0:T(8,128)(2,1)}, u32[]{:S(2)}, u32[]{:S(2)}) collective-permute-start(bf16[256,2048]{1,0:T(8,128)(2,1)} %add_convert_fusion.8), channel_id=1, source_target_pairs={{0,1},{1,2},{2,3},{3,0},{4,5},{5,6},{6,7},{7,4},{8,9},{9,10},{10,1... | collective-permute-start | bytes 3145736 | tf_op jit(solution)/shard_map/ppermute | solution.py:267
  433.2 156.1 %collective-permute-start.19 = (bf16[256,2048]{1,0:T(8,128)(2,1)}, bf16[256,2048]{1,0:T(8,128)(2,1)}, u32[]{:S(2)}, u32[]{:S(2)}) collective-permute-start(bf16[256,2048]{1,0:T(8,128)(2,1)} %add_convert_fusion.5), channel_id=1, source_target_pairs={{0,1},{1,2},{2,3},{3,0},{4,5},{5,6},{6,7},{7,4},{8,9},{9,10},{10,1... | collective-permute-start | bytes 3145736 | tf_op jit(solution)/shard_map/ppermute | solution.py:267
  433.8 47.8 %collective-permute-start.16 = (bf16[256,2048]{1,0:T(8,128)(2,1)}, bf16[256,2048]{1,0:T(8,128)(2,1)}, u32[]{:S(2)}, u32[]{:S(2)}) collective-permute-start(bf16[256,2048]{1,0:T(8,128)(2,1)} %collective-permute-done.14), channel_id=1, source_target_pairs={{0,1},{1,2},{2,3},{3,0},{4,5},{5,6},{6,7},{7,4},{8,9},{9,10},{10,1... | collective-permute-start | bytes 3145736 | tf_op jit(solution)/shard_map/ppermute | solution.py:427
  511.4 330.6 %collective-permute-start.62 = (bf16[2048,4,256]{2,0,1:T(8,128)(2,1)}, bf16[2048,4,256]{2,0,1:T(8,128)(2,1)}, u32[]{:S(2)}, u32[]{:S(2)}) collective-permute-start(bf16[2048,4,256]{2,0,1:T(8,128)(2,1)} %convolution_convert_fusion.2), channel_id=1, source_target_pairs={{0,4},{4,0},{8,12},{12,8},{16,20},{20,16},{24,28},{28,24},{1,5},{5... | collective-permute-start | bytes 12582920 | tf_op jit(solution)/shard_map/ppermute | solution.py:298
  556.6 343.2 %collective-permute-start.57 = (bf16[4,256,2,2048]{3,1,2,0:T(8,128)(2,1)}, bf16[4,256,2,2048]{3,1,2,0:T(8,128)(2,1)}, u32[]{:S(2)}, u32[]{:S(2)}) collective-permute-start(bf16[4,256,2,2048]{3,1,2,0:T(8,128)(2,1)} %convolution_convert_fusion), channel_id=1, source_target_pairs={{0,4},{4,0},{8,12},{12,8},{16,20},{20,16},{24,28},{28,24},{1,5},{5... | collective-permute-start | bytes 25165832 | tf_op jit(solution)/shard_map/ppermute | solution.py:298
  590.8 27.6 %collective-permute-start.20 = (bf16[256,2048]{1,0:T(8,128)(2,1)S(1)}, bf16[256,2048]{1,0:T(8,128)(2,1)S(1)}, u32[]{:S(2)}, u32[]{:S(2)}) collective-permute-start(bf16[256,2048]{1,0:T(8,128)(2,1)S(1)} %add_convert_fusion.4), channel_id=1, source_target_pairs={{0,1},{1,2},{2,3},{3,0},{4,5},{5,6},{6,7},{7,4},{8,9},{9,10},{10,1... | collective-permute-start | bytes 3145736 | tf_op jit(solution)/shard_map/ppermute | solution.py:267
  599.9 41.0 %collective-permute-start.17 = (bf16[256,2048]{1,0:T(8,128)(2,1)S(1)}, bf16[256,2048]{1,0:T(8,128)(2,1)S(1)}, u32[]{:S(2)}, u32[]{:S(2)}) collective-permute-start(bf16[256,2048]{1,0:T(8,128)(2,1)S(1)} %add_convert_fusion.7), channel_id=1, source_target_pairs={{0,1},{1,2},{2,3},{3,0},{4,5},{5,6},{6,7},{7,4},{8,9},{9,10},{10,1... | collective-permute-start | bytes 3145736 | tf_op jit(solution)/shard_map/ppermute | solution.py:267
  658.5 20.8 %collective-permute-start.21 = (bf16[512,256]{1,0:T(8,128)(2,1)}, bf16[512,256]{1,0:T(8,128)(2,1)}, u32[]{:S(2)}, u32[]{:S(2)}) collective-permute-start(bf16[512,256]{1,0:T(8,128)(2,1)} %get-tuple-element.126), channel_id=1, source_target_pairs={{0,3},{1,0},{2,1},{3,2},{4,7},{5,4},{6,5},{7,6},{8,11},{9,8},{10,9... | collective-permute-start | bytes 786440 | tf_op jit(solution)/shard_map/ppermute | solution.py:453
  662.4 16.9 %collective-permute-start.22 = (bf16[512,256]{1,0:T(8,128)(2,1)}, bf16[512,256]{1,0:T(8,128)(2,1)}, u32[]{:S(2)}, u32[]{:S(2)}) collective-permute-start(bf16[512,256]{1,0:T(8,128)(2,1)} %get-tuple-element.125), channel_id=1, source_target_pairs={{0,2},{1,3},{2,0},{3,1},{4,6},{5,7},{6,4},{7,5},{8,10},{9,11},{10,... | collective-permute-start | bytes 786440 | tf_op jit(solution)/shard_map/ppermute | solution.py:453
  662.4 20.8 %collective-permute-start.23 = (bf16[512,256]{1,0:T(8,128)(2,1)}, bf16[512,256]{1,0:T(8,128)(2,1)}, u32[]{:S(2)}, u32[]{:S(2)}) collective-permute-start(bf16[512,256]{1,0:T(8,128)(2,1)} %get-tuple-element.124), channel_id=1, source_target_pairs={{0,1},{1,2},{2,3},{3,0},{4,5},{5,6},{6,7},{7,4},{8,9},{9,10},{10,1... | collective-permute-start | bytes 786440 | tf_op jit(solution)/shard_map/ppermute | solution.py:453
  744.4 29.2 %collective-permute-start.24 = (bf16[768,256]{0,1:T(8,128)(2,1)}, bf16[768,256]{0,1:T(8,128)(2,1)}, u32[]{:S(2)}, u32[]{:S(2)}) collective-permute-start(bf16[768,256]{0,1:T(8,128)(2,1)} %copy.198), channel_id=1, source_target_pairs={{0,1},{1,2},{2,3},{3,0},{4,5},{5,6},{6,7},{7,4},{8,9},{9,10},{10,1... | collective-permute-start | bytes 1179656 | tf_op jit(solution)/shard_map/ppermute | solution.py:466
  748.8 31.7 %collective-permute-start.25 = (bf16[768,256]{0,1:T(8,128)(2,1)}, bf16[768,256]{0,1:T(8,128)(2,1)}, u32[]{:S(2)}, u32[]{:S(2)}) collective-permute-start(bf16[768,256]{0,1:T(8,128)(2,1)} %copy.199), channel_id=1, source_target_pairs={{0,2},{1,3},{2,0},{3,1},{4,6},{5,7},{6,4},{7,5},{8,10},{9,11},{10,... | collective-permute-start | bytes 1179656 | tf_op jit(solution)/shard_map/ppermute | solution.py:466
  753.8 26.7 %collective-permute-start.26 = (bf16[768,256]{0,1:T(8,128)(2,1)}, bf16[768,256]{0,1:T(8,128)(2,1)S(1)}, u32[]{:S(2)}, u32[]{:S(2)}) collective-permute-start(bf16[768,256]{0,1:T(8,128)(2,1)} %copy.200), channel_id=1, source_target_pairs={{0,3},{1,0},{2,1},{3,2},{4,7},{5,4},{6,5},{7,6},{8,11},{9,8},{10,9... | collective-permute-start | bytes 1179656 | tf_op jit(solution)/shard_map/ppermute | solution.py:466
  773.6 79.0 %collective-permute-start.49 = (bf16[2048,4,256]{2,0,1:T(8,128)(2,1)}, bf16[2048,4,256]{2,0,1:T(8,128)(2,1)}, u32[]{:S(2)}, u32[]{:S(2)}) collective-permute-start(bf16[2048,4,256]{2,0,1:T(8,128)(2,1)} %convolution_convert_fusion.1), channel_id=1, source_target_pairs={{0,4},{4,0},{8,12},{12,8},{16,20},{20,16},{24,28},{28,24},{1,5},{5... | collective-permute-start | bytes 12582920 | tf_op jit(solution)/shard_map/ppermute | solution.py:298
  780.5 35.5 %collective-permute-start.41 = (bf16[4,256,2,384]{3,1,2,0:T(8,128)(2,1)}, bf16[4,256,2,384]{3,1,2,0:T(8,128)(2,1)}, u32[]{:S(2)}, u32[]{:S(2)}) collective-permute-start(bf16[4,256,2,384]{3,1,2,0:T(8,128)(2,1)} %fusion.114), channel_id=1, source_target_pairs={{0,4},{4,0},{8,12},{12,8},{16,20},{20,16},{24,28},{28,24},{1,5},{5... | collective-permute-start | bytes 4718600 | tf_op jit(solution)/shard_map/ppermute | solution.py:298
  849.9 26.2 %collective-permute-start.63 = (bf16[1024,2,256]{2,0,1:T(8,128)(2,1)S(1)}, bf16[1024,2,256]{2,0,1:T(8,128)(2,1)S(1)}, u32[]{:S(2)}, u32[]{:S(2)}) collective-permute-start(bf16[1024,2,256]{2,0,1:T(8,128)(2,1)S(1)} %dynamic-slice_bitcast_fusion.3), channel_id=1, source_target_pairs={{0,8},{4,12},{8,0},{12,4},{16,24},{20,28},{24,16},{28,20},{1,9},{5... | collective-permute-start | bytes 3145736 | tf_op jit(solution)/shard_map/ppermute | solution.py:287
  851.5 26.4 %collective-permute-start.65 = (bf16[1024,2,256]{2,0,1:T(8,128)(2,1)S(1)}, bf16[1024,2,256]{2,0,1:T(8,128)(2,1)S(1)}, u32[]{:S(2)}, u32[]{:S(2)}) collective-permute-start(bf16[1024,2,256]{2,0,1:T(8,128)(2,1)S(1)} %dynamic-slice_bitcast_fusion.2), channel_id=1, source_target_pairs={{0,16},{4,20},{8,24},{12,28},{16,0},{20,4},{24,8},{28,12},{1,17},{... | collective-permute-start | bytes 3145736 | tf_op jit(solution)/shard_map/ppermute | solution.py:287
  856.5 42.0 %collective-permute-start.50 = (bf16[1024,2,256]{2,0,1:T(8,128)(2,1)S(1)}, bf16[1024,2,256]{2,0,1:T(8,128)(2,1)S(1)}, u32[]{:S(2)}, u32[]{:S(2)}) collective-permute-start(bf16[1024,2,256]{2,0,1:T(8,128)(2,1)S(1)} %dynamic-slice_bitcast_fusion.7), channel_id=1, source_target_pairs={{0,8},{4,12},{8,0},{12,4},{16,24},{20,28},{24,16},{28,20},{1,9},{5... | collective-permute-start | bytes 3145736 | tf_op jit(solution)/shard_map/ppermute | solution.py:287
  876.4 14.9 %collective-permute-start.64 = (bf16[1024,256]{1,0:T(8,128)(2,1)S(1)}, bf16[1024,256]{1,0:T(8,128)(2,1)S(1)}, u32[]{:S(2)}, u32[]{:S(2)}) collective-permute-start(bf16[1024,256]{1,0:T(8,128)(2,1)S(1)} %dynamic-slice_bitcast_fusion.9), channel_id=1, source_target_pairs={{0,16},{4,20},{8,24},{12,28},{16,0},{20,4},{24,8},{28,12},{1,17},{... | collective-permute-start | bytes 1572872 | tf_op jit(solution)/shard_map/ppermute | solution.py:287
  879.0 93.5 %collective-permute-start.66 = (bf16[1024,256]{1,0:T(8,128)(2,1)}, bf16[1024,256]{1,0:T(8,128)(2,1)}, u32[]{:S(2)}, u32[]{:S(2)}) collective-permute-start(bf16[1024,256]{1,0:T(8,128)(2,1)} %dynamic-slice_bitcast_fusion.8), channel_id=1, source_target_pairs={{0,8},{4,12},{8,0},{12,4},{16,24},{20,28},{24,16},{28,20},{1,9},{5... | collective-permute-start | bytes 1572872 | tf_op jit(solution)/shard_map/ppermute | solution.py:287
  881.2 40.6 %collective-permute-start.53 = (bf16[1024,2,256]{2,0,1:T(8,128)(2,1)}, bf16[1024,2,256]{2,0,1:T(8,128)(2,1)}, u32[]{:S(2)}, u32[]{:S(2)}) collective-permute-start(bf16[1024,2,256]{2,0,1:T(8,128)(2,1)} %dynamic-slice_bitcast_fusion.6), channel_id=1, source_target_pairs={{0,16},{4,20},{8,24},{12,28},{16,0},{20,4},{24,8},{28,12},{1,17},{... | collective-permute-start | bytes 3145736 | tf_op jit(solution)/shard_map/ppermute | solution.py:287
  919.1 60.1 %collective-permute-start.58 = (bf16[2,256,1,2048]{3,1,2,0:T(8,128)(2,1)S(1)}, bf16[2,256,1,2048]{3,1,2,0:T(8,128)(2,1)S(1)}, u32[]{:S(2)}, u32[]{:S(2)}) collective-permute-start(bf16[2,256,1,2048]{3,1,2,0:T(8,128)(2,1)S(1)} %dynamic-slice_bitcast_fusion.1), channel_id=1, source_target_pairs={{0,8},{4,12},{8,0},{12,4},{16,24},{20,28},{24,16},{28,20},{1,9},{5... | collective-permute-start | bytes 6291464 | tf_op jit(solution)/shard_map/ppermute | solution.py:287
  920.7 14.9 %collective-permute-start.51 = (bf16[1024,256]{1,0:T(8,128)(2,1)S(1)}, bf16[1024,256]{1,0:T(8,128)(2,1)S(1)}, u32[]{:S(2)}, u32[]{:S(2)}) collective-permute-start(bf16[1024,256]{1,0:T(8,128)(2,1)S(1)} %dynamic-slice_bitcast_fusion.11), channel_id=1, source_target_pairs={{0,16},{4,20},{8,24},{12,28},{16,0},{20,4},{24,8},{28,12},{1,17},{... | collective-permute-start | bytes 1572872 | tf_op jit(solution)/shard_map/ppermute | solution.py:287
  923.4 48.1 %collective-permute-start.54 = (bf16[1024,256]{1,0:T(8,128)(2,1)S(1)}, bf16[1024,256]{1,0:T(8,128)(2,1)S(1)}, u32[]{:S(2)}, u32[]{:S(2)}) collective-permute-start(bf16[1024,256]{1,0:T(8,128)(2,1)S(1)} %dynamic-slice_bitcast_fusion.10), channel_id=1, source_target_pairs={{0,8},{4,12},{8,0},{12,4},{16,24},{20,28},{24,16},{28,20},{1,9},{5... | collective-permute-start | bytes 1572872 | tf_op jit(solution)/shard_map/ppermute | solution.py:287
  924.7 58.5 %collective-permute-start.60 = (bf16[2,256,1,2048]{3,1,2,0:T(8,128)(2,1)S(1)}, bf16[2,256,1,2048]{3,1,2,0:T(8,128)(2,1)S(1)}, u32[]{:S(2)}, u32[]{:S(2)}) collective-permute-start(bf16[2,256,1,2048]{3,1,2,0:T(8,128)(2,1)S(1)} %dynamic-slice_bitcast_fusion), channel_id=1, source_target_pairs={{0,16},{4,20},{8,24},{12,28},{16,0},{20,4},{24,8},{28,12},{1,17},{... | collective-permute-start | bytes 6291464 | tf_op jit(solution)/shard_map/ppermute | solution.py:287
  935.8 35.9 %collective-permute-start.52 = (bf16[512,256]{1,0:T(8,128)(2,1)S(1)}, bf16[512,256]{1,0:T(8,128)(2,1)S(1)}, u32[]{:S(2)}, u32[]{:S(2)}) collective-permute-start(bf16[512,256]{1,0:T(8,128)(2,1)S(1)} %slice.373), channel_id=1, source_target_pairs={{0,1},{1,2},{2,3},{3,0},{4,5},{5,6},{6,7},{7,4},{8,9},{9,10},{10,1... | collective-permute-start | bytes 786440 | tf_op jit(solution)/shard_map/ppermute | solution.py:267
  980.1 17.7 %collective-permute-start.59 = (bf16[256,1,2048]{2,0,1:T(8,128)(2,1)S(1)}, bf16[256,1,2048]{2,0,1:T(8,128)(2,1)S(1)}, u32[]{:S(2)}, u32[]{:S(2)}) collective-permute-start(bf16[256,1,2048]{2,0,1:T(8,128)(2,1)S(1)} %dynamic-slice_bitcast_fusion.5), channel_id=1, source_target_pairs={{0,16},{4,20},{8,24},{12,28},{16,0},{20,4},{24,8},{28,12},{1,17},{... | collective-permute-start | bytes 3145736 | tf_op jit(solution)/shard_map/ppermute | solution.py:287
  984.2 16.1 %collective-permute-start.61 = (bf16[256,1,2048]{2,0,1:T(8,128)(2,1)S(1)}, bf16[256,1,2048]{2,0,1:T(8,128)(2,1)S(1)}, u32[]{:S(2)}, u32[]{:S(2)}) collective-permute-start(bf16[256,1,2048]{2,0,1:T(8,128)(2,1)S(1)} %dynamic-slice_bitcast_fusion.4), channel_id=1, source_target_pairs={{0,8},{4,12},{8,0},{12,4},{16,24},{20,28},{24,16},{28,20},{1,9},{5... | collective-permute-start | bytes 3145736 | tf_op jit(solution)/shard_map/ppermute | solution.py:287
  (133 other events, 1551.2 us)

commit v2 on v1

--- a/solution.py
+++ b/solution.py
@@ -244,6 +244,347 @@
     return scaled, inverse, (scaled * gain_row).astype(BF16)
 
 
+def feed_kernel(
+    n, dp, tile, cut,
+    normed_in, cot_in, gate_up_in, down_in,
+    sum_out, mixed_out, grads_out,
+    gate_up, down, normed, cots, acts, grads, arriving, sending, mixed, turned,
+    load_sems, weight_sems, out_sems, gather_send, gather_recv, sum_send, sum_recv, mixed_sems,
+):
+    share, width = normed_in.shape
+    hidden = down_in.shape[0]
+    block = width // dp
+    piece = share // cut
+    per = hidden // tile
+    me = lax.axis_index("tensor")
+    core = lax.rem(lax.axis_index("dp"), 2)
+    place = (me, n - 1 - me)
+    ends = (me < n - 1, me > 0)
+    partner = (me + 1, me - 1)
+
+    def device(way):
+        return {"tensor": partner[way]}
+
+    def rows_of(j, size=share):
+        return pl.ds(pl.multiple_of(j * share, 16), size)
+
+    barrier = pltpu.get_barrier_semaphore()
+    for way in range(2):
+
+        @pl.when(ends[way])
+        def _(way=way):
+            pl.semaphore_signal(barrier, inc=1, device_id=device(way), device_id_type=pl.DeviceIdType.MESH)
+
+    own_load = pltpu.make_async_copy(normed_in, normed.at[rows_of(me)], load_sems.at[0])
+    cot_load = pltpu.make_async_copy(cot_in, cots, load_sems.at[1])
+    own_load.start()
+
+    def weight_loads(f):
+        span = slice(f * tile, (f + 1) * tile)
+        return (
+            pltpu.make_async_copy(gate_up_in.at[0, :, span], gate_up.at[0:width, span], weight_sems.at[0, f]),
+            pltpu.make_async_copy(gate_up_in.at[1, :, span], gate_up.at[width:2 * width, span], weight_sems.at[1, f]),
+            pltpu.make_async_copy(down_in.at[span], down.at[span], weight_sems.at[2, f]),
+        )
+
+    weights = [weight_loads(f) for f in range(per)]
+    for load in weights[0]:
+        load.start()
+    cot_load.start()
+    for loads in weights[1:]:
+        for load in loads:
+            load.start()
+    inner = (me > 0) & (me < n - 1)
+
+    @pl.when(inner)
+    def _():
+        pl.semaphore_wait(barrier, 2)
+
+    @pl.when(jnp.logical_not(inner))
+    def _():
+        pl.semaphore_wait(barrier, 1)
+
+    def gather(way, j):
+        return pltpu.make_async_remote_copy(
+            src_ref=normed.at[rows_of(j)], dst_ref=normed.at[rows_of(j)],
+            send_sem=gather_send.at[way, j], recv_sem=gather_recv.at[way, j],
+            device_id=device(way), device_id_type=pl.DeviceIdType.MESH)
+
+    def gather_arrival(way, j):
+        return pltpu.make_async_copy(normed.at[rows_of(j)], normed.at[rows_of(j)], gather_recv.at[way, j])
+
+    def pass_on(way, j, q):
+        rows = pl.ds(pl.multiple_of(j * share + q * piece, 16), piece)
+        last = j == partner[way]
+        slot = jnp.where(last, n, j) if way else j
+        goal = pl.ds(pl.multiple_of(slot * share + q * piece, 16), piece)
+        return pltpu.make_async_remote_copy(
+            src_ref=sending.at[rows], dst_ref=arriving.at[goal],
+            send_sem=sum_send.at[way, j * cut + q], recv_sem=sum_recv.at[way, j * cut + q],
+            device_id=device(way), device_id_type=pl.DeviceIdType.MESH)
+
+    def sum_arrival(way, j, q, slot):
+        rows = pl.ds(pl.multiple_of(slot * share + q * piece, 16), piece)
+        return pltpu.make_async_copy(arriving.at[rows], arriving.at[rows], sum_recv.at[way, j * cut + q])
+
+    own_load.wait()
+    for way in range(2):
+
+        @pl.when(ends[way])
+        def _(way=way):
+            gather(way, me).start()
+
+    def first_half(rows, f):
+        span = pl.ds(pl.multiple_of(f * tile, tile), tile)
+        upper = pl.ds(pl.multiple_of(hidden + f * tile, tile), tile)
+        gate = nn(normed[rows, :], gate_up[0:width, span])
+        up = nn(normed[rows, :], gate_up[width:2 * width, span])
+        grad_act = nt(cots[rows, :], down[span, :])
+        sigma = 1.0 / (1.0 + jnp.exp(-gate))
+        silu = gate * sigma
+        acts[rows, span] = (silu * up).astype(BF16)
+        grads[rows, span] = (grad_act * up * (sigma + silu * (1.0 - sigma))).astype(BF16)
+        grads[rows, upper] = (grad_act * silu).astype(BF16)
+
+    def second_half(rows):
+        @pl.loop(0, width // tile)
+        def _(d):
+            span = pl.ds(pl.multiple_of(d * tile, tile), tile)
+            lower = pl.ds(pl.multiple_of(width + d * tile, tile), tile)
+            sending[rows, span] = (
+                nt(grads[rows, 0:hidden], gate_up[span, :]) + nt(grads[rows, hidden:], gate_up[lower, :])
+            ).astype(BF16)
+
+    both = jnp.minimum(me, n - 1 - me)
+    long_side = jnp.where(me < n - 1 - me, 1, -1)
+
+    def chunk_at(k):
+        near = (k + 1) // 2 * (-1 if k % 2 else 1)
+        return me + jnp.where(k <= 2 * both, near, (k - both) * long_side)
+
+    def chunk_rows(k):
+        return rows_of(chunk_at(k) if k else me)
+
+    def put_mixed(k):
+        return pltpu.make_async_copy(mixed, mixed_out.at[chunk_rows(k)], mixed_sems)
+
+    def mix(k):
+        if k:
+            put_mixed(k - 1).wait()
+
+        @pl.loop(0, width // tile)
+        def _(d):
+            span = pl.ds(pl.multiple_of(d * tile, tile), tile)
+            mixed[:, span] = nn(acts[chunk_rows(k), :], down[:, span]).astype(BF16)
+
+        put_mixed(k).start()
+
+    for f in range(per):
+        for load in weights[f]:
+            load.wait()
+        if f == 0:
+            cot_load.wait()
+        first_half(rows_of(me), f)
+    second_half(rows_of(me))
+
+    for k in range(1, n):
+        mix(k - 1)
+        for way in range(2):
+            j = me - k if way == 0 else me + k
+            there = (me >= k) if way == 0 else (me + k <= n - 1)
+
+            @pl.when(there)
+            def _(way=way, j=j):
+                gather_arrival(way, j).wait()
+
+                @pl.when(ends[way])
+                def _():
+                    gather(way, j).start()
+
+        rows = chunk_rows(k)
+
+        @pl.loop(0, per)
+        def _(f):
+            first_half(rows, f)
+
+        second_half(rows)
+        for way in range(2):
+
+            @pl.when(place[way] == 0)
+            def _(way=way):
+                j = me + k if way == 0 else me - k
+                for q in range(cut):
+                    pass_on(way, j, q).start()
+
+    room = 3 * block
+    half = dp // 4
+    items = dp // 2 * 2 * per
+
+    def put(pair, j):
+        start = pl.multiple_of((lax.rem(pair, 2) * 2 + j) * room, 16)
+        return pltpu.make_async_copy(
+            gate_up.at[pl.ds(start, room)], grads_out.at[2 * pair + j], out_sems.at[lax.rem(pair, 2), j])
+
+    def weight_item(i):
+        pair, f = lax.div(i, 2 * per), lax.rem(i, 2 * per)
+        slot = lax.rem(pair, 2)
+        other = lax.div(pair, half)
+
+        def turn(source):
+            for j in range(2):
+                column = 2 * (2 * lax.rem(pair, half) + j) + lax.rem(core + 1 + other, 2)
+                span = pl.ds(pl.multiple_of(column * block, block), block)
+                turned[pl.ds(j * block, block), :] = source[:, span].T
+
+        def store(row, goal, product):
+            for j in range(2):
+                start = pl.multiple_of((slot * 2 + j) * room + row * block, 16)
+                gate_up[pl.ds(start, block), goal] = product[j * block:(j + 1) * block]
+
+        @pl.when(f == 0)
+        def _():
+            @pl.when(pair >= 2)
+            def _():
+                for j in range(2):
+                    put(pair - 2, j).wait()
+
+            turn(normed)
+
+        @pl.when(f == per)
+        def _():
+            turn(cots)
+
+        @pl.when(f < per)
+        def _():
+            goal = pl.ds(pl.multiple_of(f * tile, tile), tile)
+            for row in range(2):
+                span = pl.ds(pl.multiple_of(row * hidden + f * tile, tile), tile)
+                store(row, goal, nn(turned[...], grads[:, span]).astype(BF16))
+
+        @pl.when(f >= per)
+        def _():
+            goal = pl.ds(pl.multiple_of((f - per) * tile, tile), tile)
+            store(2, goal, nn(turned[...], acts[:, goal]).astype(BF16))
+
+        @pl.when(f == 2 * per - 1)
+        def _():
+            for j in range(2):
+                put(pair, j).start()
+
+    first_step, last_step = cut + 1, cut * (n - 1) + n - 2
+    every = -(-items // (last_step - first_step))
+
+    def serve(step):
+        for way in range(2):
+            count = step - place[way]
+            j_place = lax.div(count, cut) + 1
+            q = lax.rem(count, cut)
+            j = j_place if way == 0 else n - 1 - j_place
+
+            @pl.when((place[way] > 0) & (j_place > place[way]) & (j_place < n))
+            def _(way=way, j=j, q=q):
+                sum_arrival(way, j, q, j).wait()
+                rows = pl.ds(pl.multiple_of(j * share + q * piece, 16), piece)
+                sending[rows, :] = (sending[rows, :].astype(F32) + arriving[rows, :].astype(F32)).astype(BF16)
+                pass_on(way, j, q).start()
+
+    @pl.loop(first_step, last_step)
+    def _(step):
+        serve(step)
+        for j in range(every):
+            item = (step - first_step) * every + j
+
+            @pl.when(item < items)
+            def _(item=item):
+                weight_item(item)
+
+
+    mix(n - 1)
+
+    for way in range(2):
+
+        @pl.when(place[way] > 0)
+        def _(way=way):
+            for q in range(cut):
+                slot = n if way else me
+                sum_arrival(way, me, q, slot).wait()
+            slot = pl.ds(n * share, share) if way else rows_of(me)
+
+            @pl.loop(0, width // tile)
+            def _(d):
+                span = pl.ds(pl.multiple_of(d * tile, tile), tile)
+                sending[rows_of(me), span] = (
+                    sending[rows_of(me), span].astype(F32) + arriving[slot, span].astype(F32)
+                ).astype(BF16)
+
+    final = pltpu.make_async_copy(sending.at[rows_of(me)], sum_out, load_sems.at[0])
+    final.start()
+    for pair in (dp // 2 - 2, dp // 2 - 1):
+        for j in range(2):
+            put(pair, j).wait()
+    put_mixed(n - 1).wait()
+    final.wait()
+    for way in range(2):
+
+        @pl.when(ends[way])
+        def _(way=way):
+            @pl.loop(0, n)
+            def _(j):
+                mine = (j <= me) if way == 0 else (j >= me)
+
+                @pl.when(mine)
+                def _():
+                    gather(way, j).wait_send()
+
+                @pl.when(jnp.logical_not(mine))
+                def _():
+                    for q in range(cut):
+                        pass_on(way, j, q).wait_send()
+
+
+def feed_forward(normed, cotangent, gate_up, down, n, dp, tile=512, cut=4):
+    share, width = normed.shape
+    hidden = down.shape[0]
+    tokens = n * share
+    block = width // dp
+    anywhere = pl.BlockSpec(memory_space=pl.ANY)
+    return pl.pallas_call(
+        partial(feed_kernel, n, dp, tile, cut),
+        out_shape=(
+            jax.ShapeDtypeStruct((share, width), BF16),
+            jax.ShapeDtypeStruct((tokens, width), BF16),
+            jax.ShapeDtypeStruct((dp, 3 * block, hidden), BF16),
+        ),
+        in_specs=[anywhere] * 4,
+        out_specs=(anywhere,) * 3,
+        scratch_shapes=[
+            pltpu.VMEM((2 * width, hidden), BF16),
+            pltpu.VMEM((hidden, width), BF16),
+            pltpu.VMEM((tokens, width), BF16),
+            pltpu.VMEM((tokens, width), BF16),
+            pltpu.VMEM((tokens, hidden), BF16),
+            pltpu.VMEM((tokens, 2 * hidden), BF16),
+            pltpu.VMEM((tokens + share, width), BF16),
+            pltpu.VMEM((tokens, width), BF16),
+            pltpu.VMEM((share, width), BF16),
+            pltpu.VMEM((2 * block, tokens), BF16),
+            pltpu.SemaphoreType.DMA((2,)),
+            pltpu.SemaphoreType.DMA((3, hidden // tile)),
+            pltpu.SemaphoreType.DMA((2, 2)),
+            pltpu.SemaphoreType.DMA((2, n)),
+            pltpu.SemaphoreType.DMA((2, n)),
+            pltpu.SemaphoreType.DMA((2, n * cut)),
+            pltpu.SemaphoreType.DMA((2, n * cut)),
+            pltpu.SemaphoreType.DMA,
+        ],
+        compiler_params=pltpu.CompilerParams(
+            collective_id=0, has_side_effects=True, vmem_limit_bytes=60 * 2**20),
+        cost_estimate=pl.CostEstimate(
+            flops=18 * tokens * width * hidden, bytes_accessed=2 * 24 * 2**20, transcendentals=tokens * hidden),
+        name="feed_forward",
+    )(normed, cotangent, gate_up, down)
+
+
 def ring(size, shift=1):
     return [(i, (i + shift) % size) for i in range(size)]
 
@@ -275,7 +616,7 @@
     return size.bit_length() - 1
 
 
-def halve(current, axis, order, left=None):
+def halve(current, axis, order):
     size = lax.axis_size("dp")
     mine = lax.axis_index("dp")
     remaining = sorted(order, reverse=True)
@@ -292,16 +633,15 @@
     return current
 
 
-def scatter_dp(make, axis, stream_axis):
+def scatter_dp(other, own):
     size = lax.axis_size("dp")
-    core = lax.axis_index("dp") & 1
-    arrived = lax.ppermute(make(1 - core).astype(BF16), "dp", flip(size, 0))
-    current = (make(core) + arrived.astype(F32)).astype(BF16)
+    arrived = lax.ppermute(other.astype(BF16), "dp", flip(size, 0))
+    current = (own.astype(F32) + arrived.astype(F32)).astype(BF16)
     rest = list(range(1, bits_of(size)))
-    half = current.shape[stream_axis] // 2
-    first = halve(lax.slice_in_dim(current, 0, half, axis=stream_axis), axis, rest)
-    second = halve(lax.slice_in_dim(current, half, 2 * half, axis=stream_axis), axis, rest[::-1])
-    return jnp.concatenate([first, second], axis=stream_axis - (1 if stream_axis > axis else 0))
+    half = current.shape[1] // 2
+    first = halve(current[:, :half], 0, rest)
+    second = halve(current[:, half:], 0, rest[::-1])
+    return jnp.concatenate([first, second], axis=0)
 
 
 def scatter_small(blocks, over_tensor):
@@ -323,36 +663,26 @@
     return blocks
 
 
-def double(pieces, order):
-    size = lax.axis_size("dp")
-    mine = lax.axis_index("dp")
-    n, rows, cols = pieces.shape
-    done = []
-    current = pieces.reshape((n, rows, cols))
-    for bit in order:
-        arrived = lax.ppermute(current, "dp", flip(size, bit))
-        own = ((mine >> bit) & 1) == 0
-        place = 1 + sum(1 for other in done if other > bit)
-        low = jnp.where(own, current, arrived)
-        high = jnp.where(own, arrived, current)
-        current = jnp.stack([low, high], axis=place)
-        done.append(bit)
-    return current.reshape(n, size * rows, cols)
-
-
 def gather_weight(shard):
-    size = lax.axis_size("dp")
+    piece = chunk_of(shard, lax.axis_index("dp"), shard.shape[0] // lax.axis_size("dp"), 0)
+    whole = lax.all_gather(piece, ("tensor", "dp"), axis=0, tiled=True)
+    return whole.reshape((lax.axis_size("tensor"),) + shard.shape)
+
+
+def exchange(parts, shift):
     n = lax.axis_size("tensor")
-    rows = shard.shape[0] // size
-    pieces = [chunk_of(shard, lax.axis_index("dp"), rows, 0)]
-    for _ in range(n - 1):
-        pieces.append(lax.ppermute(pieces[-1], "tensor", ring(n)))
-    pieces = jnp.stack(pieces)
-    half = shard.shape[1] // 2
-    rest = list(range(1, bits_of(size)))
-    first = double(pieces[:, :, :half], rest + [0])
-    second = double(pieces[:, :, half:], rest[::-1] + [0])
-    return jnp.concatenate([first, second], axis=2)
+    me = lax.axis_index("tensor")
+    came = [parts(me)]
+    for s in range(1, n):
+        came.append(lax.ppermute(parts((me + s) % n), "tensor", ring(n, s)))
+    return came
+
+
+def by_place(came):
+    n = len(came)
+    me = lax.axis_index("tensor")
+    stacked = jnp.stack(came)
+    return [pick(stacked, (me + n - j) % n, 0) for j in range(n)]
 
 
 def local(
@@ -409,37 +739,17 @@
     seg_col = segments.reshape(token_rows, 1)
     low, attended, root = attention_forward(joined, cosines, sines, maps_t, seg_row, seg_col, heads)
     attended_flat = attended.reshape(groups * query_width, token_rows)
-    att_parts = [chunk_of(attended_flat, me, share, 1)]
-    for s in range(1, n):
-        att_parts.append(
-            lax.ppermute(chunk_of(attended_flat, (me + s) % n, share, 1), "tensor", ring(n, s))
-        )
-    att_share = jnp.stack(att_parts)
-    down_places = jnp.stack([pick(down_all, (me + n - s) % n, 0) for s in range(n)])
-    lowrank_out = dot("nct,nrc->tr", att_share, down_places)
+    att_came = exchange(lambda j: chunk_of(attended_flat, j, share, 1), 1)
+    att_share = jnp.stack(by_place(att_came))
+    lowrank_out = dot("nct,nrc->tr", att_share, down_all)
     tokens_share = chunk_of(tokens, me, share, 0).astype(F32)
     hidden = tokens_share + dot("nct,ncd->td", att_share, all_branch)
     scaled_two, inverse_two, normed_two = normalize(hidden, gains[1])
 
-    normed, acts, grads, cots, mixed_parts, grad_parts = [normed_two], [], [], [], [], []
-    for k in range(n):
-        if k < n - 1:
-            normed.append(lax.ppermute(normed[k], "tensor", ring(n)))
-        cot = chunk_of(cotangent, (me + n - k) % n, share, 0)
-        gate_up = dot("td,dsf->tsf", normed[k], w_gate_up)
-        gate, upper = gate_up[:, 0], gate_up[:, 1]
-        sigma = jax.nn.sigmoid(gate)
-        silu = gate * sigma
-        act = (silu * upper).astype(BF16)
-        grad_act = dot("td,fd->tf", cot, w_down)
-        grad_gate = grad_act * upper * sigma * (1.0 + gate * (1.0 - sigma))
-        grad_gate_up = jnp.stack([grad_gate, grad_act * silu], axis=1).astype(BF16)
-        grad_parts.append(dot("tsf,dsf->td", grad_gate_up, w_gate_up).astype(BF16))
-        mixed_parts.append(dot("tf,fd->td", act, w_down).astype(BF16))
-        acts.append(act)
-        grads.append(grad_gate_up)
-        cots.append(cot)
-    grad_normed_two = ring_sum(grad_parts)
+    grad_normed_two, mixed_parts, grads_feed = feed_forward(
+        normed_two, cotangent, jnp.transpose(w_gate_up, (1, 0, 2)), w_down, n, dp
+    )
+    grad_normed_two = grad_normed_two.astype(F32)
     weighted = grad_normed_two * gains[1]
     grad_hidden = chunk_of(cotangent, me, share, 0).astype(F32) + inverse_two * (
         weighted - scaled_two * jnp.mean(weighted * scaled_two, axis=-1, keepdims=True)
@@ -448,24 +758,17 @@
     grad_branch = grad_hidden.astype(BF16)
 
     grad_att_share = dot("ncd,td->nct", all_branch, grad_branch).astype(BF16)
-    back = [grad_att_share[0]]
-    for s in range(1, n):
-        back.append(lax.ppermute(grad_att_share[s], "tensor", ring(n, -s)))
-    order = [pick(jnp.stack(back), (j + n - me) % n, 0) for j in range(n)]
-    grad_attended = jnp.concatenate(order, axis=1).reshape(groups, query_width, token_rows)
-    mixed = ring_sum(mixed_parts)
+    back = by_place(exchange(lambda j: pick(grad_att_share, j, 0), 1))
+    grad_attended = jnp.concatenate(back, axis=1).reshape(groups, query_width, token_rows)
+    mixed = ring_sum([chunk_of(mixed_parts, (me + n - s) % n, share, 0) for s in range(n)])
     output = (hidden + mixed).astype(BF16)
 
     grad_joined, grad_maps = attention_backward(
         low, cosines, sines, maps_t, maps, seg_row, seg_col, attended, root, grad_attended, heads
     )
     flat_joined = grad_joined.reshape(groups * joined_width, token_rows)
-    parts = [chunk_of(flat_joined, me, share, 1)]
-    for s in range(1, n):
-        parts.append(
-            lax.ppermute(chunk_of(flat_joined, (me + s) % n, share, 1), "tensor", ring(n, s))
-        )
-    grad_normed_one = dot("nct,ncd->td", jnp.stack(parts), all_joined)
+    joined_share = jnp.stack(by_place(exchange(lambda j: chunk_of(flat_joined, j, share, 1), 1)))
+    grad_normed_one = dot("nct,ncd->td", joined_share, all_joined)
     scaled_one, inverse_one, _ = normalize(tokens_share, gains[0])
     weighted = grad_normed_one * gains[0]
     grad_input = (
@@ -475,28 +778,26 @@
     ).astype(BF16)
     gain_one = jnp.sum(grad_normed_one * scaled_one, axis=0)
 
-    all_normed = jnp.concatenate(normed, axis=0)
-    all_acts = jnp.concatenate(acts, axis=0)
-    all_grads = jnp.concatenate(grads, axis=0)
-    all_cots = jnp.concatenate(cots, axis=0)
     width = model_width // dp
-
-    def of_core(array, core):
-        return pick(array.reshape(array.shape[0], dp // 2, 2, width), core, 2)
-
-    out_gate_up = scatter_dp(
-        lambda core: dot("tbe,tsf->besf", of_core(all_normed, core), all_grads), 0, 2
-    )
-    out_down = scatter_dp(lambda core: dot("tf,tbe->fbe", all_acts, of_core(all_cots, core)), 1, 0)
-    flat_att = att_share.reshape(-1, share)
+    core = lax.axis_index("dp") & 1
+
+    def of_core(array, which):
+        return jnp.concatenate([chunk_of(array, 2 * q + which, width, 1) for q in range(dp // 2)], axis=1)
+
+    def blocks_of(product):
+        return product.astype(BF16).reshape(dp // 2, width, -1)
+
+    out_feed = scatter_dp(grads_feed[:dp // 2], grads_feed[dp // 2:]).reshape(3, width, -1)
+    out_gate_up = jnp.transpose(out_feed[:2], (1, 0, 2))
+    out_down = out_feed[2].T
+    flat_att = jnp.concatenate(att_came, axis=0)
     out_branch = scatter_dp(
-        lambda core: dot("ct,tbe->cbe", flat_att, of_core(grad_branch, core)), 1, 0
-    )
-    branch_rows = out_branch.shape[0] // n
-    out_branch = ring_sum([out_branch[s * branch_rows:(s + 1) * branch_rows] for s in range(n)])
+        *[blocks_of(dot("tb,ct->bc", of_core(grad_branch, which), flat_att)) for which in (1 - core, core)]
+    )
+    out_branch = ring_sum([chunk_of(out_branch, s, groups * query_width, 1) for s in range(n)]).T
     out_qkv = scatter_dp(
-        lambda core: dot("tbe,kct->bekc", of_core(normed_one, core), grad_joined), 0, 1
-    )
+        *[blocks_of(dot("tb,ct->bc", of_core(normed_one, which), flat_joined)) for which in (1 - core, core)]
+    ).reshape(width, groups, joined_width)
 
     lowrank_low = lowrank.astype(BF16)
     grad_up = jnp.concatenate(
@@ -521,7 +822,6 @@
     grad_lowrank_out = dot("td,rd->tr", grad_branch, o_up).astype(BF16)
     grad_o_up = dot("tr,td->rd", lowrank_out.astype(BF16), grad_branch)
     grad_o_down = dot("tr,nct->nrc", grad_lowrank_out, att_share)
-    grad_o_down = jnp.stack([pick(grad_o_down, (me + n - j) % n, 0) for j in range(n)])
     shared = jnp.concatenate(
         [gain_one[None], gain_two[None], grad_qkv_down.reshape(-1, model_width), grad_o_up], axis=0
     )

time: 1020 us -> 773 us (0.76)
  matrix products: 298 us -> 58.7 us
  Pallas kernels: 67.3 us -> 245 us
  waiting for transfers between devices: 292 us -> 196 us
  local copies, waits for them, and re-layouts: 179 us -> 125 us
  starting transfers between devices: 78.7 us -> 38 us
  other arithmetic: 75.3 us -> 60 us
  between operations: 2.83 us -> 15.8 us
    dot_general x25 -> x5, matrix products: 270 us -> 28.4 us  [the longest x1 10.6 us: local(): grad_normed_one = dot('nct,ncd->td', joined_share, all_joined)]
    pallas_call x0 -> x1, Pallas kernels: none -> 177 us  [feed_forward(): pl.pallas_call(partial(feed_kernel, n, dp, tile, cut), out_shape=(jax.Sha...]
    ppermute x34 -> x12, waiting for transfers between devices: 163 us -> 54 us  [the longest x9 53.9 us: exchange(): came.append(lax.ppermute(parts((me + s) % n), 'tensor', ring(n, s)))]
    dynamic_slice x13 -> x8, local copies, waits for them, and re-layouts: 57.5 us -> 19.9 us  [pick(): return lax.dynamic_index_in_dim(array, index, axis, keepdims=False)]
    another operation x27 -> x4, other arithmetic: 29.8 us -> 3.85 us  [the longest x3 3.82 us: by_place(): stacked = jnp.stack(came)]
    slice x8 -> x6, local copies, waits for them, and re-layouts: 5.89 us -> 30.4 us  [the longest x2 15.1 us: local(): out_gate_up = jnp.transpose(out_feed[:2], (1, 0, 2))]
    reshape x4 -> x1, local copies, waits for them, and re-layouts: 24.6 us -> 1.29 us  [local(): out_qkv = scatter_dp(*[blocks_of(dot('tb,ct->bc', of_core(normed_one, whi...]
    ppermute x34 -> x12, starting transfers between devices: 34.8 us -> 14.3 us  [the longest x9 14.3 us: exchange(): came.append(lax.ppermute(parts((me + s) % n), 'tensor', ring(n, s)))]
  transfers between devices with their start and end apart: 67 -> 40, of which waited for: 32 -> 16; matrix products, arithmetic and copies ran while one was open for 53% -> 28% of each run, Pallas kernels for 7% -> 32%
where the time goes in v2:
time: 773 us; the launch traced here: 758 us
  Pallas kernels  245 us (32%)
  waiting for transfers between devices  196 us (25%)
  local copies, waits for them, and re-layouts  125 us (16%)
  other arithmetic  60 us (8%)
  matrix products  58.7 us (8%)
  starting transfers between devices  38 us (5%)
  blocking collectives  19.2 us (2%)
  between operations  15.8 us (2%)
    pallas_call x1, Pallas kernels, feed_forward(): pl.pallas_call(partial(feed_kernel, n, dp, tile, cut), out_shape=(jax.Sha...  177 us
    ppermute x12, waiting for transfers between devices, halve(): arrived = lax.ppermute(pick(current, 1 - own, where), 'dp', flip(size, bit))  110 us
    ppermute x9, waiting for transfers between devices, exchange(): came.append(lax.ppermute(parts((me + s) % n), 'tensor', ring(n, s)))  53.9 us
    unnamed x153, local copies, waits for them, and re-layouts  46.1 us
    pallas_call x1, Pallas kernels, attention_backward(): pl.pallas_call(partial(backward_kernel, heads, block), grid=(groups,), ou...  41.6 us
    pallas_call x1, Pallas kernels, attention_forward(): pl.pallas_call(partial(forward_kernel, heads, block), grid=(groups,), out...  25.9 us
    ppermute x6, waiting for transfers between devices, ring_sum(): arrived = lax.ppermute(running, 'tensor', ring(size)).astype(F32)  25.3 us
    dynamic_slice x8, local copies, waits for them, and re-layouts, pick(): return lax.dynamic_index_in_dim(array, index, axis, keepdims=False)  19.9 us
  transfers between devices with their start and end apart: 40, of which 16 were waited for; matrix products, arithmetic and copies ran while one was open for 28% of the time, Pallas kernels for 32%

profile of v2, /device:TPU:12, one launch (start us, length us, event | category | flops | bytes accessed | tf_op | source)
XLA Modules:
  0.0 757.9 jit_solution(12080756030871578411)
XLA Ops:
  11.6 6.7 copy.78
  18.8 3.3 fusion
  26.5 5.1 fusion.11.joined_ref
  31.6 25.9 %attention_forward.1 = (bf16[2,384,1024]{2,1,0:T(8,128)(2,1)S(1)}, bf16[2,256,1024]{2,1,0:T(8,128)(2,1)S(1)}, f32[2,4,1,1024]{3,2,1,0:T(1,128)S(1)}) custom-call(f32[2,384,1024]{2,1,0:T(8,128)} %fusion.11.joined_ref, f32[32,1024]{1,0:T(8,128)S(1)} %get-tuple-element.115.cos_ref, f32[32,1024]{1,0:T(8,128)S(1)} %get-tuple-element.114.sin_ref, ...), custom_call_target="tpu_custom_call" | custom-call | tf_op jit(solution)/shard_map/attention_forward/pallas_call | solution.py:121
  66.8 3.4 fusion.69
  72.5 4.3 constant_dynamic-slice_fusion.16
  77.0 17.6 %copy.131 = bf16[2048,2,2048]{2,0,1:T(8,128)(2,1)} copy(bf16[2048,2,2048]{2,1,0:T(2,128)(2,1)} %param.24) | data formatting | bytes 33554432 | tf_op args[11]
  94.6 19.2 %all_gather.11 = bf16[4,8,512]{2,1,0:T(8,128)(2,1)} all-gather(bf16[1,8,512]{2,1,0:T(8,128)(2,1)S(1)} %all_gather_reshape.3), channel_id=1, replica_groups=mesh['dp'=8,'tensor'=4] {'tensor'}, dimensions={0}, use_global_device_ids=true | all-gather | bytes 40960 | tf_op jit(solution)/shard_map/all_gather | solution.py:727
  117.7 6.7 multiply_reduce_fusion
  125.8 177.4 %feed_forward.1 = (bf16[256,2048]{1,0:T(8,128)(2,1)}, bf16[1024,2048]{1,0:T(8,128)(2,1)}, bf16[8,768,2048]{2,1,0:T(8,128)(2,1)}) custom-call(bf16[256,2048]{1,0:T(8,128)(2,1)} %multiply_convert_fusion.normed_in, bf16[1024,2048]{1,0:T(8,128)(2,1)} %cot_in.1, bf16[2,2048,2048]{2,1,0:T(8,128)(2,1)} %bitcast.261, bf16[2048,2048]{1,0:T(8,128)(2,1)} %down_in.1), custom_call_target="tpu_custom_call" | custom-call | flops 77309411328 | bytes 50331648 | tf_op jit(solution)/shard_map/feed_forward/pallas_call | solution.py:551
  303.2 11.0 %slice.145 = bf16[4,768,2048]{2,1,0:T(8,128)(2,1)} slice(bf16[8,768,2048]{2,1,0:T(8,128)(2,1)} %get-tuple-element.27), slice={[0:4], [0:768], [0:2048]} | slice | bytes 25165824 | tf_op jit(solution)/shard_map/slice | solution.py:790
  318.9 4.5 convolution_convert_fusion
  329.3 3.5 collective-permute-start.7
  333.9 2.7 fusion.74
  346.1 4.6 convolution_convert_fusion.1
  353.1 25.7 %collective-permute-done.8 = bf16[512,256]{1,0:T(8,128)(2,1)} collective-permute-done((bf16[512,256]{1,0:T(8,128)(2,1)}, bf16[512,256]{1,0:T(8,128)(2,1)}, u32[]{:S(2)}, u32[]{:S(2)}) %collective-permute-start.8) | collective-permute-done | bytes 262176 | tf_op jit(solution)/shard_map/ppermute | solution.py:677
  381.1 41.6 %attention_backward.1 = (bf16[2,384,1024]{2,1,0:T(8,128)(2,1)S(1)}, f32[2,5,64,64]{3,2,1,0:T(8,128)S(1)}) custom-call(bf16[2,384,1024]{2,1,0:T(8,128)(2,1)} %copy-done.2, f32[32,1024]{1,0:T(8,128)S(1)} %copy-done.4, f32[32,1024]{1,0:T(8,128)S(1)} %get-tuple-element.114.sin_ref, bf16[2,320,64]{2,1,0:T(8,128)(2,1)S(1)} %bitcast.256, ...), custom_call_target="tpu_custom_call" | custom-call | tf_op jit(solution)/shard_map/attention_backward/pallas_call | solution.py:213
  427.9 4.2 fusion.48
  436.0 4.5 fusion.51
  440.9 3.1 fusion.9
  449.3 22.8 %collective-permute-done.10 = bf16[768,256]{0,1:T(8,128)(2,1)S(1)} collective-permute-done((bf16[768,256]{0,1:T(8,128)(2,1)}, bf16[768,256]{0,1:T(8,128)(2,1)S(1)}, u32[]{:S(2)}, u32[]{:S(2)}) %collective-permute-start.10) | collective-permute-done | bytes 393248 | tf_op jit(solution)/shard_map/ppermute | solution.py:677
  472.1 3.0 collective-permute-done.11
  483.5 4.1 fusion.3
  488.7 15.9 %collective-permute-done.4 = bf16[256,2048]{1,0:T(8,128)(2,1)S(1)} collective-permute-done((bf16[256,2048]{1,0:T(8,128)(2,1)S(1)}, bf16[256,2048]{1,0:T(8,128)(2,1)S(1)}, u32[]{:S(2)}, u32[]{:S(2)}) %collective-permute-start.4) | collective-permute-done | bytes 1048608 | tf_op jit(solution)/shard_map/ppermute | solution.py:608
  507.0 8.1 %collective-permute-done.26 = bf16[2,128,2048]{2,1,0:T(8,128)(2,1)S(1)} collective-permute-done((bf16[2,128,2048]{2,1,0:T(8,128)(2,1)S(1)}, bf16[2,128,2048]{2,1,0:T(8,128)(2,1)S(1)}, u32[]{:S(2)}, u32[]{:S(2)}) %collective-permute-start.26) | collective-permute-done | bytes 1048608 | tf_op jit(solution)/shard_map/ppermute | solution.py:628
  516.0 16.5 %collective-permute-done.28 = bf16[2,128,2048]{2,1,0:T(8,128)(2,1)S(1)} collective-permute-done((bf16[2,128,2048]{2,1,0:T(8,128)(2,1)S(1)}, bf16[2,128,2048]{2,1,0:T(8,128)(2,1)S(1)}, u32[]{:S(2)}, u32[]{:S(2)}) %collective-permute-start.28) | collective-permute-done | bytes 1048608 | tf_op jit(solution)/shard_map/ppermute | solution.py:628
  534.7 11.4 %collective-permute-done.27 = bf16[128,2048]{1,0:T(8,128)(2,1)S(1)} collective-permute-done((bf16[128,2048]{1,0:T(8,128)(2,1)S(1)}, bf16[128,2048]{1,0:T(8,128)(2,1)S(1)}, u32[]{:S(2)}, u32[]{:S(2)}) %collective-permute-start.27) | collective-permute-done | bytes 524320 | tf_op jit(solution)/shard_map/ppermute | solution.py:628
  548.4 4.7 collective-permute-done.30
  556.1 4.7 collective-permute-done.31
  562.4 10.6 %fusion.28 = (f32[2048]{0:T(1024)S(1)}, f32[256]{0:T(256)}, f32[256,2048]{1,0:T(8,128)}) fusion(f32[256]{0:T(256)S(1)} %copy-done.60, bf16[1024,2048]{1,0:T(8,128)(2,1)} %param.13, s32[]{:T(128)S(6)} %select_n.228, f32[2048]{0:T(1024)S(1)} %bitcast.294, bf16[4,768,2048]{2,1,0:T(8,128)(2,1)} %bitcast.299, bf16[1,768,256]{1,2,0:T(8,128)(2,1)} %get-tuple-element.79, ...), kind=kOutput, calls=%fused_computation.55 | convolution fusion | flops 3227252480 | bytes 17319940 | tf_op jit(solution)/shard_map/nct,ncd->td/dot_general | solution.py:771
  578.9 3.1 collective-permute-done.12
  582.7 4.0 collective-permute-done.13
  586.7 10.8 %add_convert_fusion = bf16[4,768,2048]{2,1,0:T(8,128)(2,1)S(1)} fusion(bf16[4,768,2048]{2,1,0:T(8,128)(2,1)} %collective-permute-done.33, bf16[8,768,2048]{2,1,0:T(8,128)(2,1)} %get-tuple-element.27), kind=kLoop, calls=%fused_computation | loop fusion | flops 25165824 | bytes 37748736 | tf_op jit(solution)/shard_map/convert_element_type | solution.py:639
  597.5 3.9 fusion.127
  603.7 2.9 copy.106
  607.1 6.6 constant_dynamic-slice_fusion.3
  613.7 4.8 copy.104
  619.7 5.9 collective-permute-start.15
  625.6 5.5 fusion.27
  631.2 4.8 copy.122
  636.1 2.8 copy.123
  638.8 32.7 %collective-permute-done.36 = bf16[2,384,2048]{1,2,0:T(8,128)(2,1)} collective-permute-done((bf16[2,384,2048]{1,2,0:T(8,128)(2,1)}, bf16[2,384,2048]{1,2,0:T(8,128)(2,1)}, u32[]{:S(2)}, u32[]{:S(2)}) %collective-permute-start.36) | collective-permute-done | bytes 3145760 | tf_op jit(solution)/shard_map/ppermute | solution.py:628
  671.5 3.6 fusion.4
  677.0 12.7 %collective-permute-done.34 = bf16[2,384,2048]{1,2,0:T(8,128)(2,1)} collective-permute-done((bf16[2,384,2048]{1,2,0:T(8,128)(2,1)}, bf16[2,384,2048]{1,2,0:T(8,128)(2,1)}, u32[]{:S(2)}, u32[]{:S(2)}) %collective-permute-start.34) | collective-permute-done | bytes 3145760 | tf_op jit(solution)/shard_map/ppermute | solution.py:628
  699.7 23.3 %collective-permute-done.37 = bf16[384,2048]{0,1:T(8,128)(2,1)} collective-permute-done((bf16[384,2048]{0,1:T(8,128)(2,1)}, bf16[384,2048]{0,1:T(8,128)(2,1)}, u32[]{:S(2)}, u32[]{:S(2)}) %collective-permute-start.37) | collective-permute-done | bytes 1572896 | tf_op jit(solution)/shard_map/ppermute | solution.py:628
  726.2 5.0 collective-permute-done.35
  735.6 5.9 slice.149
  741.5 9.2 %copy.107 = f32[2,256,2048]{2,0,1:T(2,128)} copy(f32[2,256,2048]{1,0,2:T(2,128)} %slice.149) | data formatting | bytes 8388608 | tf_op jit(solution)/shard_map/slice | solution.py:791
  (339 shorter events, 117.9 us)
Async XLA Ops:
  7.2 15.5 %copy-start = (bf16[3,8,2048]{2,1,0:T(8,128)(2,1)S(1)}, bf16[3,8,2048]{2,1,0:T(8,128)(2,1)}, u32[]{:S(2)}) copy-start(bf16[3,8,2048]{2,1,0:T(8,128)(2,1)} %param.18) | copy-start | bytes 294916
  7.2 110.5 %all-gather.3.cloned.1.call-start = ((), (), s32[]{:S(2)}) async-start(), calls=%async_computation | async-start | bytes 8650752 | tf_op jit(solution)/shard_map/all_gather | solution.py:668
  11.3 551.1 %all-gather.5.cloned.1.call-start = ((), (), s32[]{:S(2)}) async-start(), calls=%async_computation.1 | async-start | bytes 12976128 | tf_op jit(solution)/shard_map/all_gather | solution.py:668
  59.7 54.9 %collective-permute-start = (bf16[512,256]{0,1:T(8,128)(2,1)}, bf16[512,256]{0,1:T(8,128)(2,1)}, u32[]{:S(2)}, u32[]{:S(2)}) collective-permute-start(bf16[512,256]{0,1:T(8,128)(2,1)} %copy.115), channel_id=1, source_target_pairs={{0,1},{1,2},{2,3},{3,0},{4,5},{5,6},{6,7},{7,4},{8,9},{9,10},{10,1... | collective-permute-start | bytes 786440 | tf_op jit(solution)/shard_map/ppermute | solution.py:677
  61.4 53.2 %collective-permute-start.1 = (bf16[512,256]{0,1:T(8,128)(2,1)S(1)}, bf16[512,256]{0,1:T(8,128)(2,1)}, u32[]{:S(2)}, u32[]{:S(2)}) collective-permute-start(bf16[512,256]{0,1:T(8,128)(2,1)S(1)} %copy.116), channel_id=1, source_target_pairs={{0,2},{1,3},{2,0},{3,1},{4,6},{5,7},{6,4},{7,5},{8,10},{9,11},{10,... | collective-permute-start | bytes 786440 | tf_op jit(solution)/shard_map/ppermute | solution.py:677
  62.8 51.8 %collective-permute-start.2 = (bf16[512,256]{0,1:T(8,128)(2,1)S(1)}, bf16[512,256]{0,1:T(8,128)(2,1)S(1)}, u32[]{:S(2)}, u32[]{:S(2)}) collective-permute-start(bf16[512,256]{0,1:T(8,128)(2,1)S(1)} %copy.117), channel_id=1, source_target_pairs={{0,3},{1,0},{2,1},{3,2},{4,7},{5,4},{6,5},{7,6},{8,11},{9,8},{10,9... | collective-permute-start | bytes 786440 | tf_op jit(solution)/shard_map/ppermute | solution.py:677
  70.2 353.5 %copy-start.51 = (bf16[1024,3,8]{0,2,1:T(8,128)(2,1)}, bf16[1024,3,8]{0,2,1:T(8,128)(2,1)S(1)}, u32[]{:S(2)}) copy-start(bf16[1024,3,8]{0,2,1:T(8,128)(2,1)S(1)} %fusion.69) | copy-start | bytes 147460
  77.0 38.4 %copy-start.27 = (bf16[512,256]{0,1:T(8,128)(2,1)}, bf16[512,256]{0,1:T(8,128)(2,1)S(1)}, u32[]{:S(2)}) copy-start(bf16[512,256]{0,1:T(8,128)(2,1)S(1)} %copy.114) | copy-start | bytes 786436
  124.3 190.7 %copy-start.11 = (f32[256,2048]{1,0:T(8,128)}, f32[256,2048]{1,0:T(8,128)S(1)}, u32[]{:S(2)}) copy-start(f32[256,2048]{1,0:T(8,128)S(1)} %get-tuple-element.117) | copy-start | bytes 6291460
  124.3 190.7 %copy-start.56 = (f32[256]{0:T(256)}, f32[256]{0:T(256)S(1)}, u32[]{:S(2)}) copy-start(f32[256]{0:T(256)S(1)} %add_rsqrt_fusion.2) | copy-start | bytes 3076
  323.4 159.9 %collective-permute-start.25 = (bf16[4,256,2048]{2,1,0:T(8,128)(2,1)}, bf16[4,256,2048]{2,1,0:T(8,128)(2,1)}, u32[]{:S(2)}, u32[]{:S(2)}) collective-permute-start(bf16[4,256,2048]{2,1,0:T(8,128)(2,1)} %bitcast.86), channel_id=1, source_target_pairs={{0,4},{4,0},{8,12},{12,8},{16,20},{20,16},{24,28},{28,24},{1,5},{5... | collective-permute-start | bytes 12582920 | tf_op jit(solution)/shard_map/ppermute | solution.py:638
  326.7 24.0 %collective-permute-start.6 = (bf16[512,256]{1,0:T(8,128)(2,1)}, bf16[512,256]{1,0:T(8,128)(2,1)}, u32[]{:S(2)}, u32[]{:S(2)}) collective-permute-start(bf16[512,256]{1,0:T(8,128)(2,1)} %get-tuple-element.101), channel_id=1, source_target_pairs={{0,1},{1,2},{2,3},{3,0},{4,5},{5,6},{6,7},{7,4},{8,9},{9,10},{10,1... | collective-permute-start | bytes 786440 | tf_op jit(solution)/shard_map/ppermute | solution.py:677
  329.3 23.8 %collective-permute-start.7 = (bf16[512,256]{1,0:T(8,128)(2,1)}, bf16[512,256]{1,0:T(8,128)(2,1)}, u32[]{:S(2)}, u32[]{:S(2)}) collective-permute-start(bf16[512,256]{1,0:T(8,128)(2,1)} %get-tuple-element.100), channel_id=1, source_target_pairs={{0,2},{1,3},{2,0},{3,1},{4,6},{5,7},{6,4},{7,5},{8,10},{9,11},{10,... | collective-permute-start | bytes 786440 | tf_op jit(solution)/shard_map/ppermute | solution.py:677
  332.8 46.0 %collective-permute-start.8 = (bf16[512,256]{1,0:T(8,128)(2,1)}, bf16[512,256]{1,0:T(8,128)(2,1)}, u32[]{:S(2)}, u32[]{:S(2)}) collective-permute-start(bf16[512,256]{1,0:T(8,128)(2,1)} %get-tuple-element.99), channel_id=1, source_target_pairs={{0,3},{1,0},{2,1},{3,2},{4,7},{5,4},{6,5},{7,6},{8,11},{9,8},{10,9... | collective-permute-start | bytes 786440 | tf_op jit(solution)/shard_map/ppermute | solution.py:677
  345.2 132.5 %collective-permute-start.3 = (bf16[256,2048]{1,0:T(8,128)(2,1)}, bf16[256,2048]{1,0:T(8,128)(2,1)}, u32[]{:S(2)}, u32[]{:S(2)}) collective-permute-start(bf16[256,2048]{1,0:T(8,128)(2,1)} %constant_dynamic-slice_fusion.40), channel_id=1, source_target_pairs={{0,1},{1,2},{2,3},{3,0},{4,5},{5,6},{6,7},{7,4},{8,9},{9,10},{10,1... | collective-permute-start | bytes 3145736 | tf_op jit(solution)/shard_map/ppermute | solution.py:608
  426.9 6.5 collective-permute-start.22
  432.1 47.4 %collective-permute-start.17 = (bf16[4,256,768]{2,1,0:T(8,128)(2,1)}, bf16[4,256,768]{2,1,0:T(8,128)(2,1)}, u32[]{:S(2)}, u32[]{:S(2)}) collective-permute-start(bf16[4,256,768]{2,1,0:T(8,128)(2,1)} %bitcast.60), channel_id=1, source_target_pairs={{0,4},{4,0},{8,12},{12,8},{16,20},{20,16},{24,28},{28,24},{1,5},{5... | collective-permute-start | bytes 4718600 | tf_op jit(solution)/shard_map/ppermute | solution.py:638
  433.2 12.6 %collective-permute-start.9 = (bf16[768,256]{0,1:T(8,128)(2,1)}, bf16[768,256]{0,1:T(8,128)(2,1)}, u32[]{:S(2)}, u32[]{:S(2)}) collective-permute-start(bf16[768,256]{0,1:T(8,128)(2,1)} %copy.118), channel_id=1, source_target_pairs={{0,1},{1,2},{2,3},{3,0},{4,5},{5,6},{6,7},{7,4},{8,9},{9,10},{10,1... | collective-permute-start | bytes 1179656 | tf_op jit(solution)/shard_map/ppermute | solution.py:677
  434.4 6.1 collective-permute-start.23
  440.6 5.1 collective-permute-start.24
  445.8 26.4 %collective-permute-start.10 = (bf16[768,256]{0,1:T(8,128)(2,1)}, bf16[768,256]{0,1:T(8,128)(2,1)S(1)}, u32[]{:S(2)}, u32[]{:S(2)}) collective-permute-start(bf16[768,256]{0,1:T(8,128)(2,1)} %copy.119), channel_id=1, source_target_pairs={{0,2},{1,3},{2,0},{3,1},{4,6},{5,7},{6,4},{7,5},{8,10},{9,11},{10,... | collective-permute-start | bytes 1179656 | tf_op jit(solution)/shard_map/ppermute | solution.py:677
  445.9 29.3 %collective-permute-start.11 = (bf16[768,256]{0,1:T(8,128)(2,1)S(1)}, bf16[768,256]{0,1:T(8,128)(2,1)S(1)}, u32[]{:S(2)}, u32[]{:S(2)}) collective-permute-start(bf16[768,256]{0,1:T(8,128)(2,1)S(1)} %copy.120), channel_id=1, source_target_pairs={{0,3},{1,0},{2,1},{3,2},{4,7},{5,4},{6,5},{7,6},{8,11},{9,8},{10,9... | collective-permute-start | bytes 1179656 | tf_op jit(solution)/shard_map/ppermute | solution.py:677
  472.1 114.5 %collective-permute-start.33 = (bf16[4,768,2048]{2,1,0:T(8,128)(2,1)}, bf16[4,768,2048]{2,1,0:T(8,128)(2,1)}, u32[]{:S(2)}, u32[]{:S(2)}) collective-permute-start(bf16[4,768,2048]{2,1,0:T(8,128)(2,1)} %slice.145), channel_id=1, source_target_pairs={{0,4},{4,0},{8,12},{12,8},{16,20},{20,16},{24,28},{28,24},{1,5},{5... | collective-permute-start | bytes 37748744 | tf_op jit(solution)/shard_map/ppermute | solution.py:638
  479.4 25.2 %collective-permute-start.4 = (bf16[256,2048]{1,0:T(8,128)(2,1)S(1)}, bf16[256,2048]{1,0:T(8,128)(2,1)S(1)}, u32[]{:S(2)}, u32[]{:S(2)}) collective-permute-start(bf16[256,2048]{1,0:T(8,128)(2,1)S(1)} %add_convert_fusion.3), channel_id=1, source_target_pairs={{0,1},{1,2},{2,3},{3,0},{4,5},{5,6},{6,7},{7,4},{8,9},{9,10},{10,1... | collective-permute-start | bytes 3145736 | tf_op jit(solution)/shard_map/ppermute | solution.py:608
  481.5 24.8 %collective-permute-start.18 = (bf16[2,128,768]{2,1,0:T(8,128)(2,1)S(1)}, bf16[2,128,768]{2,1,0:T(8,128)(2,1)S(1)}, u32[]{:S(2)}, u32[]{:S(2)}) collective-permute-start(bf16[2,128,768]{2,1,0:T(8,128)(2,1)S(1)} %dynamic-slice_bitcast_fusion.7), channel_id=1, source_target_pairs={{0,8},{4,12},{8,0},{12,4},{16,24},{20,28},{24,16},{28,20},{1,9},{5... | collective-permute-start | bytes 1179656 | tf_op jit(solution)/shard_map/ppermute | solution.py:628
  482.1 51.3 %collective-permute-start.20 = (bf16[2,128,768]{2,1,0:T(8,128)(2,1)S(1)}, bf16[2,128,768]{2,1,0:T(8,128)(2,1)S(1)}, u32[]{:S(2)}, u32[]{:S(2)}) collective-permute-start(bf16[2,128,768]{2,1,0:T(8,128)(2,1)S(1)} %dynamic-slice_bitcast_fusion.6), channel_id=1, source_target_pairs={{0,16},{4,20},{8,24},{12,28},{16,0},{20,4},{24,8},{28,12},{1,17},{... | collective-permute-start | bytes 1179656 | tf_op jit(solution)/shard_map/ppermute | solution.py:628
  488.0 27.1 %collective-permute-start.26 = (bf16[2,128,2048]{2,1,0:T(8,128)(2,1)S(1)}, bf16[2,128,2048]{2,1,0:T(8,128)(2,1)S(1)}, u32[]{:S(2)}, u32[]{:S(2)}) collective-permute-start(bf16[2,128,2048]{2,1,0:T(8,128)(2,1)S(1)} %dynamic-slice_bitcast_fusion.3), channel_id=1, source_target_pairs={{0,8},{4,12},{8,0},{12,4},{16,24},{20,28},{24,16},{28,20},{1,9},{5... | collective-permute-start | bytes 3145736 | tf_op jit(solution)/shard_map/ppermute | solution.py:628
  506.0 119.6 %collective-permute-start.5 = (bf16[256,2048]{1,0:T(8,128)(2,1)}, bf16[256,2048]{1,0:T(8,128)(2,1)}, u32[]{:S(2)}, u32[]{:S(2)}) collective-permute-start(bf16[256,2048]{1,0:T(8,128)(2,1)} %add_convert_fusion.2), channel_id=1, source_target_pairs={{0,1},{1,2},{2,3},{3,0},{4,5},{5,6},{6,7},{7,4},{8,9},{9,10},{10,1... | collective-permute-start | bytes 3145736 | tf_op jit(solution)/shard_map/ppermute | solution.py:608
  506.3 26.2 %collective-permute-start.28 = (bf16[2,128,2048]{2,1,0:T(8,128)(2,1)S(1)}, bf16[2,128,2048]{2,1,0:T(8,128)(2,1)S(1)}, u32[]{:S(2)}, u32[]{:S(2)}) collective-permute-start(bf16[2,128,2048]{2,1,0:T(8,128)(2,1)S(1)} %dynamic-slice_bitcast_fusion.2), channel_id=1, source_target_pairs={{0,16},{4,20},{8,24},{12,28},{16,0},{20,4},{24,8},{28,12},{1,17},{... | collective-permute-start | bytes 3145736 | tf_op jit(solution)/shard_map/ppermute | solution.py:628
  515.1 33.2 %collective-permute-start.19 = (bf16[128,768]{1,0:T(8,128)(2,1)S(1)}, bf16[128,768]{1,0:T(8,128)(2,1)S(1)}, u32[]{:S(2)}, u32[]{:S(2)}) collective-permute-start(bf16[128,768]{1,0:T(8,128)(2,1)S(1)} %dynamic-slice_bitcast_fusion.12), channel_id=1, source_target_pairs={{0,16},{4,20},{8,24},{12,28},{16,0},{20,4},{24,8},{28,12},{1,17},{... | collective-permute-start | bytes 589832 | tf_op jit(solution)/shard_map/ppermute | solution.py:628
  532.5 13.7 %collective-permute-start.27 = (bf16[128,2048]{1,0:T(8,128)(2,1)S(1)}, bf16[128,2048]{1,0:T(8,128)(2,1)S(1)}, u32[]{:S(2)}, u32[]{:S(2)}) collective-permute-start(bf16[128,2048]{1,0:T(8,128)(2,1)S(1)} %dynamic-slice_bitcast_fusion.5), channel_id=1, source_target_pairs={{0,16},{4,20},{8,24},{12,28},{16,0},{20,4},{24,8},{28,12},{1,17},{... | collective-permute-start | bytes 1572872 | tf_op jit(solution)/shard_map/ppermute | solution.py:628
  533.4 12.9 %collective-permute-start.29 = (bf16[128,2048]{1,0:T(8,128)(2,1)S(1)}, bf16[128,2048]{1,0:T(8,128)(2,1)S(1)}, u32[]{:S(2)}, u32[]{:S(2)}) collective-permute-start(bf16[128,2048]{1,0:T(8,128)(2,1)S(1)} %dynamic-slice_bitcast_fusion.4), channel_id=1, source_target_pairs={{0,8},{4,12},{8,0},{12,4},{16,24},{20,28},{24,16},{28,20},{1,9},{5... | collective-permute-start | bytes 1572872 | tf_op jit(solution)/shard_map/ppermute | solution.py:628
  546.5 6.6 collective-permute-start.30
  547.7 6.9 collective-permute-start.21
  553.2 7.5 collective-permute-start.31
  561.8 15.1 %collective-permute-start.32 = (bf16[256,512]{1,0:T(8,128)(2,1)S(1)}, bf16[256,512]{1,0:T(8,128)(2,1)}, u32[]{:S(2)}, u32[]{:S(2)}) collective-permute-start(bf16[256,512]{1,0:T(8,128)(2,1)S(1)} %fusion.84), channel_id=1, source_target_pairs={{0,1},{1,2},{2,3},{3,0},{4,5},{5,6},{6,7},{7,4},{8,9},{9,10},{10,1... | collective-permute-start | bytes 786440 | tf_op jit(solution)/shard_map/ppermute | solution.py:608
  576.4 5.6 collective-permute-start.12
  582.1 4.6 collective-permute-start.13
  606.6 64.9 %collective-permute-start.36 = (bf16[2,384,2048]{1,2,0:T(8,128)(2,1)}, bf16[2,384,2048]{1,2,0:T(8,128)(2,1)}, u32[]{:S(2)}, u32[]{:S(2)}) collective-permute-start(bf16[2,384,2048]{1,2,0:T(8,128)(2,1)} %bitcast.268), channel_id=1, source_target_pairs={{0,16},{4,20},{8,24},{12,28},{16,0},{20,4},{24,8},{28,12},{1,17},{... | collective-permute-start | bytes 9437192 | tf_op jit(solution)/shard_map/ppermute | solution.py:628
  607.1 12.5 %collective-permute-start.14 = (f32[1,4,2688]{2,1,0:T(4,128)S(1)}, f32[1,4,2688]{2,1,0:T(4,128)S(1)}, u32[]{:S(2)}, u32[]{:S(2)}) collective-permute-start(f32[1,4,2688]{2,1,0:T(4,128)S(1)} %constant_dynamic-slice_fusion.25), channel_id=1, source_target_pairs={{0,4},{4,0},{8,12},{12,8},{16,20},{20,16},{24,28},{28,24},{1,5},{5... | collective-permute-start | bytes 129032 | tf_op jit(solution)/shard_map/ppermute | solution.py:652
  613.7 11.9 %copy-start.59 = (f32[256]{0:T(256)S(1)}, f32[256]{0:T(256)}, u32[]{:S(2)}) copy-start(f32[256]{0:T(256)} %copy-done.58) | copy-start | bytes 3076
  613.7 11.9 %copy-start.61 = (f32[256]{0:T(256)S(1)}, f32[256]{0:T(256)}, u32[]{:S(2)}) copy-start(f32[256]{0:T(256)} %add_rsqrt_fusion.1) | copy-start | bytes 3076
  618.5 71.2 %collective-permute-start.34 = (bf16[2,384,2048]{1,2,0:T(8,128)(2,1)}, bf16[2,384,2048]{1,2,0:T(8,128)(2,1)}, u32[]{:S(2)}, u32[]{:S(2)}) collective-permute-start(bf16[2,384,2048]{1,2,0:T(8,128)(2,1)} %bitcast.269), channel_id=1, source_target_pairs={{0,8},{4,12},{8,0},{12,4},{16,24},{20,28},{24,16},{28,20},{1,9},{5... | collective-permute-start | bytes 9437192 | tf_op jit(solution)/shard_map/ppermute | solution.py:628
  619.7 11.4 %collective-permute-start.15 = (f32[2,2688]{1,0:T(2,128)S(1)}, f32[2,2688]{1,0:T(2,128)S(1)}, u32[]{:S(2)}, u32[]{:S(2)}) collective-permute-start(f32[2,2688]{1,0:T(2,128)S(1)} %fusion.116), channel_id=1, source_target_pairs={{0,2},{1,3},{2,0},{3,1},{4,6},{5,7},{6,4},{7,5},{8,10},{9,11},{10,... | collective-permute-start | bytes 64520 | tf_op jit(solution)/shard_map/ppermute | solution.py:659
  631.2 65.8 %collective-permute-start.16 = (f32[1,2688]{1,0:T(1,128)S(1)}, f32[1,2688]{1,0:T(1,128)S(1)}, u32[]{:S(2)}, u32[]{:S(2)}) collective-permute-start(f32[1,2688]{1,0:T(1,128)S(1)} %constant_dynamic-slice_fusion.21), channel_id=1, source_target_pairs={{0,1},{1,0},{2,3},{3,2},{4,5},{5,4},{6,7},{7,6},{8,9},{9,8},{10,11... | collective-permute-start | bytes 32264 | tf_op jit(solution)/shard_map/ppermute | solution.py:659
  675.2 14.5 %copy-start.15 = (bf16[2,1,384,2048]{2,3,0,1:T(8,128)(2,1)S(1)}, bf16[2,1,384,2048]{2,3,0,1:T(8,128)(2,1)}, u32[]{:S(2)}) copy-start(bf16[2,1,384,2048]{2,3,0,1:T(8,128)(2,1)} %copy.122) | copy-start | bytes 9437188
  676.5 46.5 %collective-permute-start.37 = (bf16[384,2048]{0,1:T(8,128)(2,1)}, bf16[384,2048]{0,1:T(8,128)(2,1)}, u32[]{:S(2)}, u32[]{:S(2)}) collective-permute-start(bf16[384,2048]{0,1:T(8,128)(2,1)} %dynamic-slice_bitcast_fusion), channel_id=1, source_target_pairs={{0,8},{4,12},{8,0},{12,4},{16,24},{20,28},{24,16},{28,20},{1,9},{5... | collective-permute-start | bytes 4718600 | tf_op jit(solution)/shard_map/ppermute | solution.py:628
  695.3 35.9 %collective-permute-start.35 = (bf16[384,2048]{0,1:T(8,128)(2,1)}, bf16[384,2048]{0,1:T(8,128)(2,1)}, u32[]{:S(2)}, u32[]{:S(2)}) collective-permute-start(bf16[384,2048]{0,1:T(8,128)(2,1)} %dynamic-slice_bitcast_fusion.1), channel_id=1, source_target_pairs={{0,16},{4,20},{8,24},{12,28},{16,0},{20,4},{24,8},{28,12},{1,17},{... | collective-permute-start | bytes 4718600 | tf_op jit(solution)/shard_map/ppermute | solution.py:628
  (57 other events, 270.6 us)
Sparse Core Ops, SparseCore 0:
  11.5 94.1 all-gather.2
  108.5 133.7 all-gather.4

commit v3 on v2

--- a/solution.py
+++ b/solution.py
@@ -131,6 +131,7 @@
         out_specs=(mine((width, length)), mine((qw, length)), mine((heads, 1, length))),
         scratch_shapes=[pltpu.VMEM((length, HEAD_SIZE), BF16), pltpu.VMEM((length, 2 * HEAD_SIZE), BF16)],
         compiler_params=pltpu.CompilerParams(vmem_limit_bytes=48 * 2**20),
+        cost_estimate=pl.CostEstimate(flops=22 * 10**9, bytes_accessed=10**7, transcendentals=10**6),
         name="attention_forward",
     )(joined_t, cosines, sines, maps_t, seg_row, seg_col)
 
@@ -227,6 +228,7 @@
             pltpu.VMEM((length, HEAD_SIZE), F32), pltpu.VMEM((length, 2 * HEAD_SIZE), F32),
             pltpu.VMEM((length, HEAD_SIZE), F32)],
         compiler_params=pltpu.CompilerParams(vmem_limit_bytes=48 * 2**20),
+        cost_estimate=pl.CostEstimate(flops=40 * 10**9, bytes_accessed=10**7, transcendentals=10**6),
         name="attention_backward",
     )(low, cosines, sines, maps_t, maps, seg_row, seg_col, att, root, gatt)
 
@@ -247,9 +249,9 @@
 def feed_kernel(
     n, dp, tile, cut,
     normed_in, cot_in, gate_up_in, down_in,
-    sum_out, mixed_out, grads_out,
+    sum_out, mixed_out, came, first_send, first_keep, second_send, second_keep,
     gate_up, down, normed, cots, acts, grads, arriving, sending, mixed, turned,
-    load_sems, weight_sems, out_sems, gather_send, gather_recv, sum_send, sum_recv, mixed_sems,
+    load_sems, weight_sems, out_sems, core_send, core_recv, fill_sems, gather_send, gather_recv, sum_send, sum_recv, mixed_sems,
 ):
     share, width = normed_in.shape
     hidden = down_in.shape[0]
@@ -257,7 +259,9 @@
     piece = share // cut
     per = hidden // tile
     me = lax.axis_index("tensor")
-    core = lax.rem(lax.axis_index("dp"), 2)
+    mine = lax.axis_index("dp")
+    core = lax.rem(mine, 2)
+    mate = {"dp": mine + 1 - 2 * core}
     place = (me, n - 1 - me)
     ends = (me < n - 1, me > 0)
     partner = (me + 1, me - 1)
@@ -275,6 +279,7 @@
         def _(way=way):
             pl.semaphore_signal(barrier, inc=1, device_id=device(way), device_id_type=pl.DeviceIdType.MESH)
 
+    pl.semaphore_signal(barrier, inc=1, device_id=mate, device_id_type=pl.DeviceIdType.MESH)
     own_load = pltpu.make_async_copy(normed_in, normed.at[rows_of(me)], load_sems.at[0])
     cot_load = pltpu.make_async_copy(cot_in, cots, load_sems.at[1])
     own_load.start()
@@ -298,11 +303,11 @@
 
     @pl.when(inner)
     def _():
-        pl.semaphore_wait(barrier, 2)
+        pl.semaphore_wait(barrier, 3)
 
     @pl.when(jnp.logical_not(inner))
     def _():
-        pl.semaphore_wait(barrier, 1)
+        pl.semaphore_wait(barrier, 2)
 
     def gather(way, j):
         return pltpu.make_async_remote_copy(
@@ -420,10 +425,38 @@
     half = dp // 4
     items = dp // 2 * 2 * per
 
-    def put(pair, j):
-        start = pl.multiple_of((lax.rem(pair, 2) * 2 + j) * room, 16)
-        return pltpu.make_async_copy(
-            gate_up.at[pl.ds(start, room)], grads_out.at[2 * pair + j], out_sems.at[lax.rem(pair, 2), j])
+    def staged(pair, j, start=0, size=room):
+        first = pl.multiple_of((lax.rem(pair, 2) * 2 + j) * room + start, 16)
+        return gate_up.at[pl.ds(first, size)]
+
+    def put_across(pair, j):
+        return pltpu.make_async_remote_copy(
+            src_ref=staged(pair, j), dst_ref=came.at[2 * pair + j],
+            send_sem=core_send.at[pair, j], recv_sem=core_recv.at[pair, j],
+            device_id=mate, device_id_type=pl.DeviceIdType.MESH)
+
+    def fill(pair, j):
+        return pltpu.make_async_copy(came.at[2 * (pair - half) + j], staged(pair, j), fill_sems.at[j])
+
+    def put_own(pair, j, act):
+        q = 2 * (pair - half) + j
+        quarter = dp // 4
+        rows = room // 2
+        place = lax.div(mine, 2)
+        for part, (other, keep, slot, goes) in enumerate((
+            (first_send, first_keep, lax.div(q, 2), lax.rem(q, 2) != lax.rem(place, 2)),
+            (second_send, second_keep, lax.rem(q, quarter), lax.div(q, quarter) != lax.div(place, quarter)),
+        )):
+            for ref, chosen in ((other, goes), (keep, jnp.logical_not(goes))):
+
+                @pl.when(chosen)
+                def _(ref=ref, part=part, slot=slot):
+                    copy = pltpu.make_async_copy(
+                        staged(pair, j, part * rows, rows), ref.at[slot], out_sems.at[lax.rem(pair, 2), j, part])
+                    if act == "start":
+                        copy.start()
+                    else:
+                        copy.wait()
 
     def weight_item(i):
         pair, f = lax.div(i, 2 * per), lax.rem(i, 2 * per)
@@ -439,37 +472,75 @@
         def store(row, goal, product):
             for j in range(2):
                 start = pl.multiple_of((slot * 2 + j) * room + row * block, 16)
-                gate_up[pl.ds(start, block), goal] = product[j * block:(j + 1) * block]
+                rows = pl.ds(start, block)
+                part = product[j * block:(j + 1) * block]
+
+                @pl.when(pair < half)
+                def _(rows=rows, part=part):
+                    gate_up[rows, goal] = part.astype(BF16)
+
+                @pl.when(pair >= half)
+                def _(rows=rows, part=part):
+                    gate_up[rows, goal] = (gate_up[rows, goal].astype(F32) + part).astype(BF16)
 
         @pl.when(f == 0)
         def _():
-            @pl.when(pair >= 2)
+            @pl.when((pair >= 2) & (pair < half))
             def _():
                 for j in range(2):
-                    put(pair - 2, j).wait()
+                    put_across(pair - 2, j).wait_send()
+
+            @pl.when(pair >= half)
+            def _():
+                for j in range(2):
+                    fill(pair, j).wait()
 
             turn(normed)
 
         @pl.when(f == per)
         def _():
             turn(cots)
+            following = pair + 1
+
+            @pl.when((following >= half) & (following < 2 * half))
+            def _():
+                @pl.when(following - 2 < half)
+                def _():
+                    for j in range(2):
+                        put_across(following - 2, j).wait_send()
+
+                @pl.when(following - 2 >= half)
+                def _():
+                    for j in range(2):
+                        put_own(following - 2, j, "wait")
+
+                for j in range(2):
+                    put_across(following - half, j).wait_recv()
+                    fill(following, j).start()
 
         @pl.when(f < per)
         def _():
             goal = pl.ds(pl.multiple_of(f * tile, tile), tile)
             for row in range(2):
                 span = pl.ds(pl.multiple_of(row * hidden + f * tile, tile), tile)
-                store(row, goal, nn(turned[...], grads[:, span]).astype(BF16))
+                store(row, goal, nn(turned[...], grads[:, span]))
 
         @pl.when(f >= per)
         def _():
             goal = pl.ds(pl.multiple_of((f - per) * tile, tile), tile)
-            store(2, goal, nn(turned[...], acts[:, goal]).astype(BF16))
+            store(2, goal, nn(turned[...], acts[:, goal]))
 
         @pl.when(f == 2 * per - 1)
         def _():
-            for j in range(2):
-                put(pair, j).start()
+            @pl.when(pair < half)
+            def _():
+                for j in range(2):
+                    put_across(pair, j).start()
+
+            @pl.when(pair >= half)
+            def _():
+                for j in range(2):
+                    put_own(pair, j, "start")
 
     first_step, last_step = cut + 1, cut * (n - 1) + n - 2
     every = -(-items // (last_step - first_step))
@@ -519,9 +590,9 @@
 
     final = pltpu.make_async_copy(sending.at[rows_of(me)], sum_out, load_sems.at[0])
     final.start()
-    for pair in (dp // 2 - 2, dp // 2 - 1):
+    for pair in (2 * half - 2, 2 * half - 1):
         for j in range(2):
-            put(pair, j).wait()
+            put_own(pair, j, "wait")
     put_mixed(n - 1).wait()
     final.wait()
     for way in range(2):
@@ -530,13 +601,13 @@
         def _(way=way):
             @pl.loop(0, n)
             def _(j):
-                mine = (j <= me) if way == 0 else (j >= me)
-
-                @pl.when(mine)
+                sent = (j <= me) if way == 0 else (j >= me)
+
+                @pl.when(sent)
                 def _():
                     gather(way, j).wait_send()
 
-                @pl.when(jnp.logical_not(mine))
+                @pl.when(jnp.logical_not(sent))
                 def _():
                     for q in range(cut):
                         pass_on(way, j, q).wait_send()
@@ -553,10 +624,14 @@
         out_shape=(
             jax.ShapeDtypeStruct((share, width), BF16),
             jax.ShapeDtypeStruct((tokens, width), BF16),
-            jax.ShapeDtypeStruct((dp, 3 * block, hidden), BF16),
+            jax.ShapeDtypeStruct((dp // 2, 3 * block, hidden), BF16),
+            jax.ShapeDtypeStruct((dp // 4, 3 * block // 2, hidden), BF16),
+            jax.ShapeDtypeStruct((dp // 4, 3 * block // 2, hidden), BF16),
+            jax.ShapeDtypeStruct((dp // 4, 3 * block // 2, hidden), BF16),
+            jax.ShapeDtypeStruct((dp // 4, 3 * block // 2, hidden), BF16),
         ),
         in_specs=[anywhere] * 4,
-        out_specs=(anywhere,) * 3,
+        out_specs=(anywhere,) * 7,
         scratch_shapes=[
             pltpu.VMEM((2 * width, hidden), BF16),
             pltpu.VMEM((hidden, width), BF16),
@@ -570,7 +645,10 @@
             pltpu.VMEM((2 * block, tokens), BF16),
             pltpu.SemaphoreType.DMA((2,)),
             pltpu.SemaphoreType.DMA((3, hidden // tile)),
-            pltpu.SemaphoreType.DMA((2, 2)),
+            pltpu.SemaphoreType.DMA((2, 2, 2)),
+            pltpu.SemaphoreType.DMA((dp // 4, 2)),
+            pltpu.SemaphoreType.DMA((dp // 4, 2)),
+            pltpu.SemaphoreType.DMA((2,)),
             pltpu.SemaphoreType.DMA((2, n)),
             pltpu.SemaphoreType.DMA((2, n)),
             pltpu.SemaphoreType.DMA((2, n * cut)),
@@ -633,15 +711,27 @@
     return current
 
 
+def scatter_rest(first_send, first_keep, second_send, second_keep):
+    size = lax.axis_size("dp")
+    rest = list(range(1, bits_of(size)))
+    halves = []
+    for send, keep, order in ((first_send, first_keep, rest), (second_send, second_keep, rest[::-1])):
+        arrived = lax.ppermute(send, "dp", flip(size, order[0]))
+        current = keep.astype(F32) + arrived.astype(F32)
+        halves.append(halve(current.astype(BF16), 0, order[1:]) if order[1:] else current[0])
+    return jnp.concatenate(halves, axis=0)
+
+
 def scatter_dp(other, own):
     size = lax.axis_size("dp")
     arrived = lax.ppermute(other.astype(BF16), "dp", flip(size, 0))
-    current = (own.astype(F32) + arrived.astype(F32)).astype(BF16)
+    current = own.astype(F32) + arrived.astype(F32)
     rest = list(range(1, bits_of(size)))
     half = current.shape[1] // 2
-    first = halve(current[:, :half], 0, rest)
-    second = halve(current[:, half:], 0, rest[::-1])
-    return jnp.concatenate([first, second], axis=0)
+    parts = []
+    for part, order in ((current[:, :half], rest), (current[:, half:], rest[::-1])):
+        parts.append(halve(part.astype(BF16), 0, order))
+    return jnp.concatenate(parts, axis=0)
 
 
 def scatter_small(blocks, over_tensor):
@@ -726,7 +816,6 @@
     w_branch = (w_out.astype(F32) + dot("rc,rd->cd", down_flat, o_up)).astype(BF16)
     down_all = lax.all_gather(down_flat, "tensor")
     all_branch = gather_weight(w_branch)
-    all_joined = gather_weight(w_joined)
 
     _, _, normed_one = normalize(tokens.astype(F32), gains[0])
     lowrank = dot("td,jrd->tjr", normed_one, qkv_down)
@@ -746,7 +835,7 @@
     hidden = tokens_share + dot("nct,ncd->td", att_share, all_branch)
     scaled_two, inverse_two, normed_two = normalize(hidden, gains[1])
 
-    grad_normed_two, mixed_parts, grads_feed = feed_forward(
+    grad_normed_two, mixed_parts, _, *grads_feed = feed_forward(
         normed_two, cotangent, jnp.transpose(w_gate_up, (1, 0, 2)), w_down, n, dp
     )
     grad_normed_two = grad_normed_two.astype(F32)
@@ -767,8 +856,9 @@
         low, cosines, sines, maps_t, maps, seg_row, seg_col, attended, root, grad_attended, heads
     )
     flat_joined = grad_joined.reshape(groups * joined_width, token_rows)
-    joined_share = jnp.stack(by_place(exchange(lambda j: chunk_of(flat_joined, j, share, 1), 1)))
-    grad_normed_one = dot("nct,ncd->td", joined_share, all_joined)
+    grad_normed_one = ring_sum(
+        [dot("ct,cd->td", chunk_of(flat_joined, (me + n - s) % n, share, 1), w_joined) for s in range(n)]
+    )
     scaled_one, inverse_one, _ = normalize(tokens_share, gains[0])
     weighted = grad_normed_one * gains[0]
     grad_input = (
@@ -787,7 +877,7 @@
     def blocks_of(product):
         return product.astype(BF16).reshape(dp // 2, width, -1)
 
-    out_feed = scatter_dp(grads_feed[:dp // 2], grads_feed[dp // 2:]).reshape(3, width, -1)
+    out_feed = scatter_rest(*grads_feed).reshape(3, width, -1)
     out_gate_up = jnp.transpose(out_feed[:2], (1, 0, 2))
     out_down = out_feed[2].T
     flat_att = jnp.concatenate(att_came, axis=0)

time: 773 us -> 657 us (0.85)
  local copies, waits for them, and re-layouts: 125 us -> 70.2 us
  Pallas kernels: 245 us -> 209 us
  waiting for transfers between devices: 196 us -> 176 us
    ppermute x6 -> x9, waiting for transfers between devices: 25.3 us -> 87.7 us  [ring_sum(): arrived = lax.ppermute(running, 'tensor', ring(size)).astype(F32)]
    ppermute x12 -> x10, waiting for transfers between devices: 110 us -> 58.7 us  [halve(): arrived = lax.ppermute(pick(current, 1 - own, where), 'dp', flip(size, bit))]
    pallas_call x1, Pallas kernels: 177 us -> 142 us  [feed_forward(): pl.pallas_call(partial(feed_kernel, n, dp, tile, cut), out_shape=(jax.Sha...]
    ppermute x9 -> x6, waiting for transfers between devices: 53.9 us -> 24.1 us  [exchange(): came.append(lax.ppermute(parts((me + s) % n), 'tensor', ring(n, s)))]
    dynamic_slice x8 -> x3, local copies, waits for them, and re-layouts: 19.9 us -> 3.11 us  [pick(): return lax.dynamic_index_in_dim(array, index, axis, keepdims=False)]
    slice x4 -> x2, local copies, waits for them, and re-layouts: 15.3 us -> 0.53 us  [scatter_dp(): current[:, :half]]
    unnamed x153 -> x171, local copies, waits for them, and re-layouts: 46.1 us -> 34.7 us
    slice x2 -> x1, local copies, waits for them, and re-layouts: 15.1 us -> 5.25 us  [local(): out_gate_up = jnp.transpose(out_feed[:2], (1, 0, 2))]
  transfers between devices with their start and end apart: 40 -> 38, of which waited for: 16 -> 16; matrix products, arithmetic and copies ran while one was open for 28% -> 24% of each run, Pallas kernels for 32% -> 10%
where the time goes in v3:
time: 657 us; the launch traced here: 644 us
  Pallas kernels  209 us (32%)
  waiting for transfers between devices  176 us (27%)
  local copies, waits for them, and re-layouts  70.2 us (11%)
  matrix products  63.5 us (10%)
  other arithmetic  53.2 us (8%)
  starting transfers between devices  34 us (5%)
  blocking collectives  23.1 us (4%)
  between operations  15.7 us (2%)
    pallas_call x1, Pallas kernels, feed_forward(): pl.pallas_call(partial(feed_kernel, n, dp, tile, cut), out_shape=(jax.Sha...  142 us
    ppermute x9, waiting for transfers between devices, ring_sum(): arrived = lax.ppermute(running, 'tensor', ring(size)).astype(F32)  87.7 us
    ppermute x10, waiting for transfers between devices, halve(): arrived = lax.ppermute(pick(current, 1 - own, where), 'dp', flip(size, bit))  58.7 us
    pallas_call x1, Pallas kernels, attention_backward(): pl.pallas_call(partial(backward_kernel, heads, block), grid=(groups,), ou...  41.6 us
    unnamed x171, local copies, waits for them, and re-layouts  34.7 us
    pallas_call x1, Pallas kernels, attention_forward(): pl.pallas_call(partial(forward_kernel, heads, block), grid=(groups,), out...  25.8 us
    ppermute x6, waiting for transfers between devices, exchange(): came.append(lax.ppermute(parts((me + s) % n), 'tensor', ring(n, s)))  24.1 us
    all_gather x1, blocking collectives, local(): down_all = lax.all_gather(down_flat, 'tensor')  23.1 us
  transfers between devices with their start and end apart: 38, of which 16 were waited for; matrix products, arithmetic and copies ran while one was open for 24% of the time, Pallas kernels for 10%

profile of v3, /device:TPU:12, one launch (start us, length us, event | category | flops | bytes accessed | tf_op | source)
XLA Modules:
  0.0 644.3 jit_solution(8011646772053722376)
XLA Ops:
  11.5 6.7 %copy.64 = bf16[2048,2,384]{0,2,1:T(8,128)(2,1)} copy(bf16[2048,2,384]{2,1,0:T(2,128)(2,1)S(1)} %copy-done.33) | data formatting | bytes 6291456 | tf_op args[4]
  18.7 3.3 fusion
  26.6 5.1 fusion.9.joined_ref
  31.7 25.8 %attention_forward.1 = (bf16[2,384,1024]{2,1,0:T(8,128)(2,1)S(1)}, bf16[2,256,1024]{2,1,0:T(8,128)(2,1)S(1)}, f32[2,4,1,1024]{3,2,1,0:T(1,128)S(1)}) custom-call(f32[2,384,1024]{2,1,0:T(8,128)} %fusion.9.joined_ref, f32[32,1024]{1,0:T(8,128)S(1)} %get-tuple-element.119.cos_ref, f32[32,1024]{1,0:T(8,128)S(1)} %get-tuple-element.118.sin_ref, ...), custom_call_target="tpu_custom_call" | custom-call | flops 22000001024 | bytes 10000000 | tf_op jit(solution)/shard_map/attention_forward/pallas_call | solution.py:121
  62.2 2.1 collective-permute-start.2
  66.6 4.1 fusion.60
  70.8 2.1 constant_dynamic-slice_fusion.12
  73.1 17.6 %copy.106 = bf16[2048,2,2048]{2,0,1:T(8,128)(2,1)} copy(bf16[2048,2,2048]{2,1,0:T(2,128)(2,1)} %param.24) | data formatting | bytes 33554432 | tf_op args[11]
  90.6 23.1 %all_gather.7 = bf16[4,8,512]{2,1,0:T(8,128)(2,1)} all-gather(bf16[1,8,512]{2,1,0:T(8,128)(2,1)S(1)} %all_gather_reshape.3), channel_id=1, replica_groups=mesh['dp'=8,'tensor'=4] {'tensor'}, dimensions={0}, use_global_device_ids=true | all-gather | bytes 40960 | tf_op jit(solution)/shard_map/all_gather | solution.py:817
  116.0 6.3 multiply_reduce_fusion
  123.7 141.6 %feed_forward.1 = (bf16[256,2048]{1,0:T(8,128)(2,1)}, bf16[1024,2048]{1,0:T(8,128)(2,1)}, bf16[4,768,2048]{2,1,0:T(8,128)(2,1)}, bf16[2,384,2048]{2,1,0:T(8,128)...) custom-call(bf16[256,2048]{1,0:T(8,128)(2,1)} %multiply_convert_fusion.normed_in,, ...), custom_call_target="tpu_custom_call" | custom-call | flops 77309411328 | bytes 50331648 | tf_op jit(solution)/shard_map/feed_forward/pallas_call | solution.py:622
  265.3 2.1 fusion.20
  270.7 6.8 %convolution_convert_fusion.3 = bf16[4,512,256]{2,1,0:T(8,128)(2,1)} fusion(bf16[4,512,2048]{2,1,0:T(8,128)(2,1)} %bitcast.284, bf16[256,2048]{1,0:T(8,128)(2,1)S(1)} %fusion.126), kind=kOutput, calls=%fused_computation.90 | convolution fusion | flops 2148007936 | bytes 10485760 | tf_op jit(solution)/shard_map/ncd,td->nct/dot_general | solution.py:849
  277.5 2.1 convolution_bitcast_fusion.1
  281.6 2.1 constant_dynamic-slice_fusion.24
  283.7 6.1 collective-permute-start.7
  289.8 2.7 fusion.65
  292.5 4.7 convolution_convert_fusion
  297.2 4.5 convolution_convert_fusion.1
  304.4 2.3 constant_dynamic-slice_fusion.25
  308.7 24.1 %collective-permute-done.8 = bf16[512,256]{1,0:T(8,128)(2,1)} collective-permute-done((bf16[512,256]{1,0:T(8,128)(2,1)}, bf16[512,256]{1,0:T(8,128)(2,1)}, u32[]{:S(2)}, u32[]{:S(2)}) %collective-permute-start.8) | collective-permute-done | bytes 262176 | tf_op jit(solution)/shard_map/ppermute | solution.py:767
  335.2 41.6 %attention_backward.1 = (bf16[2,384,1024]{2,1,0:T(8,128)(2,1)S(1)}, f32[2,5,64,64]{3,2,1,0:T(8,128)S(1)}) custom-call(bf16[2,384,1024]{2,1,0:T(8,128)(2,1)} %copy-done.11, f32[32,1024]{1,0:T(8,128)S(1)} %copy-done.7, f32[32,1024]{1,0:T(8,128)S(1)} %copy-done.5, bf16[2,320,64]{2,1,0:T(8,128)(2,1)S(1)} %bitcast.245, bf16[2,5,64,64]{3,2,1,0:T(8,128)(2,1)S(1)} %copy-done.9, ...), custom_call_target="tpu_custom_call" | custom-call | flops 40000000000 | bytes 10000000 | tf_op jit(solution)/shard_map/attention_backward/pallas_call | solution.py:214
  380.5 4.5 fusion.46
  386.9 3.8 fusion.7
  391.4 4.4 fusion.100
  403.6 2.1 add_convert_fusion.6
  405.7 21.8 %collective-permute-done.9 = bf16[256,2048]{1,0:T(8,128)(2,1)} collective-permute-done((bf16[256,2048]{1,0:T(8,128)(2,1)}, bf16[256,2048]{1,0:T(8,128)(2,1)}, u32[]{:S(2)}, u32[]{:S(2)}) %collective-permute-start.9) | collective-permute-done | bytes 1048608 | tf_op jit(solution)/shard_map/ppermute | solution.py:686
  427.5 2.2 add_convert_fusion.3
  433.4 16.5 %collective-permute-done.4 = bf16[256,2048]{1,0:T(8,128)(2,1)S(1)} collective-permute-done((bf16[256,2048]{1,0:T(8,128)(2,1)S(1)}, bf16[256,2048]{1,0:T(8,128)(2,1)S(1)}, u32[]{:S(2)}, u32[]{:S(2)}) %collective-permute-start.4) | collective-permute-done | bytes 1048608 | tf_op jit(solution)/shard_map/ppermute | solution.py:686
  450.3 2.6 add_convert_fusion.5
  453.1 6.0 collective-permute-done.20
  459.8 12.5 %collective-permute-done.10 = bf16[256,2048]{1,0:T(8,128)(2,1)S(1)} collective-permute-done((bf16[256,2048]{1,0:T(8,128)(2,1)S(1)}, bf16[256,2048]{1,0:T(8,128)(2,1)S(1)}, u32[]{:S(2)}, u32[]{:S(2)}) %collective-permute-start.10) | collective-permute-done | bytes 1048608 | tf_op jit(solution)/shard_map/ppermute | solution.py:686
  474.1 3.9 collective-permute-done.19
  479.6 4.1 collective-permute-done.21
  485.2 4.2 add_convert_fusion.1
  491.2 25.1 %collective-permute-done.11 = bf16[256,2048]{1,0:T(8,128)(2,1)S(1)} collective-permute-done((bf16[256,2048]{1,0:T(8,128)(2,1)}, bf16[256,2048]{1,0:T(8,128)(2,1)S(1)}, u32[]{:S(2)}, u32[]{:S(2)}) %collective-permute-start.11) | collective-permute-done | bytes 1048608 | tf_op jit(solution)/shard_map/ppermute | solution.py:686
  516.3 4.9 fusion.26
  527.4 3.2 add_convert_fusion
  535.9 2.0 collective-permute-done.13
  539.5 5.2 fusion.25
  546.6 4.1 fusion.3
  557.2 36.2 %collective-permute-done.26 = bf16[2,128,2048]{2,1,0:T(8,128)(2,1)} collective-permute-done((bf16[2,128,2048]{2,1,0:T(8,128)(2,1)S(1)}, bf16[2,128,2048]{2,1,0:T(8,128)(2,1)}, u32[]{:S(2)}, u32[]{:S(2)}) %collective-permute-start.26) | collective-permute-done | bytes 1048608 | tf_op jit(solution)/shard_map/ppermute | solution.py:706
  601.1 6.1 collective-permute-done.27
  607.4 2.3 collective-permute-done.29
  613.0 4.9 collective-permute-done.30
  620.1 6.9 %collective-permute-done.31 = bf16[256,512]{1,0:T(8,128)(2,1)S(1)} collective-permute-done((bf16[256,512]{1,0:T(8,128)(2,1)S(1)}, bf16[256,512]{1,0:T(8,128)(2,1)S(1)}, u32[]{:S(2)}, u32[]{:S(2)}) %collective-permute-start.31) | collective-permute-done | bytes 262176 | tf_op jit(solution)/shard_map/ppermute | solution.py:686
  628.0 5.3 copy.107
  633.2 2.9 copy.88
  (343 shorter events, 94.1 us)
Async XLA Ops:
  7.2 108.8 %all-gather.2.cloned.1.call-start = ((), (), s32[]{:S(2)}) async-start(), calls=%async_computation | async-start | bytes 8650752 | tf_op jit(solution)/shard_map/all_gather | solution.py:758
  59.0 54.7 %collective-permute-start = (bf16[512,256]{0,1:T(8,128)(2,1)S(1)}, bf16[512,256]{0,1:T(8,128)(2,1)}, u32[]{:S(2)}, u32[]{:S(2)}) collective-permute-start(bf16[512,256]{0,1:T(8,128)(2,1)S(1)} %copy.94), channel_id=1, source_target_pairs={{0,1},{1,2},{2,3},{3,0},{4,5},{5,6},{6,7},{7,4},{8,9},{9,10},{10,1... | collective-permute-start | bytes 786440 | tf_op jit(solution)/shard_map/ppermute | solution.py:767
  60.8 52.9 %collective-permute-start.1 = (bf16[512,256]{0,1:T(8,128)(2,1)S(1)}, bf16[512,256]{0,1:T(8,128)(2,1)}, u32[]{:S(2)}, u32[]{:S(2)}) collective-permute-start(bf16[512,256]{0,1:T(8,128)(2,1)S(1)} %copy.95), channel_id=1, source_target_pairs={{0,2},{1,3},{2,0},{3,1},{4,6},{5,7},{6,4},{7,5},{8,10},{9,11},{10,... | collective-permute-start | bytes 786440 | tf_op jit(solution)/shard_map/ppermute | solution.py:767
  62.2 51.5 %collective-permute-start.2 = (bf16[512,256]{0,1:T(8,128)(2,1)S(1)}, bf16[512,256]{0,1:T(8,128)(2,1)}, u32[]{:S(2)}, u32[]{:S(2)}) collective-permute-start(bf16[512,256]{0,1:T(8,128)(2,1)S(1)} %copy.96), channel_id=1, source_target_pairs={{0,3},{1,0},{2,1},{3,2},{4,7},{5,4},{6,5},{7,6},{8,11},{9,8},{10,9... | collective-permute-start | bytes 786440 | tf_op jit(solution)/shard_map/ppermute | solution.py:767
  73.0 40.7 %copy-start.37 = (bf16[512,256]{0,1:T(8,128)(2,1)}, bf16[512,256]{0,1:T(8,128)(2,1)S(1)}, u32[]{:S(2)}) copy-start(bf16[512,256]{0,1:T(8,128)(2,1)S(1)} %copy.93) | copy-start | bytes 786436
  122.3 145.1 %copy-start.14 = (f32[256,2048]{1,0:T(8,128)}, f32[256,2048]{1,0:T(8,128)S(1)}, u32[]{:S(2)}) copy-start(f32[256,2048]{1,0:T(8,128)S(1)} %get-tuple-element.121) | copy-start | bytes 6291460
  122.3 145.1 %copy-start.68 = (f32[256]{0:T(256)}, f32[256]{0:T(256)S(1)}, u32[]{:S(2)}) copy-start(f32[256]{0:T(256)S(1)} %add_rsqrt_fusion.2) | copy-start | bytes 3076
  279.6 205.6 %collective-permute-start.33 = (bf16[2,384,2048]{2,1,0:T(8,128)(2,1)}, bf16[2,384,2048]{2,1,0:T(8,128)(2,1)}, u32[]{:S(2)}, u32[]{:S(2)}) collective-permute-start(bf16[2,384,2048]{2,1,0:T(8,128)(2,1)} %get-tuple-element.31), channel_id=1, source_target_pairs={{0,8},{4,12},{8,0},{12,4},{16,24},{20,28},{24,16},{28,20},{1,9},{5... | collective-permute-start | bytes 9437192 | tf_op jit(solution)/shard_map/ppermute | solution.py:719
  281.1 246.3 %collective-permute-start.35 = (bf16[2,384,2048]{2,1,0:T(8,128)(2,1)}, bf16[2,384,2048]{2,1,0:T(8,128)(2,1)}, u32[]{:S(2)}, u32[]{:S(2)}) collective-permute-start(bf16[2,384,2048]{2,1,0:T(8,128)(2,1)} %get-tuple-element.33), channel_id=1, source_target_pairs={{0,16},{4,20},{8,24},{12,28},{16,0},{20,4},{24,8},{28,12},{1,17},{... | collective-permute-start | bytes 9437192 | tf_op jit(solution)/shard_map/ppermute | solution.py:719
  283.7 23.0 %collective-permute-start.6 = (bf16[512,256]{1,0:T(8,128)(2,1)}, bf16[512,256]{1,0:T(8,128)(2,1)}, u32[]{:S(2)}, u32[]{:S(2)}) collective-permute-start(bf16[512,256]{1,0:T(8,128)(2,1)} %get-tuple-element.105), channel_id=1, source_target_pairs={{0,1},{1,2},{2,3},{3,0},{4,5},{5,6},{6,7},{7,4},{8,9},{9,10},{10,1... | collective-permute-start | bytes 786440 | tf_op jit(solution)/shard_map/ppermute | solution.py:767
  283.7 24.9 %collective-permute-start.7 = (bf16[512,256]{1,0:T(8,128)(2,1)}, bf16[512,256]{1,0:T(8,128)(2,1)}, u32[]{:S(2)}, u32[]{:S(2)}) collective-permute-start(bf16[512,256]{1,0:T(8,128)(2,1)} %get-tuple-element.104), channel_id=1, source_target_pairs={{0,2},{1,3},{2,0},{3,1},{4,6},{5,7},{6,4},{7,5},{8,10},{9,11},{10,... | collective-permute-start | bytes 786440 | tf_op jit(solution)/shard_map/ppermute | solution.py:767
  289.8 43.0 %collective-permute-start.8 = (bf16[512,256]{1,0:T(8,128)(2,1)}, bf16[512,256]{1,0:T(8,128)(2,1)}, u32[]{:S(2)}, u32[]{:S(2)}) collective-permute-start(bf16[512,256]{1,0:T(8,128)(2,1)} %get-tuple-element.103), channel_id=1, source_target_pairs={{0,3},{1,0},{2,1},{3,2},{4,7},{5,4},{6,5},{7,6},{8,11},{9,8},{10,9... | collective-permute-start | bytes 786440 | tf_op jit(solution)/shard_map/ppermute | solution.py:767
  306.7 96.9 %collective-permute-start.3 = (bf16[256,2048]{1,0:T(8,128)(2,1)}, bf16[256,2048]{1,0:T(8,128)(2,1)}, u32[]{:S(2)}, u32[]{:S(2)}) collective-permute-start(bf16[256,2048]{1,0:T(8,128)(2,1)} %constant_dynamic-slice_fusion.25), channel_id=1, source_target_pairs={{0,1},{1,2},{2,3},{3,0},{4,5},{5,6},{6,7},{7,4},{8,9},{9,10},{10,1... | collective-permute-start | bytes 3145736 | tf_op jit(solution)/shard_map/ppermute | solution.py:686
  335.2 41.6 %copy-start.63 = (bf16[1024,3,8]{0,2,1:T(8,128)(2,1)S(1)}, bf16[1024,3,8]{0,2,1:T(8,128)(2,1)}, u32[]{:S(2)}) copy-start(bf16[1024,3,8]{0,2,1:T(8,128)(2,1)} %fusion.60) | copy-start | bytes 147460
  378.8 11.9 %collective-permute-start.22 = (f32[4,5888]{1,0:T(4,128)S(1)}, f32[4,5888]{1,0:T(4,128)S(1)}, u32[]{:S(2)}, u32[]{:S(2)}) collective-permute-start(f32[4,5888]{1,0:T(4,128)S(1)} %dynamic-slice_bitcast_fusion.14), channel_id=1, source_target_pairs={{0,16},{4,20},{8,24},{12,28},{16,0},{20,4},{24,8},{28,12},{1,17},{... | collective-permute-start | bytes 282632 | tf_op jit(solution)/shard_map/ppermute | solution.py:742
  390.8 4.9 collective-permute-start.23
  396.5 4.7 collective-permute-start.24
  398.5 31.3 %collective-permute-start.17 = (bf16[4,256,768]{2,1,0:T(8,128)(2,1)}, bf16[4,256,768]{2,1,0:T(8,128)(2,1)}, u32[]{:S(2)}, u32[]{:S(2)}) collective-permute-start(bf16[4,256,768]{2,1,0:T(8,128)(2,1)} %bitcast.54), channel_id=1, source_target_pairs={{0,4},{4,0},{8,12},{12,8},{16,20},{20,16},{24,28},{28,24},{1,5},{5... | collective-permute-start | bytes 4718600 | tf_op jit(solution)/shard_map/ppermute | solution.py:727
  401.1 26.3 %collective-permute-start.9 = (bf16[256,2048]{1,0:T(8,128)(2,1)}, bf16[256,2048]{1,0:T(8,128)(2,1)}, u32[]{:S(2)}, u32[]{:S(2)}) collective-permute-start(bf16[256,2048]{1,0:T(8,128)(2,1)} %convolution_convert_fusion.2), channel_id=1, source_target_pairs={{0,1},{1,2},{2,3},{3,0},{4,5},{5,6},{6,7},{7,4},{8,9},{9,10},{10,1... | collective-permute-start | bytes 3145736 | tf_op jit(solution)/shard_map/ppermute | solution.py:686
  403.6 23.9 %copy-start.19 = (bf16[2,384,2048]{2,1,0:T(8,128)(2,1)S(1)}, bf16[2,384,2048]{2,1,0:T(8,128)(2,1)}, u32[]{:S(2)}) copy-start(bf16[2,384,2048]{2,1,0:T(8,128)(2,1)} %copy-done.17) | copy-start | bytes 9437188
  405.6 44.2 %collective-permute-start.4 = (bf16[256,2048]{1,0:T(8,128)(2,1)S(1)}, bf16[256,2048]{1,0:T(8,128)(2,1)S(1)}, u32[]{:S(2)}, u32[]{:S(2)}) collective-permute-start(bf16[256,2048]{1,0:T(8,128)(2,1)S(1)} %add_convert_fusion.6), channel_id=1, source_target_pairs={{0,1},{1,2},{2,3},{3,0},{4,5},{5,6},{6,7},{7,4},{8,9},{9,10},{10,1... | collective-permute-start | bytes 3145736 | tf_op jit(solution)/shard_map/ppermute | solution.py:686
  429.7 42.6 %collective-permute-start.10 = (bf16[256,2048]{1,0:T(8,128)(2,1)S(1)}, bf16[256,2048]{1,0:T(8,128)(2,1)S(1)}, u32[]{:S(2)}, u32[]{:S(2)}) collective-permute-start(bf16[256,2048]{1,0:T(8,128)(2,1)S(1)} %add_convert_fusion.3), channel_id=1, source_target_pairs={{0,1},{1,2},{2,3},{3,0},{4,5},{5,6},{6,7},{7,4},{8,9},{9,10},{10,1... | collective-permute-start | bytes 3145736 | tf_op jit(solution)/shard_map/ppermute | solution.py:686
  431.7 21.2 %collective-permute-start.18 = (bf16[2,128,768]{2,1,0:T(8,128)(2,1)S(1)}, bf16[2,128,768]{2,1,0:T(8,128)(2,1)S(1)}, u32[]{:S(2)}, u32[]{:S(2)}) collective-permute-start(bf16[2,128,768]{2,1,0:T(8,128)(2,1)S(1)} %dynamic-slice_bitcast_fusion.7), channel_id=1, source_target_pairs={{0,8},{4,12},{8,0},{12,4},{16,24},{20,28},{24,16},{28,20},{1,9},{5... | collective-permute-start | bytes 1179656 | tf_op jit(solution)/shard_map/ppermute | solution.py:706
  449.9 9.2 %collective-permute-start.20 = (bf16[2,128,768]{2,1,0:T(8,128)(2,1)S(1)}, bf16[2,128,768]{2,1,0:T(8,128)(2,1)S(1)}, u32[]{:S(2)}, u32[]{:S(2)}) collective-permute-start(bf16[2,128,768]{2,1,0:T(8,128)(2,1)S(1)} %dynamic-slice_bitcast_fusion.6), channel_id=1, source_target_pairs={{0,16},{4,20},{8,24},{12,28},{16,0},{20,4},{24,8},{28,12},{1,17},{... | collective-permute-start | bytes 1179656 | tf_op jit(solution)/shard_map/ppermute | solution.py:706
  452.9 93.7 %collective-permute-start.25 = (bf16[4,256,2048]{2,1,0:T(8,128)(2,1)}, bf16[4,256,2048]{2,1,0:T(8,128)(2,1)}, u32[]{:S(2)}, u32[]{:S(2)}) collective-permute-start(bf16[4,256,2048]{2,1,0:T(8,128)(2,1)} %bitcast.80), channel_id=1, source_target_pairs={{0,4},{4,0},{8,12},{12,8},{16,20},{20,16},{24,28},{28,24},{1,5},{5... | collective-permute-start | bytes 12582920 | tf_op jit(solution)/shard_map/ppermute | solution.py:727
  459.1 80.4 %collective-permute-start.5 = (bf16[256,2048]{1,0:T(8,128)(2,1)}, bf16[256,2048]{1,0:T(8,128)(2,1)}, u32[]{:S(2)}, u32[]{:S(2)}) collective-permute-start(bf16[256,2048]{1,0:T(8,128)(2,1)} %add_convert_fusion.5), channel_id=1, source_target_pairs={{0,1},{1,2},{2,3},{3,0},{4,5},{5,6},{6,7},{7,4},{8,9},{9,10},{10,1... | collective-permute-start | bytes 3145736 | tf_op jit(solution)/shard_map/ppermute | solution.py:686
  472.3 5.7 collective-permute-start.19
  478.0 5.7 collective-permute-start.21
  483.7 32.6 %collective-permute-start.11 = (bf16[256,2048]{1,0:T(8,128)(2,1)}, bf16[256,2048]{1,0:T(8,128)(2,1)S(1)}, u32[]{:S(2)}, u32[]{:S(2)}) collective-permute-start(bf16[256,2048]{1,0:T(8,128)(2,1)} %add_convert_fusion.2), channel_id=1, source_target_pairs={{0,1},{1,2},{2,3},{3,0},{4,5},{5,6},{6,7},{7,4},{8,9},{9,10},{10,1... | collective-permute-start | bytes 3145736 | tf_op jit(solution)/shard_map/ppermute | solution.py:686
  485.2 31.1 %copy-start.53 = (f32[1,2048]{1,0:T(1,128)S(1)}, f32[1,2048]{1,0:T(1,128)}, u32[]{:S(2)}) copy-start(f32[1,2048]{1,0:T(1,128)} %copy-done.52) | copy-start | bytes 24580
  485.2 31.1 %copy-start.70 = (f32[256]{0:T(256)S(1)}, f32[256]{0:T(256)}, u32[]{:S(2)}) copy-start(f32[256]{0:T(256)} %add_rsqrt_fusion.1) | copy-start | bytes 3076
  489.5 31.8 %copy-start.21 = (bf16[2,384,2048]{2,1,0:T(8,128)(2,1)}, bf16[2,384,2048]{2,1,0:T(8,128)(2,1)S(1)}, u32[]{:S(2)}) copy-start(bf16[2,384,2048]{2,1,0:T(8,128)(2,1)S(1)} %add_convert_fusion.1) | copy-start | bytes 9437188
  489.5 26.8 %copy-start.20 = (bf16[2,384,2048]{2,1,0:T(8,128)(2,1)S(1)}, bf16[2,384,2048]{2,1,0:T(8,128)(2,1)}, u32[]{:S(2)}) copy-start(bf16[2,384,2048]{2,1,0:T(8,128)(2,1)} %copy-done.17) | copy-start | bytes 9437188
  490.7 32.1 %copy-start.36 = (f32[24,8,4,64]{3,0,2,1:T(8,128)S(1)}, f32[24,8,4,64]{3,0,2,1:T(8,128)}, u32[]{:S(2)}) copy-start(f32[24,8,4,64]{3,0,2,1:T(8,128)} %copy.77) | copy-start | bytes 589828
  490.7 108.4 %collective-permute-start.34 = (bf16[384,2048]{1,0:T(8,128)(2,1)}, bf16[384,2048]{1,0:T(8,128)(2,1)}, u32[]{:S(2)}, u32[]{:S(2)}) collective-permute-start(bf16[384,2048]{1,0:T(8,128)(2,1)} %dynamic-slice_bitcast_fusion.1), channel_id=1, source_target_pairs={{0,16},{4,20},{8,24},{12,28},{16,0},{20,4},{24,8},{28,12},{1,17},{... | collective-permute-start | bytes 4718600 | tf_op jit(solution)/shard_map/ppermute | solution.py:706
  526.9 5.6 collective-permute-start.12
  532.6 5.4 collective-permute-start.13
  535.4 75.6 %collective-permute-start.36 = (bf16[384,2048]{1,0:T(8,128)(2,1)}, bf16[384,2048]{1,0:T(8,128)(2,1)}, u32[]{:S(2)}, u32[]{:S(2)}) collective-permute-start(bf16[384,2048]{1,0:T(8,128)(2,1)} %dynamic-slice_bitcast_fusion), channel_id=1, source_target_pairs={{0,8},{4,12},{8,0},{12,4},{16,24},{20,28},{24,16},{28,20},{1,9},{5... | collective-permute-start | bytes 4718600 | tf_op jit(solution)/shard_map/ppermute | solution.py:706
  538.0 1.3 collective-permute-start.14
  539.4 5.3 collective-permute-start.15
  544.8 8.3 %collective-permute-start.16 = (f32[1,2688]{1,0:T(1,128)S(1)}, f32[1,2688]{1,0:T(1,128)S(1)}, u32[]{:S(2)}, u32[]{:S(2)}) collective-permute-start(f32[1,2688]{1,0:T(1,128)S(1)} %constant_dynamic-slice_fusion.17), channel_id=1, source_target_pairs={{0,1},{1,0},{2,3},{3,2},{4,5},{5,4},{6,7},{7,6},{8,9},{9,8},{10,11... | collective-permute-start | bytes 32264 | tf_op jit(solution)/shard_map/ppermute | solution.py:749
  551.3 42.1 %collective-permute-start.26 = (bf16[2,128,2048]{2,1,0:T(8,128)(2,1)S(1)}, bf16[2,128,2048]{2,1,0:T(8,128)(2,1)}, u32[]{:S(2)}, u32[]{:S(2)}) collective-permute-start(bf16[2,128,2048]{2,1,0:T(8,128)(2,1)S(1)} %dynamic-slice_bitcast_fusion.3), channel_id=1, source_target_pairs={{0,8},{4,12},{8,0},{12,4},{16,24},{20,28},{24,16},{28,20},{1,9},{5... | collective-permute-start | bytes 3145736 | tf_op jit(solution)/shard_map/ppermute | solution.py:706
  554.2 41.8 %collective-permute-start.28 = (bf16[2,128,2048]{2,1,0:T(8,128)(2,1)}, bf16[2,128,2048]{2,1,0:T(8,128)(2,1)}, u32[]{:S(2)}, u32[]{:S(2)}) collective-permute-start(bf16[2,128,2048]{2,1,0:T(8,128)(2,1)} %dynamic-slice_bitcast_fusion.2), channel_id=1, source_target_pairs={{0,16},{4,20},{8,24},{12,28},{16,0},{20,4},{24,8},{28,12},{1,17},{... | collective-permute-start | bytes 3145736 | tf_op jit(solution)/shard_map/ppermute | solution.py:706
  595.4 11.9 %collective-permute-start.27 = (bf16[128,2048]{1,0:T(8,128)(2,1)S(1)}, bf16[128,2048]{1,0:T(8,128)(2,1)S(1)}, u32[]{:S(2)}, u32[]{:S(2)}) collective-permute-start(bf16[128,2048]{1,0:T(8,128)(2,1)S(1)} %dynamic-slice_bitcast_fusion.5), channel_id=1, source_target_pairs={{0,16},{4,20},{8,24},{12,28},{16,0},{20,4},{24,8},{28,12},{1,17},{... | collective-permute-start | bytes 1572872 | tf_op jit(solution)/shard_map/ppermute | solution.py:706
  597.9 11.8 %collective-permute-start.29 = (bf16[128,2048]{1,0:T(8,128)(2,1)S(1)}, bf16[128,2048]{1,0:T(8,128)(2,1)S(1)}, u32[]{:S(2)}, u32[]{:S(2)}) collective-permute-start(bf16[128,2048]{1,0:T(8,128)(2,1)S(1)} %dynamic-slice_bitcast_fusion.4), channel_id=1, source_target_pairs={{0,8},{4,12},{8,0},{12,4},{16,24},{20,28},{24,16},{28,20},{1,9},{5... | collective-permute-start | bytes 1572872 | tf_op jit(solution)/shard_map/ppermute | solution.py:706
  609.9 8.0 %collective-permute-start.30 = (bf16[256,512]{1,0:T(8,128)(2,1)S(1)}, bf16[256,512]{1,0:T(8,128)(2,1)S(1)}, u32[]{:S(2)}, u32[]{:S(2)}) collective-permute-start(bf16[256,512]{1,0:T(8,128)(2,1)S(1)} %fusion.77), channel_id=1, source_target_pairs={{0,1},{1,2},{2,3},{3,0},{4,5},{5,6},{6,7},{7,4},{8,9},{9,10},{10,1... | collective-permute-start | bytes 786440 | tf_op jit(solution)/shard_map/ppermute | solution.py:686
  618.0 9.0 %collective-permute-start.31 = (bf16[256,512]{1,0:T(8,128)(2,1)S(1)}, bf16[256,512]{1,0:T(8,128)(2,1)S(1)}, u32[]{:S(2)}, u32[]{:S(2)}) collective-permute-start(bf16[256,512]{1,0:T(8,128)(2,1)S(1)} %fusion.80), channel_id=1, source_target_pairs={{0,1},{1,2},{2,3},{3,0},{4,5},{5,6},{6,7},{7,4},{8,9},{9,10},{10,1... | collective-permute-start | bytes 786440 | tf_op jit(solution)/shard_map/ppermute | solution.py:686
  627.0 9.1 %collective-permute-start.32 = (bf16[256,512]{1,0:T(8,128)(2,1)S(1)}, bf16[256,512]{1,0:T(8,128)(2,1)S(1)}, u32[]{:S(2)}, u32[]{:S(2)}) collective-permute-start(bf16[256,512]{1,0:T(8,128)(2,1)S(1)} %fusion.75), channel_id=1, source_target_pairs={{0,1},{1,2},{2,3},{3,0},{4,5},{5,6},{6,7},{7,4},{8,9},{9,10},{10,1... | collective-permute-start | bytes 786440 | tf_op jit(solution)/shard_map/ppermute | solution.py:686
  (66 other events, 344.1 us)
Sparse Core Ops, SparseCore 0:
  11.5 94.4 all-gather.1

commit v4 on v3

--- a/solution.py
+++ b/solution.py
@@ -663,6 +663,382 @@
     )(normed, cotangent, gate_up, down)
 
 
+def tail_kernel(
+    n, dp, tile, cut,
+    joined_in, w_in, normed_in, att_in, att_mate_in, grad_in, grad_mate_in, fa_keep, fa_came, fb_keep, fb_came,
+    sum_out, feed_a, feed_b, branch_out, qkv_a, qkv_b,
+    joined, w, normed, att, att_mate, grad, grad_mate, arriving, sending,
+    fa, fa2, fb, fb2, f_recvs, wm, w_recvs, w_done, w_last, qo, qm, qc, q_recvs,
+    load_sems, out_sems, sum_send, sum_recv, f_sems, w_sems, q_sems, core_sems, last_send, last_recv,
+):
+    width = w.shape[1]
+    joined_width, tokens = joined.shape
+    share = tokens // n
+    block = width // dp
+    piece = share // cut
+    columns = att.shape[0]
+    me = lax.axis_index("tensor")
+    mine = lax.axis_index("dp")
+    core = lax.rem(mine, 2)
+    bits = dp.bit_length() - 1
+    mesh_id = pl.DeviceIdType.MESH
+    place = (me, n - 1 - me)
+    ends = (me < n - 1, me > 0)
+    partner = (me + 1, me - 1)
+
+    def own_bit(bit):
+        return lax.rem(lax.div(mine, 1 << bit), 2)
+
+    def mate(bit):
+        return {"dp": mine + (1 << bit) * (1 - 2 * own_bit(bit))}
+
+    barrier = pltpu.get_barrier_semaphore()
+    for s in range(1, n):
+        pl.semaphore_signal(barrier, inc=1, device_id={"tensor": lax.rem(me + s, n)}, device_id_type=mesh_id)
+    for bit in range(bits):
+        pl.semaphore_signal(barrier, inc=1, device_id=mate(bit), device_id_type=mesh_id)
+
+    pairs = (
+        (joined_in, joined), (w_in, w), (att_in, att), (att_mate_in, att_mate), (grad_in, grad),
+        (grad_mate_in, grad_mate), (normed_in, normed), (fa_keep, fa), (fa_came, fa2), (fb_keep, fb), (fb_came, fb2),
+    )
+    loads = [pltpu.make_async_copy(a, b, load_sems.at[i]) for i, (a, b) in enumerate(pairs)]
+    for load in loads:
+        load.start()
+    pl.semaphore_wait(barrier, n - 1 + bits)
+
+    def rows_of(j):
+        return pl.ds(pl.multiple_of(j * share, 16), share)
+
+    def pass_on(way, j, q):
+        rows = pl.ds(pl.multiple_of(j * share + q * piece, 16), piece)
+        last = j == partner[way]
+        slot = jnp.where(last, n, j) if way else j
+        goal = pl.ds(pl.multiple_of(slot * share + q * piece, 16), piece)
+        return pltpu.make_async_remote_copy(
+            src_ref=sending.at[rows], dst_ref=arriving.at[goal],
+            send_sem=sum_send.at[way, j * cut + q], recv_sem=sum_recv.at[way, j * cut + q],
+            device_id={"tensor": partner[way]}, device_id_type=mesh_id)
+
+    def sum_arrival(way, j, q, slot):
+        rows = pl.ds(pl.multiple_of(slot * share + q * piece, 16), piece)
+        return pltpu.make_async_copy(arriving.at[rows], arriving.at[rows], sum_recv.at[way, j * cut + q])
+
+    loads[0].wait()
+    loads[1].wait()
+    for k in range(n):
+        distance = n - 1 - k
+        for way in range(2):
+            j = me + distance if way == 0 else me - distance
+            there = (j < n) if way == 0 else (j >= 0)
+            if distance == 0 and way:
+                continue
+
+            @pl.when(there)
+            def _(j=j, way=way, distance=distance):
+                rows = rows_of(j)
+
+                @pl.loop(0, width // tile)
+                def _(d):
+                    span = pl.ds(pl.multiple_of(d * tile, tile), tile)
+                    sending[rows, span] = lax.dot_general(
+                        joined[:, pl.ds(pl.multiple_of(j * share, 128), share)], w[:, span],
+                        (((0,), (0,)), ((), ())), preferred_element_type=F32).astype(BF16)
+
+                if distance:
+
+                    @pl.when(place[way] == 0)
+                    def _():
+                        for q in range(cut):
+                            pass_on(way, j, q).start()
+
+    def halving(cur, parts, recvs, sems, stream, order):
+        steps = []
+        current = cur
+        for step, bit in enumerate(order):
+            count = 1 << (len(order) - step - 1)
+            own = own_bit(bit)
+
+            def index(slot, which, count=count):
+                return 2 * slot + which if stream == 0 else which * count + slot
+
+            room = recvs[stream][step]
+            copies = [
+                pltpu.make_async_remote_copy(
+                    src_ref=current(index(slot, 1 - own)), dst_ref=room.at[slot],
+                    send_sem=sems.at[0, stream, step, slot], recv_sem=sems.at[1, stream, step, slot],
+                    device_id=mate(bit), device_id_type=mesh_id)
+                for slot in range(count)
+            ]
+
+            def start(copies=copies):
+                for copy in copies:
+                    copy.start()
+
+            def finish(copies=copies, current=current, room=room, count=count, own=own, index=index):
+                for slot, copy in enumerate(copies):
+                    copy.wait_recv()
+                    kept = current(index(slot, own))
+                    total = kept.shape[0]
+                    rows = 128 if total % 128 == 0 else 64 if total % 64 == 0 else total
+
+                    @pl.loop(0, total // rows)
+                    def _(r):
+                        span = pl.ds(pl.multiple_of(r * rows, 16), rows)
+                        room[slot, span, :] = (kept[span, :].astype(F32) + room[slot, span, :].astype(F32)).astype(BF16)
+
+            def settle(copies=copies):
+                for copy in copies:
+                    copy.wait_send()
+
+            steps.append((start, finish, settle))
+            current = lambda i, room=room: room.at[i]
+        return steps
+
+    rest = list(range(1, bits))
+    half_rows = block // 2
+    w_steps = [
+        halving(lambda i, s=s: wm.at[i, pl.ds(s * half_rows, half_rows)], dp // 2, w_recvs, w_sems, s, order)
+        for s, order in enumerate((rest, rest[::-1]))
+    ]
+    q_steps = [
+        halving(lambda i, s=s: qm.at[i, pl.ds(s * half_rows, half_rows)], dp // 2, q_recvs, q_sems, s, order)
+        for s, order in enumerate((rest, rest[::-1]))
+    ]
+    f_steps = [
+        halving(lambda i, ref=ref: ref.at[i], dp // 4, f_recvs, f_sems, s, order[1:])
+        for s, (ref, order) in enumerate(((fa, rest), (fb, rest[::-1])))
+    ]
+
+    for load in loads[2:6]:
+        load.wait()
+
+    @pl.loop(0, dp // 2)
+    def _(q):
+        span = pl.ds(pl.multiple_of(q * block, block), block)
+        turned, turned_mate = grad[:, span].T, grad_mate[:, span].T
+        for c in range(0, columns, tile):
+            wm[q, :, c:c + tile] = (nt(turned, att[c:c + tile, :]) + nt(turned_mate, att_mate[c:c + tile, :])).astype(BF16)
+
+    for s in range(2):
+        w_steps[s][0][0]()
+
+    loads[6].wait()
+
+    def across(q):
+        return pltpu.make_async_remote_copy(
+            src_ref=qo.at[q], dst_ref=qc.at[q], send_sem=core_sems.at[0, q], recv_sem=core_sems.at[1, q],
+            device_id=mate(0), device_id_type=mesh_id)
+
+    def projection(q, which):
+        column = 2 * q + which
+        span = pl.ds(pl.multiple_of(column * block, block), block)
+        return nt(normed[:, span].T, joined[...])
+
+    @pl.loop(0, dp // 2)
+    def _(q):
+        qo[q] = projection(q, 1 - core).astype(BF16)
+        across(q).start()
+
+    @pl.loop(0, dp // 2)
+    def _(q):
+        product = projection(q, core)
+        across(q).wait_recv()
+        qm[q] = (product + qc[q].astype(F32)).astype(BF16)
+
+    for s in range(2):
+        q_steps[s][0][0]()
+
+    for load in loads[7:]:
+        load.wait()
+    for one, other in ((fa, fa2), (fb, fb2)):
+        for i in range(dp // 4):
+            rows = 64 if one.shape[1] % 64 == 0 else one.shape[1]
+
+            @pl.loop(0, one.shape[1] // rows)
+            def _(r, one=one, other=other, i=i):
+                span = pl.ds(pl.multiple_of(r * rows, 16), rows)
+                one[i, span, :] = (one[i, span, :].astype(F32) + other[i, span, :].astype(F32)).astype(BF16)
+
+    def serve(step):
+        for way in range(2):
+            count = step - place[way]
+            reach = lax.div(count, cut)
+            j_place = n - 1 - reach
+            q = lax.rem(count, cut)
+            j = j_place if way == 0 else n - 1 - j_place
+
+            @pl.when((place[way] > 0) & (count >= 0) & (j_place > place[way]))
+            def _(way=way, j=j, q=q):
+                sum_arrival(way, j, q, j).wait()
+                rows = pl.ds(pl.multiple_of(j * share + q * piece, 16), piece)
+                sending[rows, :] = (sending[rows, :].astype(F32) + arriving[rows, :].astype(F32)).astype(BF16)
+                pass_on(way, j, q).start()
+
+    last_step = cut * (n - 2) + n - 1
+    first = 1 + cut
+    pl.loop(1, first)(serve)
+    for step in range(len(rest)):
+        for s in range(2):
+            w_steps[s][step][1]()
+            if step + 1 < len(rest):
+                w_steps[s][step + 1][0]()
+            q_steps[s][step][1]()
+            if step + 1 < len(rest):
+                q_steps[s][step + 1][0]()
+        if step == 0:
+            for s in range(2):
+                f_steps[s][0][0]()
+        begin = first + step * 2
+        end = min(begin + 2, last_step) if step + 1 < len(rest) else last_step
+        if step + 1 < len(rest):
+            pl.loop(begin, end)(serve)
+
+    own_columns = columns // n
+    for s in range(2):
+        w_done[pl.ds(s * half_rows, half_rows), :] = w_recvs[s][len(rest) - 1][0]
+
+    def deliver(s):
+        goal = lax.rem(me + s, n)
+        return pltpu.make_async_remote_copy(
+            src_ref=w_done.at[:, pl.ds(pl.multiple_of(goal * own_columns, 128), own_columns)],
+            dst_ref=w_last.at[s - 1], send_sem=last_send.at[s - 1], recv_sem=last_recv.at[s - 1],
+            device_id={"tensor": goal}, device_id_type=mesh_id)
+
+    for s in range(1, n):
+        deliver(s).start()
+    q_outs = [
+        pltpu.make_async_copy(q_recvs[s][len(rest) - 1].at[0], (qkv_a, qkv_b)[s], out_sems.at[s]) for s in range(2)
+    ]
+    for copy in q_outs:
+        copy.start()
+    pl.loop(first + 2 * (len(rest) - 1), last_step)(serve)
+
+    for step in range(len(rest) - 1):
+        for s in range(2):
+            f_steps[s][step][1]()
+            if step + 1 < len(rest) - 1:
+                f_steps[s][step + 1][0]()
+    f_outs = [
+        pltpu.make_async_copy(f_recvs[s][len(rest) - 2].at[0], (feed_a, feed_b)[s], out_sems.at[2 + s]) for s in range(2)
+    ]
+    for copy in f_outs:
+        copy.start()
+
+    mine_columns = pl.ds(pl.multiple_of(me * own_columns, 128), own_columns)
+    total = w_done[:, mine_columns].astype(F32)
+    for s in range(1, n):
+        deliver(s).wait_recv()
+        total = total + w_last[s - 1].astype(F32)
+    w_last[n - 1] = total.astype(BF16)
+    branch = pltpu.make_async_copy(w_last.at[n - 1], branch_out, out_sems.at[4])
+    branch.start()
+
+    for way in range(2):
+
+        @pl.when(place[way] > 0)
+        def _(way=way):
+            for q in range(cut):
+                slot = n if way else me
+                sum_arrival(way, me, q, slot).wait()
+            slot = pl.ds(n * share, share) if way else rows_of(me)
+
+            @pl.loop(0, width // tile)
+            def _(d):
+                span = pl.ds(pl.multiple_of(d * tile, tile), tile)
+                sending[rows_of(me), span] = (
+                    sending[rows_of(me), span].astype(F32) + arriving[slot, span].astype(F32)
+                ).astype(BF16)
+
+    final = pltpu.make_async_copy(sending.at[rows_of(me)], sum_out, out_sems.at[5])
+    final.start()
+    for copy in (*q_outs, *f_outs, branch, final):
+        copy.wait()
+    for steps in (*w_steps, *q_steps, *f_steps):
+        for _, _, settle in steps:
+            settle()
+    for s in range(1, n):
+        deliver(s).wait_send()
+
+    @pl.loop(0, dp // 2)
+    def _(q):
+        across(q).wait_send()
+
+    for way in range(2):
+
+        @pl.when(ends[way])
+        def _(way=way):
+            @pl.loop(0, n)
+            def _(j):
+                sent = (j > me) if way == 0 else (j < me)
+
+                @pl.when(sent)
+                def _():
+                    for q in range(cut):
+                        pass_on(way, j, q).wait_send()
+
+
+def tail(joined, w, normed, att, att_mate, grad, grad_mate, feed, n, dp, tile=512, cut=4):
+    joined_width, tokens = joined.shape
+    width = w.shape[1]
+    share = tokens // n
+    block = width // dp
+    columns = att.shape[0]
+    steps = dp.bit_length() - 2
+    feed_rows, hidden = feed[0].shape[1:]
+    anywhere = pl.BlockSpec(memory_space=pl.ANY)
+    half = block // 2
+
+    def rooms(rows, cols, count):
+        return [[pltpu.VMEM((1 << (count - step - 1), rows, cols), BF16) for step in range(count)] for _ in range(2)]
+
+    def like(array):
+        return pltpu.VMEM(array.shape, BF16)
+
+    return pl.pallas_call(
+        partial(tail_kernel, n, dp, tile, cut),
+        out_shape=(
+            jax.ShapeDtypeStruct((share, width), BF16),
+            jax.ShapeDtypeStruct((feed_rows, hidden), BF16),
+            jax.ShapeDtypeStruct((feed_rows, hidden), BF16),
+            jax.ShapeDtypeStruct((block, columns // n), BF16),
+            jax.ShapeDtypeStruct((half, joined_width), BF16),
+            jax.ShapeDtypeStruct((half, joined_width), BF16),
+        ),
+        in_specs=[anywhere] * 11,
+        out_specs=(anywhere,) * 6,
+        scratch_shapes=[
+            like(joined), like(w), like(normed), like(att), like(att_mate), like(grad), like(grad_mate),
+            pltpu.VMEM((tokens + share, width), BF16),
+            pltpu.VMEM((tokens, width), BF16),
+            like(feed[0]), like(feed[1]), like(feed[2]), like(feed[3]),
+            rooms(feed_rows, hidden, steps - 1),
+            pltpu.VMEM((dp // 2, block, columns), BF16),
+            rooms(half, columns, steps),
+            pltpu.VMEM((block, columns), BF16),
+            pltpu.VMEM((n, block, columns // n), BF16),
+            pltpu.VMEM((dp // 2, block, joined_width), BF16),
+            pltpu.VMEM((dp // 2, block, joined_width), BF16),
+            pltpu.VMEM((dp // 2, block, joined_width), BF16),
+            rooms(half, joined_width, steps),
+            pltpu.SemaphoreType.DMA((11,)),
+            pltpu.SemaphoreType.DMA((6,)),
+            pltpu.SemaphoreType.DMA((2, n * cut)),
+            pltpu.SemaphoreType.DMA((2, n * cut)),
+            pltpu.SemaphoreType.DMA((2, 2, steps, dp // 4)),
+            pltpu.SemaphoreType.DMA((2, 2, steps, dp // 4)),
+            pltpu.SemaphoreType.DMA((2, 2, steps, dp // 4)),
+            pltpu.SemaphoreType.DMA((2, dp // 2)),
+            pltpu.SemaphoreType.DMA((n - 1,)),
+            pltpu.SemaphoreType.DMA((n - 1,)),
+        ],
+        compiler_params=pltpu.CompilerParams(
+            collective_id=1, has_side_effects=True, vmem_limit_bytes=60 * 2**20),
+        cost_estimate=pl.CostEstimate(flops=100 * 10**9, bytes_accessed=40 * 2**20, transcendentals=0),
+        name="gradient_sums",
+    )(joined, w, normed, att, att_mate, grad, grad_mate, *feed)
+
+
 def ring(size, shift=1):
     return [(i, (i + shift) % size) for i in range(size)]
 
@@ -679,59 +1055,8 @@
     return lax.dynamic_slice_in_dim(array, index * rows, rows, axis)
 
 
-def ring_sum(parts):
-    size = len(parts)
-    running = parts[1].astype(BF16)
-    for step in range(2, size + 1):
-        arrived = lax.ppermute(running, "tensor", ring(size)).astype(F32)
-        running = arrived + parts[step % size].astype(F32)
-        if step < size:
-            running = running.astype(BF16)
-    return running
-
-
 def bits_of(size):
     return size.bit_length() - 1
-
-
-def halve(current, axis, order):
-    size = lax.axis_size("dp")
-    mine = lax.axis_index("dp")
-    remaining = sorted(order, reverse=True)
-    shape = current.shape
-    current = current.reshape(shape[:axis] + (2,) * len(remaining) + shape[axis + 1:])
-    for place, bit in enumerate(order):
-        where = axis + remaining.index(bit)
-        own = (mine >> bit) & 1
-        arrived = lax.ppermute(pick(current, 1 - own, where), "dp", flip(size, bit))
-        current = pick(current, own, where).astype(F32) + arrived.astype(F32)
-        remaining.remove(bit)
-        if place < len(order) - 1:
-            current = current.astype(BF16)
-    return current
-
-
-def scatter_rest(first_send, first_keep, second_send, second_keep):
-    size = lax.axis_size("dp")
-    rest = list(range(1, bits_of(size)))
-    halves = []
-    for send, keep, order in ((first_send, first_keep, rest), (second_send, second_keep, rest[::-1])):
-        arrived = lax.ppermute(send, "dp", flip(size, order[0]))
-        current = keep.astype(F32) + arrived.astype(F32)
-        halves.append(halve(current.astype(BF16), 0, order[1:]) if order[1:] else current[0])
-    return jnp.concatenate(halves, axis=0)
-
-
-def scatter_dp(other, own):
-    size = lax.axis_size("dp")
-    arrived = lax.ppermute(other.astype(BF16), "dp", flip(size, 0))
-    current = own.astype(F32) + arrived.astype(F32)
-    rest = list(range(1, bits_of(size)))
-    half = current.shape[1] // 2
-    parts = []
-    for part, order in ((current[:, :half], rest), (current[:, half:], rest[::-1])):
-        parts.append(halve(part.astype(BF16), 0, order))
-    return jnp.concatenate(parts, axis=0)
 
 
 def scatter_small(blocks, over_tensor):
@@ -849,16 +1174,34 @@
     grad_att_share = dot("ncd,td->nct", all_branch, grad_branch).astype(BF16)
     back = by_place(exchange(lambda j: pick(grad_att_share, j, 0), 1))
     grad_attended = jnp.concatenate(back, axis=1).reshape(groups, query_width, token_rows)
-    mixed = ring_sum([chunk_of(mixed_parts, (me + n - s) % n, share, 0) for s in range(n)])
+    mixed = lax.psum_scatter(mixed_parts, "tensor", scatter_dimension=0, tiled=True).astype(F32)
     output = (hidden + mixed).astype(BF16)
 
     grad_joined, grad_maps = attention_backward(
         low, cosines, sines, maps_t, maps, seg_row, seg_col, attended, root, grad_attended, heads
     )
     flat_joined = grad_joined.reshape(groups * joined_width, token_rows)
-    grad_normed_one = ring_sum(
-        [dot("ct,cd->td", chunk_of(flat_joined, (me + n - s) % n, share, 1), w_joined) for s in range(n)]
-    )
+    width = model_width // dp
+    core = lax.axis_index("dp") & 1
+
+    def of_core(array, which):
+        return jnp.concatenate([chunk_of(array, 2 * q + which, width, 1) for q in range(dp // 2)], axis=1)
+
+    flat_att = att_share.reshape(-1, share)
+    att_mate = lax.ppermute(flat_att, "dp", flip(dp, 0))
+    branch_own = of_core(grad_branch, core)
+    branch_mate = lax.ppermute(of_core(grad_branch, 1 - core), "dp", flip(dp, 0))
+    first_send, first_keep, second_send, second_keep = grads_feed
+    rest = list(range(1, bits_of(dp)))
+    grad_normed_one, feed_a, feed_b, out_branch, qkv_a, qkv_b = tail(
+        flat_joined, w_joined, normed_one, flat_att, att_mate, branch_own, branch_mate,
+        (
+            first_keep, lax.ppermute(first_send, "dp", flip(dp, rest[0])),
+            second_keep, lax.ppermute(second_send, "dp", flip(dp, rest[-1])),
+        ),
+        n, dp,
+    )
+    grad_normed_one = grad_normed_one.astype(F32)
     scaled_one, inverse_one, _ = normalize(tokens_share, gains[0])
     weighted = grad_normed_one * gains[0]
     grad_input = (
@@ -868,26 +1211,11 @@
     ).astype(BF16)
     gain_one = jnp.sum(grad_normed_one * scaled_one, axis=0)
 
-    width = model_width // dp
-    core = lax.axis_index("dp") & 1
-
-    def of_core(array, which):
-        return jnp.concatenate([chunk_of(array, 2 * q + which, width, 1) for q in range(dp // 2)], axis=1)
-
-    def blocks_of(product):
-        return product.astype(BF16).reshape(dp // 2, width, -1)
-
-    out_feed = scatter_rest(*grads_feed).reshape(3, width, -1)
+    out_feed = jnp.concatenate([feed_a, feed_b], axis=0).astype(F32).reshape(3, width, -1)
     out_gate_up = jnp.transpose(out_feed[:2], (1, 0, 2))
     out_down = out_feed[2].T
-    flat_att = jnp.concatenate(att_came, axis=0)
-    out_branch = scatter_dp(
-        *[blocks_of(dot("tb,ct->bc", of_core(grad_branch, which), flat_att)) for which in (1 - core, core)]
-    )
-    out_branch = ring_sum([chunk_of(out_branch, s, groups * query_width, 1) for s in range(n)]).T
-    out_qkv = scatter_dp(
-        *[blocks_of(dot("tb,ct->bc", of_core(normed_one, which), flat_joined)) for which in (1 - core, core)]
-    ).reshape(width, groups, joined_width)
+    out_branch = out_branch.T.astype(F32)
+    out_qkv = jnp.concatenate([qkv_a, qkv_b], axis=0).astype(F32).reshape(width, groups, joined_width)
 
     lowrank_low = lowrank.astype(BF16)
     grad_up = jnp.concatenate(

time: 657 us -> 588 us (0.89)
  waiting for transfers between devices: 176 us -> 33.3 us
  Pallas kernels: 209 us -> 350 us
  matrix products: 63.5 us -> 32.9 us
  other arithmetic: 53.2 us -> 34.6 us
  local copies, waits for them, and re-layouts: 70.2 us -> 61.1 us
  starting transfers between devices: 34 us -> 25.7 us
    ppermute x23 -> x4, waiting for transfers between devices: 146 us -> 0.01 us  [the longest x1 0.01 us: local(): att_mate = lax.ppermute(flat_att, 'dp', flip(dp, 0))]
    pallas_call x0 -> x1, Pallas kernels: none -> 138 us  [tail(): pl.pallas_call(partial(tail_kernel, n, dp, tile, cut), out_shape=(jax.Sha...]
    dot_general x8 -> x0, matrix products: 29.1 us -> none  [the longest x4 13.5 us: local(): dot('ct,cd->td', chunk_of(flat_joined, (me + n - s) % n, share, 1), w_joi...]
    ppermute x23 -> x4, starting transfers between devices: 16.5 us -> 2.05 us  [the longest x1 1.52 us: local(): lax.ppermute(first_send, 'dp', flip(dp, rest[0]))]
    ppermute x6, waiting for transfers between devices: 5.01 us -> 16.9 us  [scatter_small(): lax.ppermute(pick(blocks, 1 - own, 0), 'dp', flip(size, bit))]
    convert_element_type x11 -> x3, other arithmetic: 17.5 us -> 5.62 us  [the longest x1 3.47 us: local(): jnp.concatenate([feed_a, feed_b], axis=0).astype(F32).reshape(3, width, -1)]
    ppermute x6, waiting for transfers between devices: 24.1 us -> 14.6 us  [exchange(): came.append(lax.ppermute(parts((me + s) % n), 'tensor', ring(n, s)))]
    unnamed x171 -> x156, local copies, waits for them, and re-layouts: 34.7 us -> 35.5 us
  transfers between devices with their start and end apart: 38 -> 20, of which waited for: 16 -> 9; matrix products, arithmetic and copies ran while one was open for 24% -> 20% of each run, Pallas kernels for 10% -> 61%
where the time goes in v4:
time: 588 us; the launch traced here: 578 us
  Pallas kernels  350 us (60%)
  local copies, waits for them, and re-layouts  61.1 us (10%)
  other arithmetic  34.6 us (6%)
  waiting for transfers between devices  33.3 us (6%)
  matrix products  32.9 us (6%)
  starting transfers between devices  25.7 us (4%)
  blocking collectives  24.8 us (4%)
  between operations  15.5 us (3%)
    pallas_call x1, Pallas kernels, feed_forward(): pl.pallas_call(partial(feed_kernel, n, dp, tile, cut), out_shape=(jax.Sha...  146 us
    pallas_call x1, Pallas kernels, tail(): pl.pallas_call(partial(tail_kernel, n, dp, tile, cut), out_shape=(jax.Sha...  138 us
    pallas_call x1, Pallas kernels, attention_backward(): pl.pallas_call(partial(backward_kernel, heads, block), grid=(groups,), ou...  41.2 us
    unnamed x156, local copies, waits for them, and re-layouts  35.5 us
    pallas_call x1, Pallas kernels, attention_forward(): pl.pallas_call(partial(forward_kernel, heads, block), grid=(groups,), out...  25.8 us
    all_gather x1, blocking collectives, local(): down_all = lax.all_gather(down_flat, 'tensor')  24.8 us
    ppermute x6, waiting for transfers between devices, scatter_small(): lax.ppermute(pick(blocks, 1 - own, 0), 'dp', flip(size, bit))  16.9 us
    ppermute x6, waiting for transfers between devices, exchange(): came.append(lax.ppermute(parts((me + s) % n), 'tensor', ring(n, s)))  14.6 us
  transfers between devices with their start and end apart: 20, of which 9 were waited for; matrix products, arithmetic and copies ran while one was open for 20% of the time, Pallas kernels for 61%

profile of v4, /device:TPU:12, one launch (start us, length us, event | category | flops | bytes accessed | tf_op | source)
XLA Modules:
  0.0 578.3 jit_solution(7207095531082061603)
XLA Ops:
  8.0 1.7 fusion.60
  9.6 1.7 fusion.45
  11.6 6.7 %copy.64 = bf16[2048,2,384]{0,2,1:T(8,128)(2,1)} copy(bf16[2048,2,384]{2,1,0:T(2,128)(2,1)S(1)} %copy-done.25) | data formatting | bytes 6291456 | tf_op args[4]
  18.8 3.3 fusion
  23.9 1.8 copy-done.15
  26.7 5.1 fusion.8.joined_ref
  31.8 25.8 %attention_forward.1 = (bf16[2,384,1024]{2,1,0:T(8,128)(2,1)S(1)}, bf16[2,256,1024]{2,1,0:T(8,128)(2,1)S(1)}, f32[2,4,1,1024]{3,2,1,0:T(1,128)S(1)}) custom-call(f32[2,384,1024]{2,1,0:T(8,128)} %fusion.8.joined_ref, f32[32,1024]{1,0:T(8,128)S(1)} %get-tuple-element.119.cos_ref, f32[32,1024]{1,0:T(8,128)S(1)} %get-tuple-element.118.sin_ref, ...), custom_call_target="tpu_custom_call" | custom-call | flops 22000001024 | bytes 10000000 | tf_op jit(solution)/shard_map/attention_forward/pallas_call | solution.py:121
  59.1 1.6 collective-permute-start
  62.3 2.1 collective-permute-start.2
  64.4 1.5 fusion.25
  66.1 4.0 fusion.34
  70.9 17.3 %copy.104 = bf16[2048,2,2048]{2,0,1:T(8,128)(2,1)} copy(bf16[2048,2,2048]{2,1,0:T(2,128)(2,1)} %param.24) | data formatting | bytes 33554432 | tf_op args[11]
  88.2 24.8 %all_gather.7 = bf16[4,8,512]{2,1,0:T(8,128)(2,1)S(1)} all-gather(bf16[1,8,512]{2,1,0:T(8,128)(2,1)S(1)} %all_gather_reshape.3), channel_id=1, replica_groups=mesh['dp'=8,'tensor'=4] {'tensor'}, dimensions={0}, use_global_device_ids=true | all-gather | bytes 40960 | tf_op jit(solution)/shard_map/all_gather | solution.py:1142
  115.4 1.3 copy.76
  116.7 6.3 %multiply_reduce_fusion = (f32[256]{0:T(256)S(1)}, f32[256,2048]{1,0:T(8,128)S(1)}) fusion(bf16[4,512,2048]{2,1,0:T(8,128)(2,1)} %bitcast.199, bf16[1,512,256]{1,2,0:T(8,128)(2,1)} %copy-done.28, bf16[1,512,256]{1,2,0:T(8,128)(2,1)} %copy-done.30, bf16[1,512,256]{1,2,0:T(8,128)(2,1)} %copy-done.32, bf16[1,512,256]{1,2,0:T(8,128)(2,1)S(1)} %get-tuple-element.106, ...), kind=kOutput, calls=%fused_computation.42 | convolution fusion | flops 2151153408 | bytes 12583940 | tf_op jit(solution)/shard_map/nct,ncd->td/dot_general | solution.py:1160
  123.0 1.4 multiply_convert_fusion.normed_in
  124.4 145.5 %feed_forward.1 = (bf16[256,2048]{1,0:T(8,128)(2,1)}, bf16[1024,2048]{1,0:T(8,128)(2,1)}, bf16[4,768,2048]{2,1,0:T(8,128)(2,1)}, bf16[2,384,2048]{2,1,0:T(8,128)...) custom-call(bf16[256,2048]{1,0:T(8,128)(2,1)} %multiply_convert_fusion.normed_in,, ...), custom_call_target="tpu_custom_call" | custom-call | flops 77309411328 | bytes 50331648 | tf_op jit(solution)/shard_map/feed_forward/pallas_call | solution.py:622
  269.9 2.1 fusion.22
  272.1 1.9 fusion.57
  274.0 6.1 %convolution_convert_fusion = bf16[4,512,256]{2,1,0:T(8,128)(2,1)S(1)} fusion(bf16[4,512,2048]{2,1,0:T(8,128)(2,1)} %bitcast.200, bf16[256,2048]{1,0:T(8,128)(2,1)S(1)} %fusion.57), kind=kOutput, calls=%fused_computation.45 | convolution fusion | flops 2148007936 | bytes 10485760 | tf_op jit(solution)/shard_map/ncd,td->nct/dot_general | solution.py:1174
  281.2 6.1 %collective-permute-start.4 = (bf16[512,256]{1,0:T(8,128)(2,1)}, bf16[512,256]{1,0:T(8,128)(2,1)}, u32[]{:S(2)}, u32[]{:S(2)}) collective-permute-start(bf16[512,256]{1,0:T(8,128)(2,1)} %get-tuple-element.104), channel_id=1, source_target_pairs={{0,2},{1,3},{2,0},{3,1},{4,6},{5,7},{6,4},{7,5},{8,10},{9,11},{10,... | collective-permute-start | bytes 786440 | tf_op jit(solution)/shard_map/ppermute | solution.py:1092
  289.5 2.7 convolution_bitcast_fusion.1
  292.4 1.5 collective-permute-start.8
  293.9 9.3 %collective-permute-done.4 = bf16[512,256]{1,0:T(8,128)(2,1)} collective-permute-done((bf16[512,256]{1,0:T(8,128)(2,1)}, bf16[512,256]{1,0:T(8,128)(2,1)}, u32[]{:S(2)}, u32[]{:S(2)}) %collective-permute-start.4) | collective-permute-done | bytes 262176 | tf_op jit(solution)/shard_map/ppermute | solution.py:1092
  303.8 5.0 collective-permute-done.5
  311.2 41.2 %attention_backward.1 = (bf16[2,384,1024]{2,1,0:T(8,128)(2,1)S(1)}, f32[2,5,64,64]{3,2,1,0:T(8,128)S(1)}) custom-call(bf16[2,384,1024]{2,1,0:T(8,128)(2,1)} %copy-done.12, f32[32,1024]{1,0:T(8,128)S(1)} %copy-done.8, f32[32,1024]{1,0:T(8,128)S(1)} %copy-done.6, bf16[2,320,64]{2,1,0:T(8,128)(2,1)S(1)} %bitcast.173, bf16[2,5,64,64]{3,2,1,0:T(8,128)(2,1)S(1)} %copy-done.10, ...), custom_call_target="tpu_custom_call" | custom-call | flops 40000000000 | bytes 10000000 | tf_op jit(solution)/shard_map/attention_backward/pallas_call | solution.py:214
  358.8 2.0 fusion.39
  363.7 9.9 %collective-permute-done.15 = f32[4,5888]{1,0:T(4,128)S(1)} collective-permute-done((f32[4,5888]{1,0:T(4,128)S(1)}, f32[4,5888]{1,0:T(4,128)S(1)}, u32[]{:S(2)}, u32[]{:S(2)}) %collective-permute-start.15) | collective-permute-done | bytes 94240 | tf_op jit(solution)/shard_map/ppermute | solution.py:1067
  373.7 1.6 collective-permute-start.16
  376.2 1.7 collective-permute-done.16
  378.0 3.1 fusion.6
  383.3 137.9 %gradient_sums.1 = (bf16[256,2048]{1,0:T(8,128)(2,1)}, bf16[384,2048]{1,0:T(8,128)(2,1)}, bf16[384,2048]{1,0:T(8,128)(2,1)}, bf16[256,512]{1,0:T(8,128)(2,1)}, b...) custom-call(bf16[768,1024]{1,0:T(8,128)(2,1)} %bitcast.169, bf16[768,2048]{1,0:T(8,128)(2,1)} %bitcast.201, ...), custom_call_target="tpu_custom_call" | custom-call | flops 99999997952 | bytes 41943040 | tf_op jit(solution)/shard_map/gradient_sums/pallas_call | solution.py:998
  521.2 2.9 fusion.24
  524.9 2.1 maximum_bitcast_fusion
  527.0 1.3 concatenate.72
  529.8 3.5 maximum_convert_fusion
  533.3 2.2 collective-permute-done.10
  535.6 1.5 collective-permute-start.11
  537.4 2.8 collective-permute-done.11
  541.6 5.8 collective-permute-start.13
  547.5 1.7 collective-permute-done.13
  549.3 1.8 collective-permute-start.14
  551.1 1.3 maximum_convert_fusion.1
  552.4 1.8 copy.88
  554.2 2.2 slice-done
  556.4 5.2 copy.105
  561.7 2.0 copy.87
  566.5 4.8 fusion.18
  (261 shorter events, 35.7 us)
Async XLA Ops:
  7.2 15.5 %copy-start = (bf16[3,8,2048]{2,1,0:T(8,128)(2,1)S(1)}, bf16[3,8,2048]{2,1,0:T(8,128)(2,1)}, u32[]{:S(2)}) copy-start(bf16[3,8,2048]{2,1,0:T(8,128)(2,1)} %param.18) | copy-start | bytes 294916
  7.2 109.5 %all-gather.2.cloned.1.call-start = ((), (), s32[]{:S(2)}) async-start(), calls=%async_computation.1 | async-start | bytes 8650752 | tf_op jit(solution)/shard_map/all_gather | solution.py:1083
  11.3 555.1 %reduce-scatter.2.cloned.1.call-start = ((), (), s32[]{:S(2)}) async-start(), calls=%async_computation.2 | async-start | bytes 5242880 | tf_op jit(solution)/shard_map/reduce_scatter | solution.py:1177
  18.7 13.1 %copy-start.3 = (bf16[2,64,320]{1,2,0:T(8,128)(2,1)}, bf16[2,64,320]{1,2,0:T(8,128)(2,1)S(1)}, u32[]{:S(2)}) copy-start(bf16[2,64,320]{1,2,0:T(8,128)(2,1)S(1)} %copy.68) | copy-start | bytes 245764
  23.9 248.2 %copy-start.42 = (f32[1,2048]{1,0:T(1,128)}, f32[1,2048]{1,0:T(1,128)S(1)}, u32[]{:S(2)}) copy-start(f32[1,2048]{1,0:T(1,128)S(1)} %get-tuple-element.116) | copy-start | bytes 24580
  59.1 53.9 %collective-permute-start = (bf16[512,256]{0,1:T(8,128)(2,1)S(1)}, bf16[512,256]{0,1:T(8,128)(2,1)}, u32[]{:S(2)}, u32[]{:S(2)}) collective-permute-start(bf16[512,256]{0,1:T(8,128)(2,1)S(1)} %copy.93), channel_id=1, source_target_pairs={{0,1},{1,2},{2,3},{3,0},{4,5},{5,6},{6,7},{7,4},{8,9},{9,10},{10,1... | collective-permute-start | bytes 786440 | tf_op jit(solution)/shard_map/ppermute | solution.py:1092
  60.9 52.2 %collective-permute-start.1 = (bf16[512,256]{0,1:T(8,128)(2,1)S(1)}, bf16[512,256]{0,1:T(8,128)(2,1)}, u32[]{:S(2)}, u32[]{:S(2)}) collective-permute-start(bf16[512,256]{0,1:T(8,128)(2,1)S(1)} %copy.94), channel_id=1, source_target_pairs={{0,2},{1,3},{2,0},{3,1},{4,6},{5,7},{6,4},{7,5},{8,10},{9,11},{10,... | collective-permute-start | bytes 786440 | tf_op jit(solution)/shard_map/ppermute | solution.py:1092
  62.3 50.8 %collective-permute-start.2 = (bf16[512,256]{0,1:T(8,128)(2,1)S(1)}, bf16[512,256]{0,1:T(8,128)(2,1)}, u32[]{:S(2)}, u32[]{:S(2)}) collective-permute-start(bf16[512,256]{0,1:T(8,128)(2,1)S(1)} %copy.95), channel_id=1, source_target_pairs={{0,3},{1,0},{2,1},{3,2},{4,7},{5,4},{6,5},{7,6},{8,11},{9,8},{10,9... | collective-permute-start | bytes 786440 | tf_op jit(solution)/shard_map/ppermute | solution.py:1092
  114.5 175.0 %copy-start.27 = (bf16[1,512,256]{1,2,0:T(8,128)(2,1)}, bf16[1,512,256]{1,2,0:T(8,128)(2,1)S(1)}, u32[]{:S(2)}) copy-start(bf16[1,512,256]{1,2,0:T(8,128)(2,1)S(1)} %get-tuple-element.106) | copy-start | bytes 786436
  116.7 266.6 %collective-permute-start.6 = (bf16[2048,256]{1,0:T(8,128)(2,1)}, bf16[2048,256]{1,0:T(8,128)(2,1)}, u32[]{:S(2)}, u32[]{:S(2)}) collective-permute-start(bf16[2048,256]{1,0:T(8,128)(2,1)} %bitcast.180), channel_id=1, source_target_pairs={{0,4},{4,0},{8,12},{12,8},{16,20},{20,16},{24,28},{28,24},{1,5},{5... | collective-permute-start | bytes 3145736 | tf_op jit(solution)/shard_map/ppermute | solution.py:1191
  123.0 149.0 %copy-start.13 = (f32[256,2048]{1,0:T(8,128)}, f32[256,2048]{1,0:T(8,128)S(1)}, u32[]{:S(2)}) copy-start(f32[256,2048]{1,0:T(8,128)S(1)} %get-tuple-element.121) | copy-start | bytes 6291460
  123.0 149.0 %copy-start.60 = (f32[256]{0:T(256)}, f32[256]{0:T(256)S(1)}, u32[]{:S(2)}) copy-start(f32[256]{0:T(256)S(1)} %add_rsqrt_fusion.2) | copy-start | bytes 3076
  274.0 13.6 %copy-start.23 = (bf16[256,2048]{1,0:T(8,128)(2,1)}, bf16[256,2048]{1,0:T(8,128)(2,1)S(1)}, u32[]{:S(2)}) copy-start(bf16[256,2048]{1,0:T(8,128)(2,1)S(1)} %fusion.57) | copy-start | bytes 3145732
  281.1 11.3 %collective-permute-start.3 = (bf16[512,256]{1,0:T(8,128)(2,1)}, bf16[512,256]{1,0:T(8,128)(2,1)}, u32[]{:S(2)}, u32[]{:S(2)}) collective-permute-start(bf16[512,256]{1,0:T(8,128)(2,1)} %get-tuple-element.105), channel_id=1, source_target_pairs={{0,1},{1,2},{2,3},{3,0},{4,5},{5,6},{6,7},{7,4},{8,9},{9,10},{10,1... | collective-permute-start | bytes 786440 | tf_op jit(solution)/shard_map/ppermute | solution.py:1092
  281.2 22.1 %collective-permute-start.4 = (bf16[512,256]{1,0:T(8,128)(2,1)}, bf16[512,256]{1,0:T(8,128)(2,1)}, u32[]{:S(2)}, u32[]{:S(2)}) collective-permute-start(bf16[512,256]{1,0:T(8,128)(2,1)} %get-tuple-element.104), channel_id=1, source_target_pairs={{0,2},{1,3},{2,0},{3,1},{4,6},{5,7},{6,4},{7,5},{8,10},{9,11},{10,... | collective-permute-start | bytes 786440 | tf_op jit(solution)/shard_map/ppermute | solution.py:1092
  287.2 21.6 %collective-permute-start.5 = (bf16[512,256]{1,0:T(8,128)(2,1)}, bf16[512,256]{1,0:T(8,128)(2,1)}, u32[]{:S(2)}, u32[]{:S(2)}) collective-permute-start(bf16[512,256]{1,0:T(8,128)(2,1)} %get-tuple-element.103), channel_id=1, source_target_pairs={{0,3},{1,0},{2,1},{3,2},{4,7},{5,4},{6,5},{7,6},{8,11},{9,8},{10,9... | collective-permute-start | bytes 786440 | tf_op jit(solution)/shard_map/ppermute | solution.py:1092
  289.4 93.8 %collective-permute-start.7 = (bf16[256,1024]{1,0:T(8,128)(2,1)}, bf16[256,1024]{1,0:T(8,128)(2,1)}, u32[]{:S(2)}, u32[]{:S(2)}) collective-permute-start(bf16[256,1024]{1,0:T(8,128)(2,1)} %pad_maximum_fusion.5), channel_id=1, source_target_pairs={{0,4},{4,0},{8,12},{12,8},{16,20},{20,16},{24,28},{28,24},{1,5},{5... | collective-permute-start | bytes 1572872 | tf_op jit(solution)/shard_map/ppermute | solution.py:1193
  292.4 90.8 %collective-permute-start.8 = (bf16[2,384,2048]{2,1,0:T(8,128)(2,1)}, bf16[2,384,2048]{2,1,0:T(8,128)(2,1)}, u32[]{:S(2)}, u32[]{:S(2)}) collective-permute-start(bf16[2,384,2048]{2,1,0:T(8,128)(2,1)} %get-tuple-element.36), channel_id=1, source_target_pairs={{0,8},{4,12},{8,0},{12,4},{16,24},{20,28},{24,16},{28,20},{1,9},{5... | collective-permute-start | bytes 9437192 | tf_op jit(solution)/shard_map/ppermute | solution.py:1199
  303.3 80.0 %collective-permute-start.9 = (bf16[2,384,2048]{2,1,0:T(8,128)(2,1)}, bf16[2,384,2048]{2,1,0:T(8,128)(2,1)}, u32[]{:S(2)}, u32[]{:S(2)}) collective-permute-start(bf16[2,384,2048]{2,1,0:T(8,128)(2,1)} %get-tuple-element.38), channel_id=1, source_target_pairs={{0,16},{4,20},{8,24},{12,28},{16,0},{20,4},{24,8},{28,12},{1,17},{... | collective-permute-start | bytes 9437192 | tf_op jit(solution)/shard_map/ppermute | solution.py:1200
  311.2 41.2 %copy-start.55 = (bf16[1024,3,8]{0,2,1:T(8,128)(2,1)S(1)}, bf16[1024,3,8]{0,2,1:T(8,128)(2,1)}, u32[]{:S(2)}) copy-start(bf16[1024,3,8]{0,2,1:T(8,128)(2,1)} %fusion.34) | copy-start | bytes 147460
  352.4 25.6 %copy-start.2 = (bf16[2,384,1024]{2,1,0:T(8,128)(2,1)}, bf16[2,384,1024]{2,1,0:T(8,128)(2,1)S(1)}, u32[]{:S(2)}) copy-start(bf16[2,384,1024]{2,1,0:T(8,128)(2,1)S(1)} %get-tuple-element.34) | copy-start | bytes 4718596
  358.2 15.3 %collective-permute-start.15 = (f32[4,5888]{1,0:T(4,128)S(1)}, f32[4,5888]{1,0:T(4,128)S(1)}, u32[]{:S(2)}, u32[]{:S(2)}) collective-permute-start(f32[4,5888]{1,0:T(4,128)S(1)} %dynamic-slice_bitcast_fusion.4), channel_id=1, source_target_pairs={{0,16},{4,20},{8,24},{12,28},{16,0},{20,4},{24,8},{28,12},{1,17},{... | collective-permute-start | bytes 282632 | tf_op jit(solution)/shard_map/ppermute | solution.py:1067
  363.6 10.0 %copy-start.41 = (f32[2,4,5888]{2,1,0:T(4,128)S(1)}, f32[2,4,5888]{2,1,0:T(4,128)}, u32[]{:S(2)}) copy-start(f32[2,4,5888]{2,1,0:T(4,128)} %constant_dynamic-update-slice_fusion.2) | copy-start | bytes 565252
  363.6 11.7 %copy-start.36 = (bf16[256,256]{1,0:T(8,128)(2,1)S(1)}, bf16[256,256]{1,0:T(8,128)(2,1)}, u32[]{:S(2)}) copy-start(bf16[256,256]{1,0:T(8,128)(2,1)} %get-tuple-element.94) | copy-start | bytes 393220
  363.6 11.7 %copy-start.37 = (bf16[256,256]{1,0:T(8,128)(2,1)S(1)}, bf16[256,256]{1,0:T(8,128)(2,1)}, u32[]{:S(2)}) copy-start(bf16[256,256]{1,0:T(8,128)(2,1)} %get-tuple-element.95) | copy-start | bytes 393220
  363.6 11.7 %copy-start.38 = (bf16[256,256]{1,0:T(8,128)(2,1)S(1)}, bf16[256,256]{1,0:T(8,128)(2,1)}, u32[]{:S(2)}) copy-start(bf16[256,256]{1,0:T(8,128)(2,1)} %get-tuple-element.96) | copy-start | bytes 393220
  363.6 11.7 %copy-start.39 = (bf16[256,256]{1,0:T(8,128)(2,1)S(1)}, bf16[256,256]{1,0:T(8,128)(2,1)}, u32[]{:S(2)}) copy-start(bf16[256,256]{1,0:T(8,128)(2,1)} %get-tuple-element.97) | copy-start | bytes 393220
  363.6 14.4 %copy-start.50 = (bf16[1,8,2,384]{3,1,0,2:T(8,128)(2,1)S(1)}, bf16[1,8,2,384]{3,1,0,2:T(8,128)(2,1)}, u32[]{:S(2)}) copy-start(bf16[1,8,2,384]{3,1,0,2:T(8,128)(2,1)} %copy-done.49) | copy-start | bytes 36868
  363.6 14.4 %copy-start.52 = (bf16[1,8,2,384]{3,1,0,2:T(8,128)(2,1)S(1)}, bf16[1,8,2,384]{3,1,0,2:T(8,128)(2,1)}, u32[]{:S(2)}) copy-start(bf16[1,8,2,384]{3,1,0,2:T(8,128)(2,1)} %copy-done.51) | copy-start | bytes 36868
  363.6 14.4 %copy-start.54 = (bf16[1,8,2,384]{3,1,0,2:T(8,128)(2,1)S(1)}, bf16[1,8,2,384]{3,1,0,2:T(8,128)(2,1)}, u32[]{:S(2)}) copy-start(bf16[1,8,2,384]{3,1,0,2:T(8,128)(2,1)} %copy-done.53) | copy-start | bytes 36868
  373.7 4.1 collective-permute-start.16
  377.9 3.7 collective-permute-start.17
  383.2 137.9 %copy-start.47 = (f32[1,2048]{1,0:T(1,128)S(1)}, f32[1,2048]{1,0:T(1,128)}, u32[]{:S(2)}) copy-start(f32[1,2048]{1,0:T(1,128)} %copy-done.46) | copy-start | bytes 24580
  383.3 137.9 %copy-start.62 = (f32[256]{0:T(256)S(1)}, f32[256]{0:T(256)}, u32[]{:S(2)}) copy-start(f32[256]{0:T(256)} %add_rsqrt_fusion.1) | copy-start | bytes 3076
  529.2 6.3 %collective-permute-start.10 = (f32[4,4,2688]{2,1,0:T(4,128)S(1)}, f32[4,4,2688]{2,1,0:T(4,128)S(1)}, u32[]{:S(2)}, u32[]{:S(2)}) collective-permute-start(f32[4,4,2688]{2,1,0:T(4,128)S(1)} %dynamic-slice_bitcast_fusion.3), channel_id=1, source_target_pairs={{0,16},{4,20},{8,24},{12,28},{16,0},{20,4},{24,8},{28,12},{1,17},{... | collective-permute-start | bytes 516104 | tf_op jit(solution)/shard_map/ppermute | solution.py:1067
  535.6 11.8 %copy-start.66 = (f32[256]{0:T(256)S(1)}, f32[256]{0:T(256)}, u32[]{:S(2)}) copy-start(f32[256]{0:T(256)} %get-tuple-element.83) | copy-start | bytes 3076
  535.6 11.8 %copy-start.45 = (bf16[128,768]{1,0:T(8,128)(2,1)S(1)}, bf16[128,768]{1,0:T(8,128)(2,1)}, u32[]{:S(2)}) copy-start(bf16[128,768]{1,0:T(8,128)(2,1)} %get-tuple-element.40) | copy-start | bytes 589828
  535.6 11.8 %copy-start.44 = (bf16[128,768]{1,0:T(8,128)(2,1)S(1)}, bf16[128,768]{1,0:T(8,128)(2,1)}, u32[]{:S(2)}) copy-start(bf16[128,768]{1,0:T(8,128)(2,1)} %get-tuple-element.41) | copy-start | bytes 589828
  535.6 4.6 collective-permute-start.11
  540.2 1.3 collective-permute-start.12
  541.6 7.6 %collective-permute-start.13 = (f32[2,2688]{1,0:T(2,128)S(1)}, f32[2,2688]{1,0:T(2,128)S(1)}, u32[]{:S(2)}, u32[]{:S(2)}) collective-permute-start(f32[2,2688]{1,0:T(2,128)S(1)} %dynamic-slice_bitcast_fusion.7), channel_id=1, source_target_pairs={{0,2},{1,3},{2,0},{3,1},{4,6},{5,7},{6,4},{7,5},{8,10},{9,11},{10,... | collective-permute-start | bytes 64520 | tf_op jit(solution)/shard_map/ppermute | solution.py:1074
  549.3 14.4 %collective-permute-start.14 = (f32[1,2688]{1,0:T(1,128)S(1)}, f32[1,2688]{1,0:T(1,128)S(1)}, u32[]{:S(2)}, u32[]{:S(2)}) collective-permute-start(f32[1,2688]{1,0:T(1,128)S(1)} %constant_dynamic-slice_fusion.1), channel_id=1, source_target_pairs={{0,1},{1,0},{2,3},{3,2},{4,5},{5,4},{6,7},{7,6},{8,9},{9,8},{10,11... | collective-permute-start | bytes 32264 | tf_op jit(solution)/shard_map/ppermute | solution.py:1074
  556.4 10.1 %copy-start.14 = (f32[256,2048]{1,0:T(8,128)S(1)}, f32[256,2048]{1,0:T(8,128)}, u32[]{:S(2)}) copy-start(f32[256,2048]{1,0:T(8,128)} %copy-done.13) | copy-start | bytes 6291460
  556.4 10.1 %copy-start.18 = (bf16[256,2048]{1,0:T(8,128)(2,1)S(1)}, bf16[256,2048]{1,0:T(8,128)(2,1)}, u32[]{:S(2)}) copy-start(bf16[256,2048]{1,0:T(8,128)(2,1)} %get-tuple-element.31) | copy-start | bytes 3145732
  556.4 10.1 %copy-start.43 = (f32[1,2048]{1,0:T(1,128)S(1)}, f32[1,2048]{1,0:T(1,128)}, u32[]{:S(2)}) copy-start(f32[1,2048]{1,0:T(1,128)} %copy-done.42) | copy-start | bytes 24580
  556.4 10.1 %copy-start.61 = (f32[256]{0:T(256)S(1)}, f32[256]{0:T(256)}, u32[]{:S(2)}) copy-start(f32[256]{0:T(256)} %copy-done.60) | copy-start | bytes 3076
  556.4 10.1 %copy-start.63 = (f32[256]{0:T(256)S(1)}, f32[256]{0:T(256)}, u32[]{:S(2)}) copy-start(f32[256]{0:T(256)} %add_rsqrt_fusion.1) | copy-start | bytes 3076
  556.4 10.1 %copy-start.65 = (f32[256]{0:T(256)S(1)}, f32[256]{0:T(256)}, u32[]{:S(2)}) copy-start(f32[256]{0:T(256)} %copy-done.64) | copy-start | bytes 3076
  (42 other events, 176.3 us)
Sparse Core Ops, SparseCore 0:
  11.5 94.4 all-gather.1
  363.8 116.3 reduce-scatter.1

commit v5 on v4

--- a/solution.py
+++ b/solution.py
@@ -665,11 +665,11 @@
 
 def tail_kernel(
     n, dp, tile, cut,
-    joined_in, w_in, normed_in, att_in, att_mate_in, grad_in, grad_mate_in, fa_keep, fa_came, fb_keep, fb_came,
-    sum_out, feed_a, feed_b, branch_out, qkv_a, qkv_b,
+    joined_in, w_in, normed_in, att_in, att_mate_in, grad_in, grad_mate_in, fa_keep, fa_came, fb_keep, fb_came, small_in,
+    sum_out, feed_a, feed_b, branch_out, qkv_a, qkv_b, small_out, own_out,
     joined, w, normed, att, att_mate, grad, grad_mate, arriving, sending,
-    fa, fa2, fb, fb2, f_recvs, wm, w_recvs, w_done, w_last, qo, qm, qc, q_recvs,
-    load_sems, out_sems, sum_send, sum_recv, f_sems, w_sems, q_sems, core_sems, last_send, last_recv,
+    fa, fa2, fb, fb2, small, small_recvs, small_came, small_total, f_recvs, wm, w_recvs, w_done, w_last, qo, qm, qc, q_recvs,
+    load_sems, out_sems, sum_send, sum_recv, f_sems, w_sems, q_sems, core_sems, last_send, last_recv, small_sems, few_send, few_recv,
 ):
     width = w.shape[1]
     joined_width, tokens = joined.shape
@@ -699,7 +699,7 @@
         pl.semaphore_signal(barrier, inc=1, device_id=mate(bit), device_id_type=mesh_id)
 
     pairs = (
-        (joined_in, joined), (w_in, w), (att_in, att), (att_mate_in, att_mate), (grad_in, grad),
+        (small_in, small), (joined_in, joined), (w_in, w), (att_in, att), (att_mate_in, att_mate), (grad_in, grad),
         (grad_mate_in, grad_mate), (normed_in, normed), (fa_keep, fa), (fa_came, fa2), (fb_keep, fb), (fb_came, fb2),
     )
     loads = [pltpu.make_async_copy(a, b, load_sems.at[i]) for i, (a, b) in enumerate(pairs)]
@@ -724,35 +724,7 @@
         rows = pl.ds(pl.multiple_of(slot * share + q * piece, 16), piece)
         return pltpu.make_async_copy(arriving.at[rows], arriving.at[rows], sum_recv.at[way, j * cut + q])
 
-    loads[0].wait()
-    loads[1].wait()
-    for k in range(n):
-        distance = n - 1 - k
-        for way in range(2):
-            j = me + distance if way == 0 else me - distance
-            there = (j < n) if way == 0 else (j >= 0)
-            if distance == 0 and way:
-                continue
-
-            @pl.when(there)
-            def _(j=j, way=way, distance=distance):
-                rows = rows_of(j)
-
-                @pl.loop(0, width // tile)
-                def _(d):
-                    span = pl.ds(pl.multiple_of(d * tile, tile), tile)
-                    sending[rows, span] = lax.dot_general(
-                        joined[:, pl.ds(pl.multiple_of(j * share, 128), share)], w[:, span],
-                        (((0,), (0,)), ((), ())), preferred_element_type=F32).astype(BF16)
-
-                if distance:
-
-                    @pl.when(place[way] == 0)
-                    def _():
-                        for q in range(cut):
-                            pass_on(way, j, q).start()
-
-    def halving(cur, parts, recvs, sems, stream, order):
+    def halving(cur, recvs, sems, stream, order):
         steps = []
         current = cur
         for step, bit in enumerate(order):
@@ -785,7 +757,7 @@
                     @pl.loop(0, total // rows)
                     def _(r):
                         span = pl.ds(pl.multiple_of(r * rows, 16), rows)
-                        room[slot, span, :] = (kept[span, :].astype(F32) + room[slot, span, :].astype(F32)).astype(BF16)
+                        room[slot, span, :] = (kept[span, :].astype(F32) + room[slot, span, :].astype(F32)).astype(room.dtype)
 
             def settle(copies=copies):
                 for copy in copies:
@@ -795,22 +767,59 @@
             current = lambda i, room=room: room.at[i]
         return steps
 
+    loads[0].wait()
+    small_steps = halving(lambda i: small.at[i], [None, small_recvs], small_sems, 1, list(range(bits))[::-1])
+    small_steps[0][0]()
+    loads[1].wait()
+    loads[2].wait()
+    for k in range(n):
+        distance = n - 1 - k
+        for way in range(2):
+            j = me + distance if way == 0 else me - distance
+            there = (j < n) if way == 0 else (j >= 0)
+            if distance == 0 and way:
+                continue
+
+            @pl.when(there)
+            def _(j=j, way=way, distance=distance):
+                rows = rows_of(j)
+
+                @pl.loop(0, width // tile)
+                def _(d):
+                    span = pl.ds(pl.multiple_of(d * tile, tile), tile)
+                    sending[rows, span] = lax.dot_general(
+                        joined[:, pl.ds(pl.multiple_of(j * share, 128), share)], w[:, span],
+                        (((0,), (0,)), ((), ())), preferred_element_type=F32).astype(BF16)
+
+                if distance:
+
+                    @pl.when(place[way] == 0)
+                    def _():
+                        for q in range(cut):
+                            pass_on(way, j, q).start()
+
     rest = list(range(1, bits))
     half_rows = block // 2
     w_steps = [
-        halving(lambda i, s=s: wm.at[i, pl.ds(s * half_rows, half_rows)], dp // 2, w_recvs, w_sems, s, order)
+        halving(lambda i, s=s: wm.at[i, pl.ds(s * half_rows, half_rows)], w_recvs, w_sems, s, order)
         for s, order in enumerate((rest, rest[::-1]))
     ]
     q_steps = [
-        halving(lambda i, s=s: qm.at[i, pl.ds(s * half_rows, half_rows)], dp // 2, q_recvs, q_sems, s, order)
+        halving(lambda i, s=s: qm.at[i, pl.ds(s * half_rows, half_rows)], q_recvs, q_sems, s, order)
         for s, order in enumerate((rest, rest[::-1]))
     ]
     f_steps = [
-        halving(lambda i, ref=ref: ref.at[i], dp // 4, f_recvs, f_sems, s, order[1:])
+        halving(lambda i, ref=ref: ref.at[i], f_recvs, f_sems, s, order[1:])
         for s, (ref, order) in enumerate(((fa, rest), (fb, rest[::-1])))
     ]
 
-    for load in loads[2:6]:
+    def next_small(step):
+        small_steps[step][1]()
+        if step + 1 < bits:
+            small_steps[step + 1][0]()
+
+    next_small(0)
+    for load in loads[3:7]:
         load.wait()
 
     @pl.loop(0, dp // 2)
@@ -823,7 +832,7 @@
     for s in range(2):
         w_steps[s][0][0]()
 
-    loads[6].wait()
+    loads[7].wait()
 
     def across(q):
         return pltpu.make_async_remote_copy(
@@ -849,7 +858,9 @@
     for s in range(2):
         q_steps[s][0][0]()
 
-    for load in loads[7:]:
+    for step in range(1, bits):
+        next_small(step)
+    for load in loads[8:]:
         load.wait()
     for one, other in ((fa, fa2), (fb, fb2)):
         for i in range(dp // 4):
@@ -875,6 +886,20 @@
                 sending[rows, :] = (sending[rows, :].astype(F32) + arriving[rows, :].astype(F32)).astype(BF16)
                 pass_on(way, j, q).start()
 
+    few = small_total.shape[0]
+
+    def deliver_small(s):
+        goal = lax.rem(me + s, n)
+        return pltpu.make_async_remote_copy(
+            src_ref=small_recvs[bits - 1].at[0, pl.ds(pl.multiple_of(goal * few, 8), few)],
+            dst_ref=small_came.at[s - 1], send_sem=few_send.at[s - 1], recv_sem=few_recv.at[s - 1],
+            device_id={"tensor": goal}, device_id_type=mesh_id)
+
+    for s in range(1, n):
+        deliver_small(s).start()
+    own_copy = pltpu.make_async_copy(
+        small_recvs[bits - 1].at[0, pl.ds(n * few, own_out.shape[0])], own_out, out_sems.at[6])
+    own_copy.start()
     last_step = cut * (n - 2) + n - 1
     first = 1 + cut
     pl.loop(1, first)(serve)
@@ -934,6 +959,14 @@
     branch = pltpu.make_async_copy(w_last.at[n - 1], branch_out, out_sems.at[4])
     branch.start()
 
+    total = small_recvs[bits - 1][0, pl.ds(pl.multiple_of(me * few, 8), few), :]
+    for s in range(1, n):
+        deliver_small(s).wait_recv()
+        total = total + small_came[s - 1]
+    small_total[...] = total
+    few_copy = pltpu.make_async_copy(small_total, small_out, out_sems.at[7])
+    few_copy.start()
+
     for way in range(2):
 
         @pl.when(place[way] > 0)
@@ -952,13 +985,14 @@
 
     final = pltpu.make_async_copy(sending.at[rows_of(me)], sum_out, out_sems.at[5])
     final.start()
-    for copy in (*q_outs, *f_outs, branch, final):
+    for copy in (*q_outs, *f_outs, branch, final, own_copy, few_copy):
         copy.wait()
-    for steps in (*w_steps, *q_steps, *f_steps):
+    for steps in (*w_steps, *q_steps, *f_steps, small_steps):
         for _, _, settle in steps:
             settle()
     for s in range(1, n):
         deliver(s).wait_send()
+        deliver_small(s).wait_send()
 
     @pl.loop(0, dp // 2)
     def _(q):
@@ -978,7 +1012,7 @@
                         pass_on(way, j, q).wait_send()
 
 
-def tail(joined, w, normed, att, att_mate, grad, grad_mate, feed, n, dp, tile=512, cut=4):
+def tail(joined, w, normed, att, att_mate, grad, grad_mate, feed, small, few, n, dp, tile=512, cut=4):
     joined_width, tokens = joined.shape
     width = w.shape[1]
     share = tokens // n
@@ -1004,14 +1038,20 @@
             jax.ShapeDtypeStruct((block, columns // n), BF16),
             jax.ShapeDtypeStruct((half, joined_width), BF16),
             jax.ShapeDtypeStruct((half, joined_width), BF16),
+            jax.ShapeDtypeStruct((few, small.shape[2]), F32),
+            jax.ShapeDtypeStruct((small.shape[1] - n * few, small.shape[2]), F32),
         ),
-        in_specs=[anywhere] * 11,
-        out_specs=(anywhere,) * 6,
+        in_specs=[anywhere] * 12,
+        out_specs=(anywhere,) * 8,
         scratch_shapes=[
             like(joined), like(w), like(normed), like(att), like(att_mate), like(grad), like(grad_mate),
             pltpu.VMEM((tokens + share, width), BF16),
             pltpu.VMEM((tokens, width), BF16),
             like(feed[0]), like(feed[1]), like(feed[2]), like(feed[3]),
+            pltpu.VMEM(small.shape, F32),
+            [pltpu.VMEM((1 << (steps - step),) + small.shape[1:], F32) for step in range(steps + 1)],
+            pltpu.VMEM((n - 1, few, small.shape[2]), F32),
+            pltpu.VMEM((few, small.shape[2]), F32),
             rooms(feed_rows, hidden, steps - 1),
             pltpu.VMEM((dp // 2, block, columns), BF16),
             rooms(half, columns, steps),
@@ -1021,8 +1061,8 @@
             pltpu.VMEM((dp // 2, block, joined_width), BF16),
             pltpu.VMEM((dp // 2, block, joined_width), BF16),
             rooms(half, joined_width, steps),
-            pltpu.SemaphoreType.DMA((11,)),
-            pltpu.SemaphoreType.DMA((6,)),
+            pltpu.SemaphoreType.DMA((12,)),
+            pltpu.SemaphoreType.DMA((8,)),
             pltpu.SemaphoreType.DMA((2, n * cut)),
             pltpu.SemaphoreType.DMA((2, n * cut)),
             pltpu.SemaphoreType.DMA((2, 2, steps, dp // 4)),
@@ -1031,12 +1071,15 @@
             pltpu.SemaphoreType.DMA((2, dp // 2)),
             pltpu.SemaphoreType.DMA((n - 1,)),
             pltpu.SemaphoreType.DMA((n - 1,)),
+            pltpu.SemaphoreType.DMA((2, 2, steps + 1, dp // 2)),
+            pltpu.SemaphoreType.DMA((n - 1,)),
+            pltpu.SemaphoreType.DMA((n - 1,)),
         ],
         compiler_params=pltpu.CompilerParams(
             collective_id=1, has_side_effects=True, vmem_limit_bytes=60 * 2**20),
-        cost_estimate=pl.CostEstimate(flops=100 * 10**9, bytes_accessed=40 * 2**20, transcendentals=0),
+        cost_estimate=pl.CostEstimate(flops=10**6, bytes_accessed=10**5, transcendentals=0),
         name="gradient_sums",
-    )(joined, w, normed, att, att_mate, grad, grad_mate, *feed)
+    )(joined, w, normed, att, att_mate, grad, grad_mate, *feed, small)
 
 
 def ring(size, shift=1):
@@ -1057,25 +1100,6 @@
 
 def bits_of(size):
     return size.bit_length() - 1
-
-
-def scatter_small(blocks, over_tensor):
-    size = lax.axis_size("dp")
-    for bit in reversed(range(bits_of(size))):
-        own = (lax.axis_index("dp") >> bit) & 1
-        blocks = blocks.reshape((2, blocks.shape[0] // 2) + blocks.shape[1:])
-        blocks = pick(blocks, own, 0) + lax.ppermute(pick(blocks, 1 - own, 0), "dp", flip(size, bit))
-    blocks = blocks[0]
-    if over_tensor:
-        size = lax.axis_size("tensor")
-        for bit in reversed(range(bits_of(size))):
-            own = (lax.axis_index("tensor") >> bit) & 1
-            blocks = blocks.reshape((2, blocks.shape[0] // 2) + blocks.shape[1:])
-            blocks = pick(blocks, own, 0) + lax.ppermute(
-                pick(blocks, 1 - own, 0), "tensor", flip(size, bit)
-            )
-        blocks = blocks[0]
-    return blocks
 
 
 def gather_weight(shard):
@@ -1174,13 +1198,48 @@
     grad_att_share = dot("ncd,td->nct", all_branch, grad_branch).astype(BF16)
     back = by_place(exchange(lambda j: pick(grad_att_share, j, 0), 1))
     grad_attended = jnp.concatenate(back, axis=1).reshape(groups, query_width, token_rows)
-    mixed = lax.psum_scatter(mixed_parts, "tensor", scatter_dimension=0, tiled=True).astype(F32)
-    output = (hidden + mixed).astype(BF16)
+    mixed_parts, grad_attended = lax.optimization_barrier((mixed_parts, grad_attended))
+    mixed_came = exchange(lambda j: chunk_of(mixed_parts, j, share, 0), 1)
 
     grad_joined, grad_maps = attention_backward(
         low, cosines, sines, maps_t, maps, seg_row, seg_col, attended, root, grad_attended, heads
     )
     flat_joined = grad_joined.reshape(groups * joined_width, token_rows)
+    near = [part for s, part in enumerate(mixed_came) if s != n // 2]
+    flat_joined, near = lax.optimization_barrier((flat_joined, near))
+    mixed = sum(part.astype(F32) for part in (*near, mixed_came[n // 2]))
+    lowrank_low = lowrank.astype(BF16)
+    grad_up = jnp.concatenate(
+        [dot("tr,kct->rkc", lowrank_low[:, j], grad_joined[:, a:b]) for j, (a, b) in enumerate(edges)],
+        axis=2,
+    )
+    grad_maps = jnp.transpose(grad_maps, (0, 2, 1, 3)).reshape(groups, HEAD_SIZE, -1)
+    small = jnp.concatenate(
+        [
+            jnp.moveaxis(grad_up.reshape(rank, groups, dp, -1), 2, 0).reshape(dp, -1),
+            jnp.moveaxis(grad_maps.reshape(groups, HEAD_SIZE, dp, -1), 2, 0).reshape(dp, -1),
+        ],
+        axis=1,
+    )
+    grad_lowrank = dot("kct,jrkc->jrt", grad_joined, up_wide).astype(BF16)
+    grad_qkv_down = dot("jrt,td->jrd", grad_lowrank, normed_one)
+    grad_lowrank_out = dot("td,rd->tr", grad_branch, o_up).astype(BF16)
+    grad_o_up = dot("tr,td->rd", lowrank_out.astype(BF16), grad_branch)
+    grad_o_down = dot("tr,nct->nrc", grad_lowrank_out, att_share)
+    gain_one = jnp.sum(dot("ct,cd->td", flat_joined, w_joined) * normed_one.astype(F32), axis=0)
+    shared = jnp.concatenate(
+        [gain_one[None] / gains[:1], gain_two[None], grad_qkv_down.reshape(-1, model_width), grad_o_up], axis=0
+    )
+    lines = shared.shape[0]
+    shared = jnp.transpose(shared.reshape(lines, dp, n, -1), (1, 2, 0, 3)).reshape(dp, n, -1)
+    downs = grad_o_down.reshape(n, rank, groups, dp, -1)
+    downs = jnp.transpose(downs, (3, 0, 1, 2, 4)).reshape(dp, n, -1)
+    packed = jnp.concatenate([shared, downs], axis=2)
+    few = -(-packed.shape[2] // 1024) * 8
+    packed = jnp.pad(packed, ((0, 0), (0, 0), (0, few * 128 - packed.shape[2]))).reshape(dp, n * few, 128)
+    tall = -(-small.shape[1] // 1024) * 8
+    small = jnp.pad(small, ((0, 0), (0, tall * 128 - small.shape[1]))).reshape(dp, tall, 128)
+    packed = jnp.concatenate([packed, small], axis=1)
     width = model_width // dp
     core = lax.axis_index("dp") & 1
 
@@ -1193,15 +1252,24 @@
     branch_mate = lax.ppermute(of_core(grad_branch, 1 - core), "dp", flip(dp, 0))
     first_send, first_keep, second_send, second_keep = grads_feed
     rest = list(range(1, bits_of(dp)))
-    grad_normed_one, feed_a, feed_b, out_branch, qkv_a, qkv_b = tail(
+    grad_normed_one, feed_a, feed_b, out_branch, qkv_a, qkv_b, few_small, own_small = tail(
         flat_joined, w_joined, normed_one, flat_att, att_mate, branch_own, branch_mate,
         (
             first_keep, lax.ppermute(first_send, "dp", flip(dp, rest[0])),
             second_keep, lax.ppermute(second_send, "dp", flip(dp, rest[-1])),
         ),
-        n, dp,
-    )
+        packed, few, n, dp,
+    )
+    own_small = own_small.reshape(-1)
+    cut = rank * groups * (joined_width // dp)
+    out_up = own_small[:cut].reshape(rank, groups, -1)
+    out_maps = own_small[cut:cut + groups * HEAD_SIZE * (feature_maps.shape[2] // dp)].reshape(groups, HEAD_SIZE, -1)
+    few_small = few_small.reshape(-1)
+    cut = lines * (model_width // (dp * n))
+    shared = few_small[:cut].reshape(lines, -1)
+    out_o_down = few_small[cut:cut + rank * groups * (query_width // dp)].reshape(rank, groups, -1)
     grad_normed_one = grad_normed_one.astype(F32)
+    output = (hidden + mixed).astype(BF16)
     scaled_one, inverse_one, _ = normalize(tokens_share, gains[0])
     weighted = grad_normed_one * gains[0]
     grad_input = (
@@ -1209,48 +1277,12 @@
         + inverse_one
         * (weighted - scaled_one * jnp.mean(weighted * scaled_one, axis=-1, keepdims=True))
     ).astype(BF16)
-    gain_one = jnp.sum(grad_normed_one * scaled_one, axis=0)
-
     out_feed = jnp.concatenate([feed_a, feed_b], axis=0).astype(F32).reshape(3, width, -1)
     out_gate_up = jnp.transpose(out_feed[:2], (1, 0, 2))
     out_down = out_feed[2].T
     out_branch = out_branch.T.astype(F32)
     out_qkv = jnp.concatenate([qkv_a, qkv_b], axis=0).astype(F32).reshape(width, groups, joined_width)
 
-    lowrank_low = lowrank.astype(BF16)
-    grad_up = jnp.concatenate(
-        [dot("tr,kct->rkc", lowrank_low[:, j], grad_joined[:, a:b]) for j, (a, b) in enumerate(edges)],
-        axis=2,
-    )
-    grad_maps = jnp.transpose(grad_maps, (0, 2, 1, 3)).reshape(groups, HEAD_SIZE, -1)
-    small = jnp.concatenate(
-        [
-            jnp.moveaxis(grad_up.reshape(rank, groups, dp, -1), 2, 0).reshape(dp, -1),
-            jnp.moveaxis(grad_maps.reshape(groups, HEAD_SIZE, dp, -1), 2, 0).reshape(dp, -1),
-        ],
-        axis=1,
-    )
-    small = scatter_small(small, False)
-    cut = rank * groups * (joined_width // dp)
-    out_up = small[:cut].reshape(rank, groups, -1)
-    out_maps = small[cut:].reshape(groups, HEAD_SIZE, -1)
-
-    grad_lowrank = dot("kct,jrkc->jrt", grad_joined, up_wide).astype(BF16)
-    grad_qkv_down = dot("jrt,td->jrd", grad_lowrank, normed_one)
-    grad_lowrank_out = dot("td,rd->tr", grad_branch, o_up).astype(BF16)
-    grad_o_up = dot("tr,td->rd", lowrank_out.astype(BF16), grad_branch)
-    grad_o_down = dot("tr,nct->nrc", grad_lowrank_out, att_share)
-    shared = jnp.concatenate(
-        [gain_one[None], gain_two[None], grad_qkv_down.reshape(-1, model_width), grad_o_up], axis=0
-    )
-    lines = shared.shape[0]
-    shared = jnp.transpose(shared.reshape(lines, dp, n, -1), (1, 2, 0, 3)).reshape(dp, n, -1)
-    downs = grad_o_down.reshape(n, rank, groups, dp, -1)
-    downs = jnp.transpose(downs, (3, 0, 1, 2, 4)).reshape(dp, n, -1)
-    cut = shared.shape[2]
-    packed = scatter_small(jnp.concatenate([shared, downs], axis=2), True)
-    shared = packed[:cut].reshape(lines, -1)
-    out_o_down = packed[cut:].reshape(rank, groups, -1)
     return (
         output,
         grad_input,

time: 588 us -> 546 us (0.929)
  Pallas kernels: 350 us -> 326 us
  waiting for transfers between devices: 33.3 us -> 16.3 us
  starting transfers between devices: 25.7 us -> 15.5 us
  matrix products: 32.9 us -> 40.5 us
    pallas_call x1, Pallas kernels: 138 us -> 113 us  [tail(): pl.pallas_call(partial(tail_kernel, n, dp, tile, cut), out_shape=(jax.Sha...]
    ppermute x8 -> x0, waiting for transfers between devices: 18.7 us -> none  [the longest x6 16.9 us: scatter_small(): lax.ppermute(pick(blocks, 1 - own, 0), 'dp', flip(size, bit))]
    ppermute x8 -> x0, starting transfers between devices: 12.1 us -> none  [the longest x2 7.6 us: scatter_small(): lax.ppermute(pick(blocks, 1 - own, 0), 'tensor', flip(size, bit))]
    dot_general x0 -> x1, matrix products: none -> 6.34 us  [local(): dot('ct,cd->td', flat_joined, w_joined) * normed_one.astype(F32)]
    unnamed x156 -> x138, local copies, waits for them, and re-layouts: 35.5 us -> 39.5 us
    ppermute x6 -> x9, starting transfers between devices: 11.5 us -> 13.4 us  [exchange(): came.append(lax.ppermute(parts((me + s) % n), 'tensor', ring(n, s)))]
    ppermute x6 -> x9, waiting for transfers between devices: 14.6 us -> 16.3 us  [exchange(): came.append(lax.ppermute(parts((me + s) % n), 'tensor', ring(n, s)))]
  transfers between devices with their start and end apart: 20 -> 14, of which waited for: 9 -> 3; matrix products, arithmetic and copies ran while one was open for 20% -> 22% of each run, Pallas kernels for 61% -> 61%
where the time goes in v5:
time: 546 us; the launch traced here: 538 us
  Pallas kernels  326 us (60%)
  local copies, waits for them, and re-layouts  62.6 us (11%)
  matrix products  40.5 us (7%)
  other arithmetic  36.4 us (7%)
  blocking collectives  24.9 us (5%)
  waiting for transfers between devices  16.3 us (3%)
  starting transfers between devices  15.5 us (3%)
  between operations  15.5 us (3%)
    pallas_call x1, Pallas kernels, feed_forward(): pl.pallas_call(partial(feed_kernel, n, dp, tile, cut), out_shape=(jax.Sha...  146 us
    pallas_call x1, Pallas kernels, tail(): pl.pallas_call(partial(tail_kernel, n, dp, tile, cut), out_shape=(jax.Sha...  113 us
    pallas_call x1, Pallas kernels, attention_backward(): pl.pallas_call(partial(backward_kernel, heads, block), grid=(groups,), ou...  41.2 us
    unnamed x138, local copies, waits for them, and re-layouts  39.5 us
    pallas_call x1, Pallas kernels, attention_forward(): pl.pallas_call(partial(forward_kernel, heads, block), grid=(groups,), out...  25.8 us
    all_gather x1, blocking collectives, local(): down_all = lax.all_gather(down_flat, 'tensor')  24.9 us
    ppermute x9, waiting for transfers between devices, exchange(): came.append(lax.ppermute(parts((me + s) % n), 'tensor', ring(n, s)))  16.3 us
    ppermute x9, starting transfers between devices, exchange(): came.append(lax.ppermute(parts((me + s) % n), 'tensor', ring(n, s)))  13.4 us
  transfers between devices with their start and end apart: 14, of which 3 were waited for; matrix products, arithmetic and copies ran while one was open for 22% of the time, Pallas kernels for 61%

profile of v5, /device:TPU:12, one launch (start us, length us, event | category | flops | bytes accessed | tf_op | source)
XLA Modules:
  0.0 537.8 jit_solution(8442441487780673346)
XLA Ops:
  8.0 1.7 fusion.59
  9.6 1.7 fusion.43
  11.5 6.7 %copy.98 = bf16[2048,2,384]{0,2,1:T(8,128)(2,1)} copy(bf16[2048,2,384]{2,1,0:T(2,128)(2,1)S(1)} %copy-done.26) | data formatting | bytes 6291456 | tf_op args[4]
  18.7 3.3 fusion
  23.8 1.7 copy-done.16
  25.5 1.0 fusion.2.normed_in
  26.6 5.1 fusion.8.joined_ref
  31.7 25.8 %attention_forward.1 = (bf16[2,384,1024]{2,1,0:T(8,128)(2,1)S(1)}, bf16[2,256,1024]{2,1,0:T(8,128)(2,1)S(1)}, f32[2,4,1,1024]{3,2,1,0:T(1,128)S(1)}) custom-call(f32[2,384,1024]{2,1,0:T(8,128)} %fusion.8.joined_ref, f32[32,1024]{1,0:T(8,128)S(1)} %get-tuple-element.149.cos_ref, f32[32,1024]{1,0:T(8,128)S(1)} %get-tuple-element.148.sin_ref, ...), custom_call_target="tpu_custom_call" | custom-call | flops 22000001024 | bytes 10000000 | tf_op jit(solution)/shard_map/attention_forward/pallas_call | solution.py:121
  57.6 1.1 copy-done.12
  59.0 1.7 collective-permute-start
  60.8 1.3 collective-permute-start.1
  62.2 2.1 collective-permute-start.2
  64.3 1.5 fusion.23
  66.0 4.1 fusion.32
  71.4 17.3 %copy.142 = bf16[2048,2,2048]{2,0,1:T(8,128)(2,1)} copy(bf16[2048,2,2048]{2,1,0:T(2,128)(2,1)} %param.24) | data formatting | bytes 33554432 | tf_op args[11]
  88.7 24.9 %all_gather.7 = bf16[4,8,512]{2,1,0:T(8,128)(2,1)} all-gather(bf16[1,8,512]{2,1,0:T(8,128)(2,1)S(1)} %all_gather_reshape.3), channel_id=1, replica_groups=mesh['dp'=8,'tensor'=4] {'tensor'}, dimensions={0}, use_global_device_ids=true | all-gather | bytes 40960 | tf_op jit(solution)/shard_map/all_gather | solution.py:1166
  113.7 1.3 pad_maximum_fusion
  116.0 1.3 copy.110
  117.3 6.3 %multiply_reduce_fusion.1 = (f32[256]{0:T(256)S(1)}, f32[256,2048]{1,0:T(8,128)S(1)}) fusion(bf16[4,512,2048]{2,1,0:T(8,128)(2,1)} %bitcast.187, bf16[1,512,256]{1,2,0:T(8,128)(2,1)} %copy-done.28, bf16[1,512,256]{1,2,0:T(8,128)(2,1)} %copy-done.30, bf16[1,512,256]{1,2,0:T(8,128)(2,1)} %copy-done.32, bf16[1,512,256]{1,2,0:T(8,128)(2,1)S(1)} %get-tuple-element.134, ...), kind=kOutput, calls=%fused_computation.41 | convolution fusion | flops 2151153408 | bytes 12583940 | tf_op jit(solution)/shard_map/nct,ncd->td/dot_general | solution.py:1184
  123.7 1.4 multiply_convert_fusion.normed_in
  125.1 146.0 %feed_forward.1 = (bf16[256,2048]{1,0:T(8,128)(2,1)}, bf16[1024,2048]{1,0:T(8,128)(2,1)}, bf16[4,768,2048]{2,1,0:T(8,128)(2,1)}, bf16[2,384,2048]{2,1,0:T(8,128)...) custom-call(bf16[256,2048]{1,0:T(8,128)(2,1)} %multiply_convert_fusion.normed_in,, ...), custom_call_target="tpu_custom_call" | custom-call | flops 77309411328 | bytes 50331648 | tf_op jit(solution)/shard_map/feed_forward/pallas_call | solution.py:622
  271.1 2.7 fusion.22
  274.4 1.9 fusion.55
  277.3 6.8 %convolution_convert_fusion = bf16[4,512,256]{2,1,0:T(8,128)(2,1)} fusion(bf16[4,512,2048]{2,1,0:T(8,128)(2,1)} %bitcast.188, bf16[256,2048]{1,0:T(8,128)(2,1)S(1)} %fusion.55), kind=kOutput, calls=%fused_computation.44 | convolution fusion | flops 2148007936 | bytes 10485760 | tf_op jit(solution)/shard_map/ncd,td->nct/dot_general | solution.py:1198
  284.1 2.2 convolution_bitcast_fusion.1
  286.4 2.5 fusion.37
  290.6 2.1 constant_dynamic-slice_fusion.16
  292.7 6.1 %collective-permute-start.4 = (bf16[512,256]{1,0:T(8,128)(2,1)}, bf16[512,256]{1,0:T(8,128)(2,1)}, u32[]{:S(2)}, u32[]{:S(2)}) collective-permute-start(bf16[512,256]{1,0:T(8,128)(2,1)} %get-tuple-element.132), channel_id=1, source_target_pairs={{0,2},{1,3},{2,0},{3,1},{4,6},{5,7},{6,4},{7,5},{8,10},{9,11},{10,... | collective-permute-start | bytes 786440 | tf_op jit(solution)/shard_map/ppermute | solution.py:1116
  300.1 1.5 collective-permute-start.11
  304.4 10.3 %collective-permute-done.4 = bf16[512,256]{1,0:T(8,128)(2,1)} collective-permute-done((bf16[512,256]{1,0:T(8,128)(2,1)}, bf16[512,256]{1,0:T(8,128)(2,1)}, u32[]{:S(2)}, u32[]{:S(2)}) %collective-permute-start.4) | collective-permute-done | bytes 262176 | tf_op jit(solution)/shard_map/ppermute | solution.py:1116
  314.8 5.5 %collective-permute-done.5 = bf16[512,256]{1,0:T(8,128)(2,1)} collective-permute-done((bf16[512,256]{1,0:T(8,128)(2,1)}, bf16[512,256]{1,0:T(8,128)(2,1)}, u32[]{:S(2)}, u32[]{:S(2)}) %collective-permute-start.5) | collective-permute-done | bytes 262176 | tf_op jit(solution)/shard_map/ppermute | solution.py:1116
  320.2 1.2 pad_maximum_fusion.2
  321.7 2.0 copy-done.22
  323.7 2.2 constant_dynamic-slice_fusion.9
  325.9 2.2 collective-permute-start.7
  328.1 41.2 %attention_backward.1 = (bf16[2,384,1024]{2,1,0:T(8,128)(2,1)S(1)}, f32[2,5,64,64]{3,2,1,0:T(8,128)S(1)}) custom-call(bf16[2,384,1024]{2,1,0:T(8,128)(2,1)} %copy-done.12, f32[32,1024]{1,0:T(8,128)S(1)} %copy-done.8, f32[32,1024]{1,0:T(8,128)S(1)} %copy-done.6, bf16[2,320,64]{2,1,0:T(8,128)(2,1)S(1)} %bitcast.161, bf16[2,5,64,64]{3,2,1,0:T(8,128)(2,1)S(1)} %copy-done.10, ...), custom_call_target="tpu_custom_call" | custom-call | flops 40000000000 | bytes 10000000 | tf_op jit(solution)/shard_map/attention_backward/pallas_call | solution.py:214
  369.3 3.7 fusion.6
  375.7 6.3 %multiply_reduce_fusion = f32[2048]{0:T(1024)S(1)} fusion(bf16[1024,2048]{1,0:T(8,128)(2,1)} %copy-done.13, bf16[768,1024]{1,0:T(8,128)(2,1)S(1)} %bitcast.156, bf16[768,2048]{1,0:T(8,128)(2,1)} %bitcast.166), kind=kOutput, calls=%fused_computation.6 | convolution fusion | flops 3227514880 | bytes 8921088 | tf_op jit(solution)/shard_map/ct,cd->td/dot_general | solution.py:1229
  384.9 113.1 %gradient_sums.1 = (bf16[256,2048]{1,0:T(8,128)(2,1)}, bf16[384,2048]{1,0:T(8,128)(2,1)}, bf16[384,2048]{1,0:T(8,128)(2,1)}, bf16[256,512]{1,0:T(8,128)(2,1)}, b...) custom-call(bf16[768,1024]{1,0:T(8,128)(2,1)} %bitcast.157, ...), custom_call_target="tpu_custom_call" | custom-call | flops 1000000 | bytes 100000 | tf_op jit(solution)/shard_map/gradient_sums/pallas_call | solution.py:1032
  498.0 1.6 convert_bitcast_fusion
  500.2 3.5 maximum_convert_fusion
  503.7 1.8 copy.125
  505.5 2.2 slice-done
  507.7 5.2 copy.143
  514.6 2.2 copy.124
  520.9 2.3 maximum_convert_fusion.1
  523.2 2.1 fusion.14
  525.4 5.1 fusion.18
  (221 shorter events, 25.6 us)
Async XLA Ops:
  7.2 15.5 %copy-start = (bf16[3,8,2048]{2,1,0:T(8,128)(2,1)S(1)}, bf16[3,8,2048]{2,1,0:T(8,128)(2,1)}, u32[]{:S(2)}) copy-start(bf16[3,8,2048]{2,1,0:T(8,128)(2,1)} %param.18) | copy-start | bytes 294916
  7.2 110.1 %all-gather.2.cloned.1.call-start = ((), (), s32[]{:S(2)}) async-start(), calls=%async_computation | async-start | bytes 8650752 | tf_op jit(solution)/shard_map/all_gather | solution.py:1107
  11.5 6.7 %copy-start.11 = (s32[1,1024]{1,0:T(1,128)S(1)}, s32[1,1024]{1,0:T(1,128)}, u32[]{:S(2)}) copy-start(s32[1,1024]{1,0:T(1,128)} %row_ref.3) | copy-start | bytes 12292
  11.5 6.9 %copy-start.33 = (bf16[2,64,320]{2,1,0:T(8,128)(2,1)S(1)}, bf16[2,64,320]{2,1,0:T(8,128)(2,1)}, u32[]{:S(2)}) copy-start(bf16[2,64,320]{2,1,0:T(8,128)(2,1)} %param.20) | copy-start | bytes 245764
  18.6 13.1 %copy-start.3 = (bf16[2,64,320]{1,2,0:T(8,128)(2,1)}, bf16[2,64,320]{1,2,0:T(8,128)(2,1)S(1)}, u32[]{:S(2)}) copy-start(bf16[2,64,320]{1,2,0:T(8,128)(2,1)S(1)} %copy.102) | copy-start | bytes 245764
  22.6 9.1 %copy-start.5 = (f32[32,1024]{1,0:T(8,128)}, f32[32,1024]{1,0:T(8,128)S(1)}, u32[]{:S(2)}) copy-start(f32[32,1024]{1,0:T(8,128)S(1)} %get-tuple-element.148.sin_ref) | copy-start | bytes 393220
  22.6 9.1 %copy-start.7 = (f32[32,1024]{1,0:T(8,128)}, f32[32,1024]{1,0:T(8,128)S(1)}, u32[]{:S(2)}) copy-start(f32[32,1024]{1,0:T(8,128)S(1)} %get-tuple-element.149.cos_ref) | copy-start | bytes 393220
  26.6 5.1 copy-start.13
  58.7 7.1 %copy-start.34 = (bf16[2,64,320]{2,1,0:T(8,128)(2,1)S(1)}, bf16[2,64,320]{2,1,0:T(8,128)(2,1)}, u32[]{:S(2)}) copy-start(bf16[2,64,320]{2,1,0:T(8,128)(2,1)} %param.20) | copy-start | bytes 245764
  59.0 54.7 %collective-permute-start = (bf16[512,256]{0,1:T(8,128)(2,1)S(1)}, bf16[512,256]{0,1:T(8,128)(2,1)}, u32[]{:S(2)}, u32[]{:S(2)}) collective-permute-start(bf16[512,256]{0,1:T(8,128)(2,1)S(1)} %copy.130), channel_id=1, source_target_pairs={{0,1},{1,2},{2,3},{3,0},{4,5},{5,6},{6,7},{7,4},{8,9},{9,10},{10,1... | collective-permute-start | bytes 786440 | tf_op jit(solution)/shard_map/ppermute | solution.py:1116
  60.8 52.9 %collective-permute-start.1 = (bf16[512,256]{0,1:T(8,128)(2,1)S(1)}, bf16[512,256]{0,1:T(8,128)(2,1)}, u32[]{:S(2)}, u32[]{:S(2)}) collective-permute-start(bf16[512,256]{0,1:T(8,128)(2,1)S(1)} %copy.131), channel_id=1, source_target_pairs={{0,2},{1,3},{2,0},{3,1},{4,6},{5,7},{6,4},{7,5},{8,10},{9,11},{10,... | collective-permute-start | bytes 786440 | tf_op jit(solution)/shard_map/ppermute | solution.py:1116
  62.2 51.5 %collective-permute-start.2 = (bf16[512,256]{0,1:T(8,128)(2,1)S(1)}, bf16[512,256]{0,1:T(8,128)(2,1)}, u32[]{:S(2)}, u32[]{:S(2)}) collective-permute-start(bf16[512,256]{0,1:T(8,128)(2,1)S(1)} %copy.132), channel_id=1, source_target_pairs={{0,3},{1,0},{2,1},{3,2},{4,7},{5,4},{6,5},{7,6},{8,11},{9,8},{10,9... | collective-permute-start | bytes 786440 | tf_op jit(solution)/shard_map/ppermute | solution.py:1116
  66.0 4.6 copy-start.53
  117.3 266.8 %collective-permute-start.9 = (bf16[2048,256]{1,0:T(8,128)(2,1)}, bf16[2048,256]{1,0:T(8,128)(2,1)}, u32[]{:S(2)}, u32[]{:S(2)}) collective-permute-start(bf16[2048,256]{1,0:T(8,128)(2,1)} %bitcast.38.att_in), channel_id=1, source_target_pairs={{0,4},{4,0},{8,12},{12,8},{16,20},{20,16},{24,28},{28,24},{1,5},{5... | collective-permute-start | bytes 3145736 | tf_op jit(solution)/shard_map/ppermute | solution.py:1250
  123.7 150.1 %copy-start.14 = (f32[256,2048]{1,0:T(8,128)}, f32[256,2048]{1,0:T(8,128)S(1)}, u32[]{:S(2)}) copy-start(f32[256,2048]{1,0:T(8,128)S(1)} %get-tuple-element.151) | copy-start | bytes 6291460
  277.3 6.8 %copy-start.29 = (bf16[1,512,256]{1,2,0:T(8,128)(2,1)S(1)}, bf16[1,512,256]{1,2,0:T(8,128)(2,1)}, u32[]{:S(2)}) copy-start(bf16[1,512,256]{1,2,0:T(8,128)(2,1)} %copy-done.28) | copy-start | bytes 786436
  277.3 6.8 %copy-start.31 = (bf16[1,512,256]{1,2,0:T(8,128)(2,1)S(1)}, bf16[1,512,256]{1,2,0:T(8,128)(2,1)}, u32[]{:S(2)}) copy-start(bf16[1,512,256]{1,2,0:T(8,128)(2,1)} %copy-done.30) | copy-start | bytes 786436
  277.3 6.8 %copy-start.51 = (bf16[8,2048]{1,0:T(8,128)(2,1)S(1)}, bf16[8,2048]{1,0:T(8,128)(2,1)}, u32[]{:S(2)}) copy-start(bf16[8,2048]{1,0:T(8,128)(2,1)} %param.23) | copy-start | bytes 98308
  288.9 9.9 %copy-start.52 = (f32[2048]{0:T(1024)S(1)}, f32[2048]{0:T(1024)}, u32[]{:S(2)}) copy-start(f32[2048]{0:T(1024)} %get-tuple-element.110) | copy-start | bytes 24580
  292.6 11.3 %collective-permute-start.3 = (bf16[512,256]{1,0:T(8,128)(2,1)}, bf16[512,256]{1,0:T(8,128)(2,1)}, u32[]{:S(2)}, u32[]{:S(2)}) collective-permute-start(bf16[512,256]{1,0:T(8,128)(2,1)} %get-tuple-element.133), channel_id=1, source_target_pairs={{0,1},{1,2},{2,3},{3,0},{4,5},{5,6},{6,7},{7,4},{8,9},{9,10},{10,1... | collective-permute-start | bytes 786440 | tf_op jit(solution)/shard_map/ppermute | solution.py:1116
  292.7 22.1 %collective-permute-start.4 = (bf16[512,256]{1,0:T(8,128)(2,1)}, bf16[512,256]{1,0:T(8,128)(2,1)}, u32[]{:S(2)}, u32[]{:S(2)}) collective-permute-start(bf16[512,256]{1,0:T(8,128)(2,1)} %get-tuple-element.132), channel_id=1, source_target_pairs={{0,2},{1,3},{2,0},{3,1},{4,6},{5,7},{6,4},{7,5},{8,10},{9,11},{10,... | collective-permute-start | bytes 786440 | tf_op jit(solution)/shard_map/ppermute | solution.py:1116
  298.7 21.5 %collective-permute-start.5 = (bf16[512,256]{1,0:T(8,128)(2,1)}, bf16[512,256]{1,0:T(8,128)(2,1)}, u32[]{:S(2)}, u32[]{:S(2)}) collective-permute-start(bf16[512,256]{1,0:T(8,128)(2,1)} %get-tuple-element.131), channel_id=1, source_target_pairs={{0,3},{1,0},{2,1},{3,2},{4,7},{5,4},{6,5},{7,6},{8,11},{9,8},{10,9... | collective-permute-start | bytes 786440 | tf_op jit(solution)/shard_map/ppermute | solution.py:1116
  300.1 84.0 %collective-permute-start.11 = (bf16[2,384,2048]{2,1,0:T(8,128)(2,1)}, bf16[2,384,2048]{2,1,0:T(8,128)(2,1)}, u32[]{:S(2)}, u32[]{:S(2)}) collective-permute-start(bf16[2,384,2048]{2,1,0:T(8,128)(2,1)} %get-tuple-element.50), channel_id=1, source_target_pairs={{0,8},{4,12},{8,0},{12,4},{16,24},{20,28},{24,16},{28,20},{1,9},{5... | collective-permute-start | bytes 9437192 | tf_op jit(solution)/shard_map/ppermute | solution.py:1258
  303.9 80.2 %collective-permute-start.12 = (bf16[2,384,2048]{2,1,0:T(8,128)(2,1)}, bf16[2,384,2048]{2,1,0:T(8,128)(2,1)}, u32[]{:S(2)}, u32[]{:S(2)}) collective-permute-start(bf16[2,384,2048]{2,1,0:T(8,128)(2,1)} %get-tuple-element.52), channel_id=1, source_target_pairs={{0,16},{4,20},{8,24},{12,28},{16,0},{20,4},{24,8},{28,12},{1,17},{... | collective-permute-start | bytes 9437192 | tf_op jit(solution)/shard_map/ppermute | solution.py:1259
  323.6 4.4 copy-start.4
  323.6 4.4 copy-start.6
  323.7 4.4 copy-start.8
  323.7 4.4 copy-start.10
  325.9 49.6 %collective-permute-start.6 = (bf16[256,2048]{1,0:T(8,128)(2,1)}, bf16[256,2048]{1,0:T(8,128)(2,1)}, u32[]{:S(2)}, u32[]{:S(2)}) collective-permute-start(bf16[256,2048]{1,0:T(8,128)(2,1)} %get-tuple-element.114), channel_id=1, source_target_pairs={{0,1},{1,2},{2,3},{3,0},{4,5},{5,6},{6,7},{7,4},{8,9},{9,10},{10,1... | collective-permute-start | bytes 3145736 | tf_op jit(solution)/shard_map/ppermute | solution.py:1116
  325.9 49.7 %collective-permute-start.7 = (bf16[256,2048]{1,0:T(8,128)(2,1)}, bf16[256,2048]{1,0:T(8,128)(2,1)}, u32[]{:S(2)}, u32[]{:S(2)}) collective-permute-start(bf16[256,2048]{1,0:T(8,128)(2,1)} %get-tuple-element.112), channel_id=1, source_target_pairs={{0,3},{1,0},{2,1},{3,2},{4,7},{5,4},{6,5},{7,6},{8,11},{9,8},{10,9... | collective-permute-start | bytes 3145736 | tf_op jit(solution)/shard_map/ppermute | solution.py:1116
  328.1 41.2 %copy-start.45 = (bf16[1,8,2,384]{3,1,0,2:T(8,128)(2,1)S(1)}, bf16[1,8,2,384]{3,1,0,2:T(8,128)(2,1)}, u32[]{:S(2)}) copy-start(bf16[1,8,2,384]{3,1,0,2:T(8,128)(2,1)} %copy-done.44) | copy-start | bytes 36868
  369.3 6.3 %copy-start.2 = (bf16[2,384,1024]{2,1,0:T(8,128)(2,1)}, bf16[2,384,1024]{2,1,0:T(8,128)(2,1)S(1)}, u32[]{:S(2)}) copy-start(bf16[2,384,1024]{2,1,0:T(8,128)(2,1)S(1)} %get-tuple-element.43) | copy-start | bytes 4718596
  369.3 4.2 copy-start.48
  375.5 8.6 %collective-permute-start.10 = (bf16[256,1024]{1,0:T(8,128)(2,1)}, bf16[256,1024]{1,0:T(8,128)(2,1)S(1)}, u32[]{:S(2)}, u32[]{:S(2)}) collective-permute-start(bf16[256,1024]{1,0:T(8,128)(2,1)} %pad_maximum_fusion.6), channel_id=1, source_target_pairs={{0,4},{4,0},{8,12},{12,8},{16,20},{20,16},{24,28},{28,24},{1,5},{5... | collective-permute-start | bytes 1572872 | tf_op jit(solution)/shard_map/ppermute | solution.py:1252
  375.5 149.8 %collective-permute-start.8 = (bf16[256,2048]{1,0:T(8,128)(2,1)}, bf16[256,2048]{1,0:T(8,128)(2,1)}, u32[]{:S(2)}, u32[]{:S(2)}) collective-permute-start(bf16[256,2048]{1,0:T(8,128)(2,1)} %get-tuple-element.113), channel_id=1, source_target_pairs={{0,2},{1,3},{2,0},{3,1},{4,6},{5,7},{6,4},{7,5},{8,10},{9,11},{10,... | collective-permute-start | bytes 3145736 | tf_op jit(solution)/shard_map/ppermute | solution.py:1116
  375.6 6.4 %copy-start.49 = (f32[2,2048]{1,0:T(2,128)S(1)}, f32[2,2048]{1,0:T(2,128)}, u32[]{:S(2)}) copy-start(f32[2,2048]{1,0:T(2,128)} %convert_element_type.106) | copy-start | bytes 49156
  375.6 6.5 %copy-start.36 = (f32[8,8,4,64]{3,0,1,2:T(8,128)S(1)}, f32[8,8,4,64]{3,0,1,2:T(8,128)}, u32[]{:S(2)}) copy-start(f32[8,8,4,64]{3,0,1,2:T(8,128)} %copy.115) | copy-start | bytes 196612
  507.7 5.3 copy-start.40
  507.7 5.3 copy-start.39
  507.7 6.1 %copy-start.37 = (bf16[256,512]{1,0:T(8,128)(2,1)S(1)}, bf16[256,512]{1,0:T(8,128)(2,1)}, u32[]{:S(2)}) copy-start(bf16[256,512]{1,0:T(8,128)(2,1)} %get-tuple-element.59) | copy-start | bytes 786436
  512.9 4.6 copy-start.55
  512.9 10.3 %copy-start.42 = (f32[1,2048]{1,0:T(1,128)S(1)}, f32[1,2048]{1,0:T(1,128)}, u32[]{:S(2)}) copy-start(f32[1,2048]{1,0:T(1,128)} %copy-done.41) | copy-start | bytes 24580
  512.9 10.3 %copy-start.56 = (f32[256]{0:T(256)S(1)}, f32[256]{0:T(256)}, u32[]{:S(2)}) copy-start(f32[256]{0:T(256)} %add_rsqrt_fusion.1) | copy-start | bytes 3076
  514.6 10.8 %copy-start.15 = (f32[256,2048]{1,0:T(8,128)S(1)}, f32[256,2048]{1,0:T(8,128)}, u32[]{:S(2)}) copy-start(f32[256,2048]{1,0:T(8,128)} %copy-done.14) | copy-start | bytes 6291460
  514.6 10.8 %copy-start.18 = (bf16[256,2048]{1,0:T(8,128)(2,1)S(1)}, bf16[256,2048]{1,0:T(8,128)(2,1)}, u32[]{:S(2)}) copy-start(bf16[256,2048]{1,0:T(8,128)(2,1)} %get-tuple-element.41) | copy-start | bytes 3145732
  514.6 10.8 %copy-start.58 = (f32[256]{0:T(256)S(1)}, f32[256]{0:T(256)}, u32[]{:S(2)}) copy-start(f32[256]{0:T(256)} %copy-done.57) | copy-start | bytes 3076
  520.9 4.4 copy-start.21
  525.4 5.2 copy-start.1
  (27 other events, 60.1 us)
Sparse Core Ops, SparseCore 0:
  11.5 94.5 all-gather.1

commit v6 on v5

--- a/solution.py
+++ b/solution.py
@@ -110,7 +110,7 @@
             att_ref[0, rows, cols] = att.astype(BF16)
             return carry
 
-        lax.fori_loop(0, heads, one_head, 0)
+        lax.fori_loop(0, heads, one_head, 0, unroll=True)
 
 
 def attention_forward(joined_t, cosines, sines, maps_t, seg_row, seg_col, heads, block=256):
@@ -190,7 +190,7 @@
             grad_ref[0, rows, cols] = rotate_back_t(gquery, cos_ref[:, cols], sin_ref[:, cols]).astype(BF16)
             return carry
 
-        lax.fori_loop(0, heads, one_head, 0)
+        lax.fori_loop(0, heads, one_head, 0, unroll=True)
     glogits = softmaxes_back_t(key_up, key_down, gkfeat[...].T)
     gkey_t = gkeys[...].T + nn(back_ref[0, heads], glogits)
     gmap_ref[0, heads] = nt(key_t, glogits)
@@ -1277,9 +1277,10 @@
         + inverse_one
         * (weighted - scaled_one * jnp.mean(weighted * scaled_one, axis=-1, keepdims=True))
     ).astype(BF16)
-    out_feed = jnp.concatenate([feed_a, feed_b], axis=0).astype(F32).reshape(3, width, -1)
-    out_gate_up = jnp.transpose(out_feed[:2], (1, 0, 2))
-    out_down = out_feed[2].T
+    over = feed_a.shape[0] - width
+    out_up_rows = jnp.concatenate([feed_a[width:], feed_b[:width - over]], axis=0)
+    out_gate_up = jnp.stack([feed_a[:width], out_up_rows], axis=1).astype(F32)
+    out_down = feed_b[width - over:].T.astype(F32)
     out_branch = out_branch.T.astype(F32)
     out_qkv = jnp.concatenate([qkv_a, qkv_b], axis=0).astype(F32).reshape(width, groups, joined_width)
 

time: 546 us -> 520 us (0.952)
  Pallas kernels: 326 us -> 305 us
  blocking collectives: 24.9 us -> 15.9 us
    pallas_call x1, Pallas kernels: 25.8 us -> 15.1 us  [attention_forward(): pl.pallas_call(partial(forward_kernel, heads, block), grid=(groups,), out...]
    all_gather x1, blocking collectives: 24.9 us -> 15.9 us  [local(): down_all = lax.all_gather(down_flat, 'tensor')]
    slice x3 -> x2, local copies, waits for them, and re-layouts: 7.43 us -> 1.24 us  [the longest x1 1.19 us: local(): feed_a[width:]]
    unnamed x138 -> x137, local copies, waits for them, and re-layouts: 39.5 us -> 44.9 us
  transfers between devices with their start and end apart: 14 -> 14, of which waited for: 3 -> 4; matrix products, arithmetic and copies ran while one was open for 22% -> 23% of each run, Pallas kernels for 61% -> 60%
where the time goes in v6:
time: 520 us; the launch traced here: 513 us
  Pallas kernels  305 us (59%)
  local copies, waits for them, and re-layouts  63.5 us (12%)
  matrix products  40.4 us (8%)
  other arithmetic  32 us (6%)
  waiting for transfers between devices  21 us (4%)
  starting transfers between devices  19.2 us (4%)
  blocking collectives  15.9 us (3%)
  between operations  15.5 us (3%)
    pallas_call x1, Pallas kernels, feed_forward(): pl.pallas_call(partial(feed_kernel, n, dp, tile, cut), out_shape=(jax.Sha...  145 us
    pallas_call x1, Pallas kernels, tail(): pl.pallas_call(partial(tail_kernel, n, dp, tile, cut), out_shape=(jax.Sha...  109 us
    unnamed x137, local copies, waits for them, and re-layouts  44.9 us
    pallas_call x1, Pallas kernels, attention_backward(): pl.pallas_call(partial(backward_kernel, heads, block), grid=(groups,), ou...  36.2 us
    ppermute x9, starting transfers between devices, exchange(): came.append(lax.ppermute(parts((me + s) % n), 'tensor', ring(n, s)))  17.7 us
    ppermute x9, waiting for transfers between devices, exchange(): came.append(lax.ppermute(parts((me + s) % n), 'tensor', ring(n, s)))  16.7 us
    all_gather x1, blocking collectives, local(): down_all = lax.all_gather(down_flat, 'tensor')  15.9 us
    pallas_call x1, Pallas kernels, attention_forward(): pl.pallas_call(partial(forward_kernel, heads, block), grid=(groups,), out...  15.1 us
  transfers between devices with their start and end apart: 14, of which 4 were waited for; matrix products, arithmetic and copies ran while one was open for 23% of the time, Pallas kernels for 60%

profile of v6, /device:TPU:12, one launch (start us, length us, event | category | flops | bytes accessed | tf_op | source)
XLA Modules:
  0.0 512.8 jit_solution(335047948021694514)
XLA Ops:
  8.0 1.7 fusion.59
  9.6 1.7 fusion.43
  11.5 6.7 %copy.98 = bf16[2048,2,384]{0,2,1:T(8,128)(2,1)} copy(bf16[2048,2,384]{2,1,0:T(2,128)(2,1)S(1)} %copy-done.24) | data formatting | bytes 6291456 | tf_op args[4]
  18.7 3.3 fusion
  23.8 1.8 copy-done.16
  26.6 5.1 fusion.8.joined_ref
  31.7 15.1 %attention_forward.1 = (bf16[2,384,1024]{2,1,0:T(8,128)(2,1)S(1)}, bf16[2,256,1024]{2,1,0:T(8,128)(2,1)S(1)}, f32[2,4,1,1024]{3,2,1,0:T(1,128)S(1)}) custom-call(f32[2,384,1024]{2,1,0:T(8,128)} %fusion.8.joined_ref, f32[32,1024]{1,0:T(8,128)S(1)} %get-tuple-element.149.cos_ref, f32[32,1024]{1,0:T(8,128)S(1)} %get-tuple-element.148.sin_ref, ...), custom_call_target="tpu_custom_call" | custom-call | flops 22000001024 | bytes 10000000 | tf_op jit(solution)/shard_map/attention_forward/pallas_call | solution.py:121
  46.9 1.1 copy-done.12
  48.3 1.6 collective-permute-start
  50.1 1.3 collective-permute-start.1
  51.5 1.9 collective-permute-start.2
  53.4 1.5 fusion.23
  55.1 4.0 fusion.32
  60.5 17.6 %copy.141 = bf16[2048,2,2048]{2,0,1:T(8,128)(2,1)} copy(bf16[2048,2,2048]{2,1,0:T(2,128)(2,1)} %param.24) | data formatting | bytes 33554432 | tf_op args[11]
  78.1 15.9 %all_gather.7 = bf16[4,8,512]{2,1,0:T(8,128)(2,1)} all-gather(bf16[1,8,512]{2,1,0:T(8,128)(2,1)S(1)} %all_gather_reshape.3), channel_id=1, replica_groups=mesh['dp'=8,'tensor'=4] {'tensor'}, dimensions={0}, use_global_device_ids=true | all-gather | bytes 40960 | tf_op jit(solution)/shard_map/all_gather | solution.py:1166
  94.0 1.3 pad_maximum_fusion
  96.3 1.7 copy.110
  98.1 4.2 all-gather.2.cloned.1.call-done
  102.3 6.3 %multiply_reduce_fusion.1 = (f32[256]{0:T(256)S(1)}, f32[256,2048]{1,0:T(8,128)S(1)}) fusion(bf16[4,512,2048]{2,1,0:T(8,128)(2,1)} %bitcast.185, bf16[1,512,256]{1,2,0:T(8,128)(2,1)} %copy-done.27, bf16[1,512,256]{1,2,0:T(8,128)(2,1)} %copy-done.29, bf16[1,512,256]{1,2,0:T(8,128)(2,1)} %copy-done.31, bf16[1,512,256]{1,2,0:T(8,128)(2,1)S(1)} %get-tuple-element.134, ...), kind=kOutput, calls=%fused_computation.40 | convolution fusion | flops 2151153408 | bytes 12583940 | tf_op jit(solution)/shard_map/nct,ncd->td/dot_general | solution.py:1184
  108.6 1.4 multiply_convert_fusion.normed_in
  110.0 145.1 %feed_forward.1 = (bf16[256,2048]{1,0:T(8,128)(2,1)}, bf16[1024,2048]{1,0:T(8,128)(2,1)}, bf16[4,768,2048]{2,1,0:T(8,128)(2,1)}, bf16[2,384,2048]{2,1,0:T(8,128)...) custom-call(bf16[256,2048]{1,0:T(8,128)(2,1)} %multiply_convert_fusion.normed_in,, ...), custom_call_target="tpu_custom_call" | custom-call | flops 77309411328 | bytes 50331648 | tf_op jit(solution)/shard_map/feed_forward/pallas_call | solution.py:622
  255.2 2.7 fusion.22
  258.4 1.9 fusion.55
  261.4 6.8 %convolution_convert_fusion = bf16[4,512,256]{2,1,0:T(8,128)(2,1)} fusion(bf16[4,512,2048]{2,1,0:T(8,128)(2,1)} %bitcast.186, bf16[256,2048]{1,0:T(8,128)(2,1)S(1)} %fusion.55), kind=kOutput, calls=%fused_computation.43 | convolution fusion | flops 2148007936 | bytes 10485760 | tf_op jit(solution)/shard_map/ncd,td->nct/dot_general | solution.py:1198
  268.2 2.2 convolution_bitcast_fusion.1
  270.5 2.5 fusion.37
  274.6 2.1 constant_dynamic-slice_fusion.16
  277.5 5.3 %collective-permute-start.4 = (bf16[512,256]{1,0:T(8,128)(2,1)}, bf16[512,256]{1,0:T(8,128)(2,1)}, u32[]{:S(2)}, u32[]{:S(2)}) collective-permute-start(bf16[512,256]{1,0:T(8,128)(2,1)} %get-tuple-element.132), channel_id=1, source_target_pairs={{0,2},{1,3},{2,0},{3,1},{4,6},{5,7},{6,4},{7,5},{8,10},{9,11},{10,... | collective-permute-start | bytes 786440 | tf_op jit(solution)/shard_map/ppermute | solution.py:1116
  286.8 1.2 collective-permute-done.3
  288.6 10.3 %collective-permute-done.4 = bf16[512,256]{1,0:T(8,128)(2,1)} collective-permute-done((bf16[512,256]{1,0:T(8,128)(2,1)}, bf16[512,256]{1,0:T(8,128)(2,1)}, u32[]{:S(2)}, u32[]{:S(2)}) %collective-permute-start.4) | collective-permute-done | bytes 262176 | tf_op jit(solution)/shard_map/ppermute | solution.py:1116
  298.8 5.3 %collective-permute-done.5 = bf16[512,256]{1,0:T(8,128)(2,1)} collective-permute-done((bf16[512,256]{1,0:T(8,128)(2,1)}, bf16[512,256]{1,0:T(8,128)(2,1)}, u32[]{:S(2)}, u32[]{:S(2)}) %collective-permute-start.5) | collective-permute-done | bytes 262176 | tf_op jit(solution)/shard_map/ppermute | solution.py:1116
  304.1 1.2 pad_maximum_fusion.2
  305.6 2.0 copy-done.20
  307.5 2.2 constant_dynamic-slice_fusion.9
  309.7 2.0 collective-permute-start.7
  311.8 36.2 %attention_backward.1 = (bf16[2,384,1024]{2,1,0:T(8,128)(2,1)S(1)}, f32[2,5,64,64]{3,2,1,0:T(8,128)S(1)}) custom-call(bf16[2,384,1024]{2,1,0:T(8,128)(2,1)} %copy-done.12, f32[32,1024]{1,0:T(8,128)S(1)} %copy-done.8, f32[32,1024]{1,0:T(8,128)S(1)} %copy-done.6, bf16[2,320,64]{2,1,0:T(8,128)(2,1)S(1)} %bitcast.161, bf16[2,5,64,64]{3,2,1,0:T(8,128)(2,1)S(1)} %copy-done.10, ...), custom_call_target="tpu_custom_call" | custom-call | flops 40000000000 | bytes 10000000 | tf_op jit(solution)/shard_map/attention_backward/pallas_call | solution.py:214
  348.0 3.7 fusion.6
  354.2 4.8 collective-permute-start.8
  359.0 6.4 %multiply_reduce_fusion = f32[2048]{0:T(1024)S(1)} fusion(bf16[1024,2048]{1,0:T(8,128)(2,1)} %copy-done.13, bf16[768,1024]{1,0:T(8,128)(2,1)S(1)} %bitcast.156, bf16[768,2048]{1,0:T(8,128)(2,1)} %bitcast.164), kind=kOutput, calls=%fused_computation.6 | convolution fusion | flops 3227514880 | bytes 8921088 | tf_op jit(solution)/shard_map/ct,cd->td/dot_general | solution.py:1229
  368.2 108.9 %gradient_sums.1 = (bf16[256,2048]{1,0:T(8,128)(2,1)}, bf16[384,2048]{1,0:T(8,128)(2,1)}, bf16[384,2048]{1,0:T(8,128)(2,1)}, bf16[256,512]{1,0:T(8,128)(2,1)}, b...) custom-call(bf16[768,1024]{1,0:T(8,128)(2,1)} %bitcast.157, ...), custom_call_target="tpu_custom_call" | custom-call | flops 1000000 | bytes 100000 | tf_op jit(solution)/shard_map/gradient_sums/pallas_call | solution.py:1032
  477.1 1.2 slice.119
  478.3 1.3 slice_bitcast_fusion
  480.8 5.2 %copy.124 = f32[256,2,2048]{2,1,0:T(2,128)} copy(f32[256,2,2048]{2,0,1:T(8,128)S(1)} %maximum_convert_fusion) | data formatting | bytes 8388608
  486.8 1.8 copy.125
  489.5 2.2 copy.123
  495.9 2.3 maximum_convert_fusion.1
  498.2 2.1 fusion.14
  500.3 5.1 %fusion.18 = (bf16[256,2048]{1,0:T(8,128)(2,1)}, bf16[256,2048]{1,0:T(8,128)(2,1)}) fusion(bf16[256,2048]{1,0:T(8,128)(2,1)} %get-tuple-element.54, f32[256]{0:T(256)S(1)} %broadcast_multiply_fusion, f32[2048]{0:T(1024)S(1)} %bitcast.181, f32[256]{0:T(256)S(1)} %copy-done.55, bf16[1024,2048]{1,0:T(8,128)(2,1)} %param.13, s32[]{:T(128)S(6)} %select_n.113, ...), kind=kLoop, calls=%fused_computation.29 | loop fusion | flops 13631488 | bytes 12603396 | tf_op jit(solution)/shard_map/convert_element_type | solution.py:1279
  (221 shorter events, 28.2 us)
Async XLA Ops:
  7.2 15.5 %copy-start = (bf16[3,8,2048]{2,1,0:T(8,128)(2,1)S(1)}, bf16[3,8,2048]{2,1,0:T(8,128)(2,1)}, u32[]{:S(2)}) copy-start(bf16[3,8,2048]{2,1,0:T(8,128)(2,1)} %param.18) | copy-start | bytes 294916
  7.2 95.1 %all-gather.2.cloned.1.call-start = ((), (), s32[]{:S(2)}) async-start(), calls=%async_computation | async-start | bytes 8650752 | tf_op jit(solution)/shard_map/all_gather | solution.py:1107
  11.5 6.7 %copy-start.11 = (s32[1,1024]{1,0:T(1,128)S(1)}, s32[1,1024]{1,0:T(1,128)}, u32[]{:S(2)}) copy-start(s32[1,1024]{1,0:T(1,128)} %row_ref.3) | copy-start | bytes 12292
  11.5 6.9 %copy-start.32 = (bf16[2,64,320]{2,1,0:T(8,128)(2,1)S(1)}, bf16[2,64,320]{2,1,0:T(8,128)(2,1)}, u32[]{:S(2)}) copy-start(bf16[2,64,320]{2,1,0:T(8,128)(2,1)} %param.20) | copy-start | bytes 245764
  18.6 13.1 %copy-start.3 = (bf16[2,64,320]{1,2,0:T(8,128)(2,1)}, bf16[2,64,320]{1,2,0:T(8,128)(2,1)S(1)}, u32[]{:S(2)}) copy-start(bf16[2,64,320]{1,2,0:T(8,128)(2,1)S(1)} %copy.102) | copy-start | bytes 245764
  18.7 3.9 copy-start.25
  22.6 9.1 %copy-start.5 = (f32[32,1024]{1,0:T(8,128)}, f32[32,1024]{1,0:T(8,128)S(1)}, u32[]{:S(2)}) copy-start(f32[32,1024]{1,0:T(8,128)S(1)} %get-tuple-element.148.sin_ref) | copy-start | bytes 393220
  22.6 9.1 %copy-start.7 = (f32[32,1024]{1,0:T(8,128)}, f32[32,1024]{1,0:T(8,128)S(1)}, u32[]{:S(2)}) copy-start(f32[32,1024]{1,0:T(8,128)S(1)} %get-tuple-element.149.cos_ref) | copy-start | bytes 393220
  26.6 5.1 copy-start.13
  48.0 6.9 %copy-start.33 = (bf16[2,64,320]{2,1,0:T(8,128)(2,1)S(1)}, bf16[2,64,320]{2,1,0:T(8,128)(2,1)}, u32[]{:S(2)}) copy-start(bf16[2,64,320]{2,1,0:T(8,128)(2,1)} %param.20) | copy-start | bytes 245764
  48.3 45.7 %collective-permute-start = (bf16[512,256]{0,1:T(8,128)(2,1)S(1)}, bf16[512,256]{0,1:T(8,128)(2,1)}, u32[]{:S(2)}, u32[]{:S(2)}) collective-permute-start(bf16[512,256]{0,1:T(8,128)(2,1)S(1)} %copy.130), channel_id=1, source_target_pairs={{0,1},{1,2},{2,3},{3,0},{4,5},{5,6},{6,7},{7,4},{8,9},{9,10},{10,1... | collective-permute-start | bytes 786440 | tf_op jit(solution)/shard_map/ppermute | solution.py:1116
  50.1 43.9 %collective-permute-start.1 = (bf16[512,256]{0,1:T(8,128)(2,1)S(1)}, bf16[512,256]{0,1:T(8,128)(2,1)}, u32[]{:S(2)}, u32[]{:S(2)}) collective-permute-start(bf16[512,256]{0,1:T(8,128)(2,1)S(1)} %copy.131), channel_id=1, source_target_pairs={{0,2},{1,3},{2,0},{3,1},{4,6},{5,7},{6,4},{7,5},{8,10},{9,11},{10,... | collective-permute-start | bytes 786440 | tf_op jit(solution)/shard_map/ppermute | solution.py:1116
  51.5 42.5 %collective-permute-start.2 = (bf16[512,256]{0,1:T(8,128)(2,1)S(1)}, bf16[512,256]{0,1:T(8,128)(2,1)}, u32[]{:S(2)}, u32[]{:S(2)}) collective-permute-start(bf16[512,256]{0,1:T(8,128)(2,1)S(1)} %copy.132), channel_id=1, source_target_pairs={{0,3},{1,0},{2,1},{3,2},{4,7},{5,4},{6,5},{7,6},{8,11},{9,8},{10,9... | collective-permute-start | bytes 786440 | tf_op jit(solution)/shard_map/ppermute | solution.py:1116
  55.1 4.6 copy-start.52
  98.1 269.4 %collective-permute-start.9 = (bf16[2048,256]{1,0:T(8,128)(2,1)}, bf16[2048,256]{1,0:T(8,128)(2,1)}, u32[]{:S(2)}, u32[]{:S(2)}) collective-permute-start(bf16[2048,256]{1,0:T(8,128)(2,1)} %bitcast.38.att_in), channel_id=1, source_target_pairs={{0,4},{4,0},{8,12},{12,8},{16,20},{20,16},{24,28},{28,24},{1,5},{5... | collective-permute-start | bytes 3145736 | tf_op jit(solution)/shard_map/ppermute | solution.py:1250
  108.6 149.3 %copy-start.14 = (f32[256,2048]{1,0:T(8,128)}, f32[256,2048]{1,0:T(8,128)S(1)}, u32[]{:S(2)}) copy-start(f32[256,2048]{1,0:T(8,128)S(1)} %get-tuple-element.151) | copy-start | bytes 6291460
  261.4 6.8 %copy-start.28 = (bf16[1,512,256]{1,2,0:T(8,128)(2,1)S(1)}, bf16[1,512,256]{1,2,0:T(8,128)(2,1)}, u32[]{:S(2)}) copy-start(bf16[1,512,256]{1,2,0:T(8,128)(2,1)} %copy-done.27) | copy-start | bytes 786436
  261.4 6.8 %copy-start.30 = (bf16[1,512,256]{1,2,0:T(8,128)(2,1)S(1)}, bf16[1,512,256]{1,2,0:T(8,128)(2,1)}, u32[]{:S(2)}) copy-start(bf16[1,512,256]{1,2,0:T(8,128)(2,1)} %copy-done.29) | copy-start | bytes 786436
  261.4 6.8 %copy-start.50 = (bf16[8,2048]{1,0:T(8,128)(2,1)S(1)}, bf16[8,2048]{1,0:T(8,128)(2,1)}, u32[]{:S(2)}) copy-start(bf16[8,2048]{1,0:T(8,128)(2,1)} %param.23) | copy-start | bytes 98308
  272.9 9.9 %copy-start.51 = (f32[2048]{0:T(1024)S(1)}, f32[2048]{0:T(1024)}, u32[]{:S(2)}) copy-start(f32[2048]{0:T(1024)} %get-tuple-element.110) | copy-start | bytes 24580
  276.7 11.3 %collective-permute-start.3 = (bf16[512,256]{1,0:T(8,128)(2,1)}, bf16[512,256]{1,0:T(8,128)(2,1)}, u32[]{:S(2)}, u32[]{:S(2)}) collective-permute-start(bf16[512,256]{1,0:T(8,128)(2,1)} %get-tuple-element.133), channel_id=1, source_target_pairs={{0,1},{1,2},{2,3},{3,0},{4,5},{5,6},{6,7},{7,4},{8,9},{9,10},{10,1... | collective-permute-start | bytes 786440 | tf_op jit(solution)/shard_map/ppermute | solution.py:1116
  277.5 21.4 %collective-permute-start.4 = (bf16[512,256]{1,0:T(8,128)(2,1)}, bf16[512,256]{1,0:T(8,128)(2,1)}, u32[]{:S(2)}, u32[]{:S(2)}) collective-permute-start(bf16[512,256]{1,0:T(8,128)(2,1)} %get-tuple-element.132), channel_id=1, source_target_pairs={{0,2},{1,3},{2,0},{3,1},{4,6},{5,7},{6,4},{7,5},{8,10},{9,11},{10,... | collective-permute-start | bytes 786440 | tf_op jit(solution)/shard_map/ppermute | solution.py:1116
  282.8 21.3 %collective-permute-start.5 = (bf16[512,256]{1,0:T(8,128)(2,1)}, bf16[512,256]{1,0:T(8,128)(2,1)}, u32[]{:S(2)}, u32[]{:S(2)}) collective-permute-start(bf16[512,256]{1,0:T(8,128)(2,1)} %get-tuple-element.131), channel_id=1, source_target_pairs={{0,3},{1,0},{2,1},{3,2},{4,7},{5,4},{6,5},{7,6},{8,11},{9,8},{10,9... | collective-permute-start | bytes 786440 | tf_op jit(solution)/shard_map/ppermute | solution.py:1116
  284.1 83.3 %collective-permute-start.11 = (bf16[2,384,2048]{2,1,0:T(8,128)(2,1)}, bf16[2,384,2048]{2,1,0:T(8,128)(2,1)}, u32[]{:S(2)}, u32[]{:S(2)}) collective-permute-start(bf16[2,384,2048]{2,1,0:T(8,128)(2,1)} %get-tuple-element.50), channel_id=1, source_target_pairs={{0,8},{4,12},{8,0},{12,4},{16,24},{20,28},{24,16},{28,20},{1,9},{5... | collective-permute-start | bytes 9437192 | tf_op jit(solution)/shard_map/ppermute | solution.py:1258
  288.0 79.5 %collective-permute-start.12 = (bf16[2,384,2048]{2,1,0:T(8,128)(2,1)}, bf16[2,384,2048]{2,1,0:T(8,128)(2,1)}, u32[]{:S(2)}, u32[]{:S(2)}) collective-permute-start(bf16[2,384,2048]{2,1,0:T(8,128)(2,1)} %get-tuple-element.52), channel_id=1, source_target_pairs={{0,16},{4,20},{8,24},{12,28},{16,0},{20,4},{24,8},{28,12},{1,17},{... | collective-permute-start | bytes 9437192 | tf_op jit(solution)/shard_map/ppermute | solution.py:1259
  307.5 4.2 copy-start.4
  307.5 4.2 copy-start.6
  307.5 4.2 copy-start.8
  307.5 4.2 copy-start.10
  309.7 44.4 %collective-permute-start.6 = (bf16[256,2048]{1,0:T(8,128)(2,1)}, bf16[256,2048]{1,0:T(8,128)(2,1)}, u32[]{:S(2)}, u32[]{:S(2)}) collective-permute-start(bf16[256,2048]{1,0:T(8,128)(2,1)} %get-tuple-element.114), channel_id=1, source_target_pairs={{0,1},{1,2},{2,3},{3,0},{4,5},{5,6},{6,7},{7,4},{8,9},{9,10},{10,1... | collective-permute-start | bytes 3145736 | tf_op jit(solution)/shard_map/ppermute | solution.py:1116
  309.7 44.5 %collective-permute-start.7 = (bf16[256,2048]{1,0:T(8,128)(2,1)}, bf16[256,2048]{1,0:T(8,128)(2,1)}, u32[]{:S(2)}, u32[]{:S(2)}) collective-permute-start(bf16[256,2048]{1,0:T(8,128)(2,1)} %get-tuple-element.112), channel_id=1, source_target_pairs={{0,3},{1,0},{2,1},{3,2},{4,7},{5,4},{6,5},{7,6},{8,11},{9,8},{10,9... | collective-permute-start | bytes 3145736 | tf_op jit(solution)/shard_map/ppermute | solution.py:1116
  311.8 36.2 %copy-start.44 = (bf16[1,8,2,384]{3,1,0,2:T(8,128)(2,1)S(1)}, bf16[1,8,2,384]{3,1,0,2:T(8,128)(2,1)}, u32[]{:S(2)}) copy-start(bf16[1,8,2,384]{3,1,0,2:T(8,128)(2,1)} %copy-done.43) | copy-start | bytes 36868
  348.0 11.0 %copy-start.2 = (bf16[2,384,1024]{2,1,0:T(8,128)(2,1)}, bf16[2,384,1024]{2,1,0:T(8,128)(2,1)S(1)}, u32[]{:S(2)}) copy-start(bf16[2,384,1024]{2,1,0:T(8,128)(2,1)S(1)} %get-tuple-element.43) | copy-start | bytes 4718596
  348.0 4.2 copy-start.47
  354.1 13.3 %collective-permute-start.10 = (bf16[256,1024]{1,0:T(8,128)(2,1)}, bf16[256,1024]{1,0:T(8,128)(2,1)S(1)}, u32[]{:S(2)}, u32[]{:S(2)}) collective-permute-start(bf16[256,1024]{1,0:T(8,128)(2,1)} %pad_maximum_fusion.6), channel_id=1, source_target_pairs={{0,4},{4,0},{8,12},{12,8},{16,20},{20,16},{24,28},{28,24},{1,5},{5... | collective-permute-start | bytes 1572872 | tf_op jit(solution)/shard_map/ppermute | solution.py:1252
  354.2 146.1 %collective-permute-start.8 = (bf16[256,2048]{1,0:T(8,128)(2,1)}, bf16[256,2048]{1,0:T(8,128)(2,1)}, u32[]{:S(2)}, u32[]{:S(2)}) collective-permute-start(bf16[256,2048]{1,0:T(8,128)(2,1)} %get-tuple-element.113), channel_id=1, source_target_pairs={{0,2},{1,3},{2,0},{3,1},{4,6},{5,7},{6,4},{7,5},{8,10},{9,11},{10,... | collective-permute-start | bytes 3145736 | tf_op jit(solution)/shard_map/ppermute | solution.py:1116
  359.0 6.4 %copy-start.48 = (f32[2,2048]{1,0:T(2,128)S(1)}, f32[2,2048]{1,0:T(2,128)}, u32[]{:S(2)}) copy-start(f32[2,2048]{1,0:T(2,128)} %convert_element_type.112) | copy-start | bytes 49156
  359.0 6.5 %copy-start.35 = (f32[8,8,4,64]{3,0,1,2:T(8,128)S(1)}, f32[8,8,4,64]{3,0,1,2:T(8,128)}, u32[]{:S(2)}) copy-start(f32[8,8,4,64]{3,0,1,2:T(8,128)} %copy.115) | copy-start | bytes 196612
  480.8 5.3 %copy-start.39 = (bf16[128,768]{1,0:T(8,128)(2,1)S(1)}, bf16[128,768]{1,0:T(8,128)(2,1)}, u32[]{:S(2)}) copy-start(bf16[128,768]{1,0:T(8,128)(2,1)} %get-tuple-element.56) | copy-start | bytes 589828
  480.8 5.3 %copy-start.38 = (bf16[128,768]{1,0:T(8,128)(2,1)S(1)}, bf16[128,768]{1,0:T(8,128)(2,1)}, u32[]{:S(2)}) copy-start(bf16[128,768]{1,0:T(8,128)(2,1)} %get-tuple-element.57) | copy-start | bytes 589828
  486.8 5.7 %copy-start.54 = (f32[24,128]{1,0:T(8,128)S(1)}, f32[24,128]{1,0:T(8,128)}, u32[]{:S(2)}) copy-start(f32[24,128]{1,0:T(8,128)} %get-tuple-element.55) | copy-start | bytes 36868
  488.6 9.5 %copy-start.41 = (f32[1,2048]{1,0:T(1,128)S(1)}, f32[1,2048]{1,0:T(1,128)}, u32[]{:S(2)}) copy-start(f32[1,2048]{1,0:T(1,128)} %copy-done.40) | copy-start | bytes 24580
  488.7 9.5 %copy-start.55 = (f32[256]{0:T(256)S(1)}, f32[256]{0:T(256)}, u32[]{:S(2)}) copy-start(f32[256]{0:T(256)} %add_rsqrt_fusion.1) | copy-start | bytes 3076
  489.5 10.8 %copy-start.15 = (f32[256,2048]{1,0:T(8,128)S(1)}, f32[256,2048]{1,0:T(8,128)}, u32[]{:S(2)}) copy-start(f32[256,2048]{1,0:T(8,128)} %copy-done.14) | copy-start | bytes 6291460
  489.5 10.8 %copy-start.18 = (bf16[256,2048]{1,0:T(8,128)(2,1)S(1)}, bf16[256,2048]{1,0:T(8,128)(2,1)}, u32[]{:S(2)}) copy-start(bf16[256,2048]{1,0:T(8,128)(2,1)} %get-tuple-element.41) | copy-start | bytes 3145732
  489.5 10.8 %copy-start.57 = (f32[256]{0:T(256)S(1)}, f32[256]{0:T(256)}, u32[]{:S(2)}) copy-start(f32[256]{0:T(256)} %copy-done.56) | copy-start | bytes 3076
  495.9 4.4 copy-start.19
  500.3 5.2 %copy-start.1 = (bf16[3,8,2048]{2,1,0:T(8,128)(2,1)S(1)}, bf16[3,8,2048]{2,1,0:T(8,128)(2,1)}, u32[]{:S(2)}) copy-start(bf16[3,8,2048]{2,1,0:T(8,128)(2,1)} %param.18) | copy-start | bytes 294916
  (25 other events, 52.1 us)
Sparse Core Ops, SparseCore 0:
  11.5 90.7 all-gather.1
